TPU v7x, 256 devices: a whole 4x4x8 slice. The times are simulated.
256 devices in a mesh: lat: 8 (over x, y_hi), lon: 32 (over y_lo, z, core).
Axes of the slice: x: 4, y: 4 (y_hi: 2, y_lo: 2; y = y_hi * 2 + y_lo), z: 8, core: 2. Of those that a mesh axis runs over, the one named last changes fastest.
Arguments:
- latent: bfloat16 [48, 1536, 512], P('lat', 'lon'), may hold values from -6 to 6
- norm_gain: float32 [512], replicated, may hold values from 0.1 to 1.9
- w_qkv: bfloat16 [512, 1536], replicated, may hold values from -0.5 to 0.5
- w_out: bfloat16 [512, 512], replicated, may hold values from -0.25 to 0.25
- cotangent: bfloat16 [48, 1536, 512], P('lat', 'lon'), may hold values from -6 to 6
Outputs:
- mixed: bfloat16 [48, 1536, 512], P('lat', 'lon')
- d_latent: bfloat16 [48, 1536, 512], P('lat', 'lon')
- grad_qkv: float32 [512, 1536], replicated
- grad_out: float32 [512, 512], replicated
- grad_gain: float32 [512], replicated
All inputs are finite; a program needn't handle non-finite values.
Results may differ from a plain program's by a relative error of at most 0.013.
Values may be sent and summed in bfloat16 or wider, within the bound.
No kernel may reach another device: no remote copies, remote signals or barrier semaphores. Data moves between devices by JAX's collectives and lax.ppermute only.
A program may use at most 64 MiB of HBM per device.

v0:
```python
import jax
import jax.numpy as jnp
from jax import lax
from jax.sharding import PartitionSpec as P

HEADS = 16
HS = 32
WL = 6
WW = 12


def passed_along(value, axis, by):
    devices = lax.axis_size(axis)
    return lax.ppermute(value, axis, [(i, (i + by) % devices) for i in range(devices)])


def to_windows(field):
    height, breadth, features = field.shape
    blocks = field.reshape(height // WL, WL, breadth // WW, WW, features)
    return blocks.transpose(0, 2, 1, 3, 4).reshape(-1, WL * WW, features)


def from_windows(stacked, height, breadth):
    features = stacked.shape[-1]
    blocks = stacked.reshape(height // WL, breadth // WW, WL, WW, features)
    return blocks.transpose(0, 2, 1, 3, 4).reshape(height, breadth, features)


def lon_ahead(block_in):
    arrived = passed_along(block_in[:, : WW // 2], "lon", -1)
    return jnp.concatenate([block_in[:, WW // 2 :], arrived], axis=1)


def lat_ahead(block_in):
    arrived = passed_along(block_in[: WL // 2], "lat", -1)
    return jnp.concatenate([block_in[WL // 2 :], arrived], axis=0)


def lon_behind(block_in):
    arrived = passed_along(block_in[:, -(WW // 2) :], "lon", 1)
    return jnp.concatenate([arrived, block_in[:, : -(WW // 2)]], axis=1)


def lat_behind(block_in):
    arrived = passed_along(block_in[-(WL // 2) :], "lat", 1)
    return jnp.concatenate([arrived, block_in[: -(WL // 2)]], axis=0)


def shift_ahead(block_in):
    return lat_ahead(lon_ahead(block_in))


def shift_behind(block_in):
    return lat_behind(lon_behind(block_in))


def sum_grads(grad_items):
    return lax.psum((grad_items[0], grad_items[1], grad_items[2]), ("lat", "lon"))


def attend(packed, d_context, region):
    win_count, win_size, _ = packed.shape
    parts = packed.reshape(win_count, win_size, 3, HEADS, HS)
    queries = parts[:, :, 0]
    key_rows = parts[:, :, 1]
    values = parts[:, :, 2]
    scaling = HS ** (-0.5)
    scores = (
        jnp.einsum("bqhd,bkhd->bhqk", queries, key_rows, preferred_element_type=jnp.float32)
        * scaling
    )
    allowed = (region[:, :, None] == region[:, None, :])[:, None]
    masked = jnp.where(allowed, scores, -1e30)
    row_max = jnp.max(masked, axis=-1, keepdims=True)
    expo_terms = jnp.exp(masked - row_max)
    probs = expo_terms / jnp.sum(expo_terms, axis=-1, keepdims=True)
    weights = probs.astype(jnp.bfloat16)
    context = jnp.einsum(
        "bhqk,bkhd->bqhd", weights, values, preferred_element_type=jnp.float32
    ).astype(jnp.bfloat16)
    context = context.reshape(win_count, win_size, HEADS * HS)
    grad_ctx = d_context.reshape(win_count, win_size, HEADS, HS)
    d_weights = jnp.einsum("bqhd,bkhd->bhqk", grad_ctx, values, preferred_element_type=jnp.float32)
    d_values = jnp.einsum(
        "bhqk,bqhd->bkhd", weights, grad_ctx, preferred_element_type=jnp.float32
    ).astype(jnp.bfloat16)
    d_scores = probs * (d_weights - jnp.sum(d_weights * probs, axis=-1, keepdims=True))
    d_scaled = (d_scores * scaling).astype(jnp.bfloat16)
    d_queries = jnp.einsum(
        "bhqk,bkhd->bqhd", d_scaled, key_rows, preferred_element_type=jnp.float32
    ).astype(jnp.bfloat16)
    d_key_rows = jnp.einsum(
        "bhqk,bqhd->bkhd", d_scaled, queries, preferred_element_type=jnp.float32
    ).astype(jnp.bfloat16)
    d_packed = jnp.stack([d_queries, d_key_rows, d_values], axis=2)
    return (context, d_packed.reshape(win_count, win_size, 3 * HEADS * HS))


def local(latent, norm_gain, w_qkv, w_out, cotangent):
    height, breadth, features = latent.shape
    tokens_dev = height * breadth
    latent_f = latent.astype(jnp.float32)
    centred = latent_f - jnp.mean(latent_f, axis=-1, keepdims=True)
    variance = jnp.mean(centred * centred, axis=-1, keepdims=True)
    recip_std = lax.rsqrt(variance + 1e-05)
    normed = centred * recip_std
    scaled_in = (normed * norm_gain).astype(jnp.bfloat16)
    shifted_in = shift_ahead(scaled_in)
    shifted_cot = shift_ahead(cotangent)
    last_row = lax.axis_index("lat") == lax.axis_size("lat") - 1
    wrapped = jnp.logical_and(last_row, jnp.arange(height) >= height - WL // 2).astype(jnp.int32)
    region_grid = jnp.broadcast_to(wrapped[:, None, None], (height, breadth, 1))
    region_win = to_windows(region_grid)[:, :, 0]
    flat_in = shifted_in.reshape(tokens_dev, features)
    flat_cot = shifted_cot.reshape(tokens_dev, features)
    packed = jnp.dot(flat_in, w_qkv, preferred_element_type=jnp.float32).astype(jnp.bfloat16)
    d_context = jnp.einsum("te,de->td", flat_cot, w_out, preferred_element_type=jnp.float32).astype(
        jnp.bfloat16
    )
    context_w, d_packed_w = attend(
        to_windows(packed.reshape(height, breadth, 3 * features)),
        to_windows(d_context.reshape(height, breadth, features)),
        region_win,
    )
    context_flat = from_windows(context_w, height, breadth).reshape(tokens_dev, features)
    attn_out = jnp.dot(context_flat, w_out, preferred_element_type=jnp.float32).astype(jnp.bfloat16)
    grad_out = jnp.einsum("td,te->de", context_flat, flat_cot, preferred_element_type=jnp.float32)
    d_packed_flat = from_windows(d_packed_w, height, breadth).reshape(tokens_dev, 3 * features)
    grad_qkv = jnp.einsum("td,tf->df", flat_in, d_packed_flat, preferred_element_type=jnp.float32)
    d_shifted = jnp.einsum(
        "tf,df->td", d_packed_flat, w_qkv, preferred_element_type=jnp.float32
    ).astype(jnp.bfloat16)
    attn_moved = shift_behind(attn_out.reshape(height, breadth, features))
    d_moved = shift_behind(d_shifted.reshape(height, breadth, features)).astype(jnp.float32)
    mixed = (latent_f + attn_moved.astype(jnp.float32)).astype(jnp.bfloat16)
    grad_gain = jnp.sum(d_moved * normed, axis=(0, 1))
    hidden_grad = d_moved * norm_gain
    d_norm_part = recip_std * (
        hidden_grad
        - jnp.mean(hidden_grad, axis=-1, keepdims=True)
        - normed * jnp.mean(hidden_grad * normed, axis=-1, keepdims=True)
    )
    d_latent = (cotangent.astype(jnp.float32) + d_norm_part).astype(jnp.bfloat16)
    grad_qkv, grad_out, grad_gain = sum_grads((grad_qkv, grad_out, grad_gain))
    return (mixed, d_latent, grad_qkv, grad_out, grad_gain)


def solution(mesh):
    in_specs = (P("lat", "lon", None), P(), P(), P(), P("lat", "lon", None))
    out_specs = (P("lat", "lon", None), P("lat", "lon", None), P(), P(), P())
    return jax.shard_map(local, mesh=mesh, in_specs=in_specs, out_specs=out_specs, check_vma=False)
```

profile of v0, /device:TPU:1, one launch (start us, length us, event | category | flops | bytes accessed | tf_op | source)
XLA Modules:
  0.0 378.5 jit_solution(4275524844844538332)
XLA Ops:
  7.2 1.0 slice.69
  8.2 3.2 collective-permute-start.4
  11.4 1.1 convert_reduce_fusion
  12.5 1.2 fusion.43
  13.7 1.1 fusion.38
  14.9 4.7 %collective-permute-start = (bf16[6,6,512]{2,1,0:T(8,128)(2,1)S(1)}, bf16[6,6,512]{2,1,0:T(8,128)(2,1)S(1)}, u32[]{:S(2)}, u32[]{:S(2)}) collective-permute-start(bf16[6,6,512]{2,1,0:T(8,128)(2,1)S(1)} %slice.77), channel_id=1, source_target_pairs={{0,31},{1,0},{2,1},{3,2},{4,3},{5,4},{6,5},{7,6},{8,7},{9,8},{10,9... | collective-permute-start | bytes 110600 | tf_op jit(solution)/shard_map/ppermute | solution.py:14
  19.5 1.0 slice.68
  20.6 0.1 transpose.46
  20.6 0.1 transpose.47
  20.8 4.9 %collective-permute-start.5 = (bf16[3,48,512]{2,1,0:T(8,128)(2,1)S(1)}, bf16[3,48,512]{2,1,0:T(8,128)(2,1)S(1)}, u32[]{:S(2)}, u32[]{:S(2)}) collective-permute-start(bf16[3,48,512]{2,1,0:T(8,128)(2,1)S(1)} %get-tuple-element.15), channel_id=1, source_target_pairs={{0,224},{32,0},{64,32},{96,64},{128,96},{160,128},{192,160},{224,1... | collective-permute-start | bytes 442376 | tf_op jit(solution)/shard_map/ppermute | solution.py:14
  25.6 0.1 broadcast_compare_fusion
  25.7 0.1 slice.76
  25.8 0.7 fusion.70
  26.6 0.4 collective-permute-start.1
  26.9 1.2 collective-permute-done.5
  28.2 0.3 convolution_convert_fusion.4
  28.6 0.1 reshape_reshape.28
  28.6 0.2 copy.22
  28.9 0.6 reshape_reshape.29
  29.4 2.1 copy.23
  31.6 1.2 collective-permute-done.1
  32.8 1.0 pad_maximum_fusion.3
  33.8 0.7 copy-done.7
  34.5 1.5 convolution_convert_fusion
  36.0 1.3 reshape_reshape.24
  37.3 1.6 copy.15
  38.9 5.1 %reshape_reshape.25 = bf16[4,72,3,16,32]{4,3,2,0,1:T(8,128)(2,1)} reshape(bf16[1,4,6,12,1536]{4,1,3,2,0:T(4,128)(2,1)} %copy.15) | data formatting | bytes 1769472 | tf_op jit(solution)/shard_map/reshape;reshape | solution.py:63
  44.0 4.5 %fusion.82 = (bf16[4,72,1,16,32]{4,3,2,0,1:T(8,128)(2,1)}, bf16[4,72,1,16,32]{4,3,2,0,1:T(8,128)(2,1)S(1)}, bf16[4,72,1,16,32]{4,3,2,0,1:T(8,128)(2,1)}) fusion(bf16[4,72,3,16,32]{4,3,2,0,1:T(8,128)(2,1)} %reshape_reshape.25), kind=kLoop, calls=%fused_computation.92 | loop fusion | bytes 1769472 | tf_op jit(solution)/shard_map/slice | solution.py:64
  48.5 2.9 copy.36
  51.5 2.9 copy.35
  54.4 1.9 copy.34
  56.3 3.5 fusion.54
  59.9 2.6 fusion.83
  62.4 3.2 fusion.19
  65.6 5.5 %fusion.20 = bf16[4,72,1,16,32]{1,4,3,0,2:T(8,128)(2,1)} fusion(f32[4,16,72,72]{2,3,1,0:T(8,128)} %fusion.54, bf16[4,72,1,16,32]{1,4,3,0,2:T(8,128)(2,1)S(1)} %copy-done.11, f32[4,16,72,72]{2,3,1,0:T(8,128)} %get-tuple-element.21, f32[4,16,72]{2,1,0:T(8,128)S(1)} %get-tuple-element.20), kind=kOutput, calls=%fused_computation.18 | convolution fusion | flops 23708232 | bytes 3262464 | tf_op jit(solution)/shard_map/bhqk,bqhd->bkhd/dot_general | solution.py:92
  71.1 5.5 %fusion.23 = bf16[4,72,1,16,32]{1,4,3,0,2:T(8,128)(2,1)} fusion(f32[4,16,72,72]{2,3,1,0:T(8,128)} %fusion.54, bf16[4,72,1,16,32]{1,4,3,0,2:T(8,128)(2,1)S(1)} %copy-done.10, f32[4,16,72,72]{2,3,1,0:T(8,128)} %get-tuple-element.21, f32[4,16,72]{2,1,0:T(8,128)S(1)} %get-tuple-element.20), kind=kOutput, calls=%fused_computation.19 | convolution fusion | flops 23708232 | bytes 3262464 | tf_op jit(solution)/shard_map/bhqk,bkhd->bqhd/dot_general | solution.py:89
  76.7 3.0 fusion.18
  79.7 0.4 pad_maximum_fusion
  80.1 4.0 %copy.28 = bf16[4,72,3,16,32]{4,3,2,0,1:T(8,128)(2,1)} copy(bf16[4,72,3,16,32]{1,4,3,0,2:T(8,128)(2,1)S(1)} %pad_maximum_fusion) | data formatting | bytes 1769472 | tf_op jit(solution)/shard_map/stack | solution.py:95
  84.1 5.8 %reshape_reshape.30 = bf16[1,4,6,12,1536]{4,1,3,2,0:T(4,128)(2,1)} reshape(bf16[4,72,3,16,32]{4,3,2,0,1:T(8,128)(2,1)} %copy.28) | data formatting | bytes 1769472 | tf_op jit(solution)/shard_map/reshape;reshape | solution.py:25
  89.9 1.4 copy.29
  91.3 1.1 reshape_reshape.31
  92.4 2.7 copy.20
  95.1 0.9 reshape_reshape.26
  96.0 0.1 copy.21
  96.0 0.1 reshape_reshape.27
  96.1 3.9 %fusion.88 = f32[512,1536]{1,0:T(8,128)} fusion(bf16[288,512]{1,0:T(8,128)(2,1)} %bitcast.89, bf16[288,1536]{1,0:T(8,128)(2,1)} %reshape_reshape.31), kind=kOutput, calls=%fused_computation.94 | convolution fusion | flops 452984832 | bytes 4325376 | tf_op jit(solution)/shard_map/td,tf->df/dot_general | solution.py:129
  100.1 1.4 fusion.89
  101.5 1.1 copy-done.2
  102.7 0.6 convolution_convert_fusion.3
  103.3 0.1 collective-permute-start.6
  103.4 0.3 copy-done.4
  103.7 0.3 convolution_convert_fusion.5
  104.0 0.1 collective-permute-start.2
  104.1 1.9 collective-permute-done.6
  106.1 2.1 collective-permute-start.7
  108.2 0.6 collective-permute-start.3
  108.9 5.4 %collective-permute-done.7 = bf16[3,48,512]{2,1,0:T(8,128)(2,1)S(1)} collective-permute-done((bf16[3,48,512]{2,1,0:T(8,128)(2,1)S(1)}, bf16[3,48,512]{2,1,0:T(8,128)(2,1)S(1)}, u32[]{:S(2)}, u32[]{:S(2)}) %collective-permute-start.7) | collective-permute-done | bytes 147488 | tf_op jit(solution)/shard_map/ppermute | solution.py:14
  114.2 0.4 fusion.45
  114.7 79.4 %psum.23 = f32[512]{0:T(512)} all-reduce(f32[512]{0:T(512)S(1)} %get-tuple-element.5), channel_id=1, replica_groups=mesh['lat'=8,'lon'=32] {'lat','lon'}, use_global_device_ids=true, to_apply=%region_10.11 | all-reduce | flops 512 | bytes 4096 | tf_op jit(solution)/shard_map/psum | solution.py:58
  194.1 1.1 fusion.42
  195.2 171.7 %all-reduce.3.cloned.1.call-done = (f32[512,1536]{1,0:T(8,128)}, f32[512,512]{1,0:T(8,128)}) async-done(((f32[512,1536]{1,0:T(8,128)}, f32[512,512]{1,0:T(8,128)}), (f32[512,1536]{1,0:T(8,128)}, f32[512,512]{1,0:T(8,128)})) %all-reduce.3.cloned.1.call-update) | async-done | bytes 4194320 | tf_op jit(solution)/shard_map/psum | solution.py:58
  366.9 3.8 %copy.39 = f32[512,1536]{1,0:T(8,128)} copy(f32[512,1536]{1,0:T(8,128)} %get-tuple-element.26) | data formatting | bytes 6291456
  370.7 1.0 copy.40
  (46 shorter events, 0.3 us)
Async XLA Ops:
  7.2 27.3 %copy-start = (bf16[512,1536]{1,0:T(8,128)(2,1)S(1)}, bf16[512,1536]{1,0:T(8,128)(2,1)}, u32[]{:S(2)}) copy-start(bf16[512,1536]{1,0:T(8,128)(2,1)} %param.7) | copy-start | bytes 4718596
  7.2 21.0 %copy-start.3 = (bf16[512,512]{1,0:T(8,128)(2,1)S(1)}, bf16[512,512]{1,0:T(8,128)(2,1)}, u32[]{:S(2)}) copy-start(bf16[512,512]{1,0:T(8,128)(2,1)} %param.8) | copy-start | bytes 1572868
  7.2 359.7 %all-reduce.3.cloned.1.call-start = ((), (), s32[]{:S(2)}) async-start(), calls=%async_computation | async-start | bytes 8388608 | tf_op jit(solution)/shard_map/psum | solution.py:58
  8.2 12.5 %collective-permute-start.4 = (bf16[6,6,512]{2,1,0:T(8,128)(2,1)S(1)}, bf16[6,6,512]{2,1,0:T(8,128)(2,1)S(1)}, u32[]{:S(2)}, u32[]{:S(2)}) collective-permute-start(bf16[6,6,512]{2,1,0:T(8,128)(2,1)S(1)} %slice.69), channel_id=1, source_target_pairs={{0,31},{1,0},{2,1},{3,2},{4,3},{5,4},{6,5},{7,6},{8,7},{9,8},{10,9... | collective-permute-start | bytes 110600 | tf_op jit(solution)/shard_map/ppermute | solution.py:14
  14.9 10.9 %collective-permute-start = (bf16[6,6,512]{2,1,0:T(8,128)(2,1)S(1)}, bf16[6,6,512]{2,1,0:T(8,128)(2,1)S(1)}, u32[]{:S(2)}, u32[]{:S(2)}) collective-permute-start(bf16[6,6,512]{2,1,0:T(8,128)(2,1)S(1)} %slice.77), channel_id=1, source_target_pairs={{0,31},{1,0},{2,1},{3,2},{4,3},{5,4},{6,5},{7,6},{8,7},{9,8},{10,9... | collective-permute-start | bytes 110600 | tf_op jit(solution)/shard_map/ppermute | solution.py:14
  20.8 7.4 %collective-permute-start.5 = (bf16[3,48,512]{2,1,0:T(8,128)(2,1)S(1)}, bf16[3,48,512]{2,1,0:T(8,128)(2,1)S(1)}, u32[]{:S(2)}, u32[]{:S(2)}) collective-permute-start(bf16[3,48,512]{2,1,0:T(8,128)(2,1)S(1)} %get-tuple-element.15), channel_id=1, source_target_pairs={{0,224},{32,0},{64,32},{96,64},{128,96},{160,128},{192,160},{224,1... | collective-permute-start | bytes 442376 | tf_op jit(solution)/shard_map/ppermute | solution.py:14
  26.6 6.2 %collective-permute-start.1 = (bf16[3,48,512]{2,1,0:T(8,128)(2,1)}, bf16[3,48,512]{2,1,0:T(8,128)(2,1)}, u32[]{:S(2)}, u32[]{:S(2)}) collective-permute-start(bf16[3,48,512]{2,1,0:T(8,128)(2,1)} %get-tuple-element.17), channel_id=1, source_target_pairs={{0,224},{32,0},{64,32},{96,64},{128,96},{160,128},{192,160},{224,1... | collective-permute-start | bytes 442376 | tf_op jit(solution)/shard_map/ppermute | solution.py:14
  33.8 0.7 copy-start.7
  56.3 3.5 copy-start.10
  56.3 3.5 copy-start.11
  59.9 2.6 copy-start.5
  71.1 5.5 %copy-start.6 = (bf16[4,72,1,16,32]{1,4,3,0,2:T(8,128)(2,1)S(1)}, bf16[4,72,1,16,32]{1,4,3,0,2:T(8,128)(2,1)}, u32[]{:S(2)}) copy-start(bf16[4,72,1,16,32]{1,4,3,0,2:T(8,128)(2,1)} %copy.34) | copy-start | bytes 884740
  76.6 3.1 copy-start.12
  76.6 3.1 copy-start.13
  76.7 3.1 copy-start.14
  101.5 1.2 copy-start.2
  102.6 1.0 copy-start.4
  102.6 11.6 %copy-start.1 = (bf16[6,48,512]{2,1,0:T(8,128)(2,1)S(1)}, bf16[6,48,512]{2,1,0:T(8,128)(2,1)}, u32[]{:S(2)}) copy-start(bf16[6,48,512]{2,1,0:T(8,128)(2,1)} %param.5) | copy-start | bytes 884740
  102.7 11.6 %copy-start.15 = (f32[512]{0:T(512)S(1)}, f32[512]{0:T(512)}, u32[]{:S(2)}) copy-start(f32[512]{0:T(512)} %param.6) | copy-start | bytes 6148
  103.3 90.8 %copy-start.8 = (bf16[6,48,512]{2,1,0:T(8,128)(2,1)S(1)}, bf16[6,48,512]{2,1,0:T(8,128)(2,1)}, u32[]{:S(2)}) copy-start(bf16[6,48,512]{2,1,0:T(8,128)(2,1)} %param.9) | copy-start | bytes 884740
  103.3 2.7 collective-permute-start.6
  104.0 4.2 %collective-permute-start.2 = (bf16[6,6,512]{2,1,0:T(8,128)(2,1)S(1)}, bf16[6,6,512]{2,1,0:T(8,128)(2,1)S(1)}, u32[]{:S(2)}, u32[]{:S(2)}) collective-permute-start(bf16[6,6,512]{2,1,0:T(8,128)(2,1)S(1)} %slice.83), channel_id=1, source_target_pairs={{0,1},{1,2},{2,3},{3,4},{4,5},{5,6},{6,7},{7,8},{8,9},{9,10},{10,1... | collective-permute-start | bytes 110600 | tf_op jit(solution)/shard_map/ppermute | solution.py:14
  106.1 8.2 %collective-permute-start.7 = (bf16[3,48,512]{2,1,0:T(8,128)(2,1)S(1)}, bf16[3,48,512]{2,1,0:T(8,128)(2,1)S(1)}, u32[]{:S(2)}, u32[]{:S(2)}) collective-permute-start(bf16[3,48,512]{2,1,0:T(8,128)(2,1)S(1)} %fusion.67), channel_id=1, source_target_pairs={{0,32},{32,64},{64,96},{96,128},{128,160},{160,192},{192,224},{224... | collective-permute-start | bytes 442376 | tf_op jit(solution)/shard_map/ppermute | solution.py:14
  108.2 85.9 %collective-permute-start.3 = (bf16[3,48,512]{2,1,0:T(8,128)(2,1)S(1)}, bf16[3,48,512]{2,1,0:T(8,128)(2,1)S(1)}, u32[]{:S(2)}, u32[]{:S(2)}) collective-permute-start(bf16[3,48,512]{2,1,0:T(8,128)(2,1)S(1)} %fusion.69), channel_id=1, source_target_pairs={{0,32},{32,64},{64,96},{96,128},{128,160},{160,192},{192,224},{224... | collective-permute-start | bytes 442376 | tf_op jit(solution)/shard_map/ppermute | solution.py:14
  366.9 3.8 %copy-start.9 = (f32[512,512]{1,0:T(8,128)S(1)}, f32[512,512]{1,0:T(8,128)}, u32[]{:S(2)}) copy-start(f32[512,512]{1,0:T(8,128)} %get-tuple-element.27) | copy-start | bytes 3145732
Sparse Core Ops, SparseCore 0:
  101.6 265.2 all-reduce.2
where the time goes:
time: 380 us; the launch traced here: 379 us
  waiting for transfers between devices  181 us (48%)
  blocking collectives  79.4 us (21%)
  local copies, waits for them, and re-layouts  48.5 us (13%)
  matrix products  31.5 us (8%)
  starting transfers between devices  16.1 us (4%)
  between operations  14.4 us (4%)
  other arithmetic  7.31 us (2%)
    psum x1, waiting for transfers between devices, sum_grads(): lax.psum((grad_items[0], grad_items[1], grad_items[2]), ('lat', 'lon'))  172 us
    psum x1, blocking collectives, sum_grads(): lax.psum((grad_items[0], grad_items[1], grad_items[2]), ('lat', 'lon'))  79.4 us
    ppermute x8, starting transfers between devices, passed_along(): lax.ppermute(value, axis, [(i, (i + by) % devices) for i in range(devices)])  16.1 us
    unnamed x37, local copies, waits for them, and re-layouts  14.8 us
    ppermute x8, waiting for transfers between devices, passed_along(): lax.ppermute(value, axis, [(i, (i + by) % devices) for i in range(devices)])  9.7 us
  transfers between devices with their start and end apart: 9, of which 5 were waited for; matrix products, arithmetic and copies ran while one was open for 3% of the time, Pallas kernels for 0%

commit v1 on v0

--- a/solution.py
+++ b/solution.py
@@ -1,8 +1,11 @@
 import jax
 import jax.numpy as jnp
 from jax import lax
-from jax.sharding import PartitionSpec as P
+from jax.sharding import Mesh, PartitionSpec as P
 
+ALL = ("x", "yh", "yl", "z", "c")
+LAT = ("x", "yh")
+LON = ("yl", "z", "c")
 HEADS = 16
 HS = 32
 WL = 6
@@ -10,7 +13,7 @@
 
 
 def passed_along(value, axis, by):
-    devices = lax.axis_size(axis)
+    devices = 8 if axis == LAT else 32
     return lax.ppermute(value, axis, [(i, (i + by) % devices) for i in range(devices)])
 
 
@@ -27,22 +30,22 @@
 
 
 def lon_ahead(block_in):
-    arrived = passed_along(block_in[:, : WW // 2], "lon", -1)
+    arrived = passed_along(block_in[:, : WW // 2], LON, -1)
     return jnp.concatenate([block_in[:, WW // 2 :], arrived], axis=1)
 
 
 def lat_ahead(block_in):
-    arrived = passed_along(block_in[: WL // 2], "lat", -1)
+    arrived = passed_along(block_in[: WL // 2], LAT, -1)
     return jnp.concatenate([block_in[WL // 2 :], arrived], axis=0)
 
 
 def lon_behind(block_in):
-    arrived = passed_along(block_in[:, -(WW // 2) :], "lon", 1)
+    arrived = passed_along(block_in[:, -(WW // 2) :], LON, 1)
     return jnp.concatenate([arrived, block_in[:, : -(WW // 2)]], axis=1)
 
 
 def lat_behind(block_in):
-    arrived = passed_along(block_in[-(WL // 2) :], "lat", 1)
+    arrived = passed_along(block_in[-(WL // 2) :], LAT, 1)
     return jnp.concatenate([arrived, block_in[: -(WL // 2)]], axis=0)
 
 
@@ -54,8 +57,47 @@
     return lat_behind(lon_behind(block_in))
 
 
+def flat_perm(mesh_ids):
+    return [(i, int(j)) for i, j in enumerate(mesh_ids)]
+
+
+def core_swap():
+    return flat_perm([i ^ 1 for i in range(256)])
+
+
+def z_swap(bit):
+    return flat_perm([i ^ (2 * bit) for i in range(256)])
+
+
 def sum_grads(grad_items):
-    return lax.psum((grad_items[0], grad_items[1], grad_items[2]), ("lat", "lon"))
+    grad_qkv, grad_out, grad_gain = grad_items
+    strips = jnp.concatenate([grad_qkv, grad_out], axis=1).astype(jnp.bfloat16)
+    strips = strips.reshape(512, 16, 128).transpose(1, 0, 2).reshape(8192, 128)
+    core = lax.axis_index("c")
+    mine = lax.dynamic_slice_in_dim(strips, core * 4096, 4096, 0)
+    other = lax.dynamic_slice_in_dim(strips, (1 - core) * 4096, 4096, 0)
+    arrived = lax.ppermute(other, ALL, core_swap())
+    half = (mine.astype(jnp.float32) + arrived.astype(jnp.float32)).astype(jnp.bfloat16)
+    gain = jnp.pad(grad_gain.reshape(4, 128), ((0, 12), (0, 0))).astype(jnp.bfloat16)
+    gain_in = lax.ppermute(gain, ALL, core_swap())
+    gain = (gain.astype(jnp.float32) + gain_in.astype(jnp.float32)).astype(jnp.bfloat16)
+    chunks = jnp.concatenate(
+        [half.reshape(16, 256, 128), jnp.broadcast_to(gain, (16, 16, 128))], axis=1
+    )
+    pieces = lax.all_to_all(chunks, ("x", "yh", "yl"), 0, 0, tiled=True)
+    total = jnp.sum(pieces.astype(jnp.float32), axis=0).astype(jnp.bfloat16)
+    for bit in (1, 2, 4):
+        arrived = lax.ppermute(total, ALL, z_swap(bit))
+        total = (total.astype(jnp.float32) + arrived.astype(jnp.float32)).astype(jnp.bfloat16)
+    spread = jnp.broadcast_to(total, (16, 272, 128))
+    half = lax.all_to_all(spread, ("x", "yh", "yl"), 0, 0, tiled=True)
+    arrived = lax.ppermute(half, ALL, core_swap())
+    low = jnp.where(core == 0, half, arrived)
+    high = jnp.where(core == 0, arrived, half)
+    grad_gain = low[0, 256:260].reshape(512).astype(jnp.float32)
+    whole = jnp.concatenate([low[:, :256], high[:, :256]], axis=0).reshape(16, 512, 128)
+    whole = whole.transpose(1, 0, 2).reshape(512, 2048).astype(jnp.float32)
+    return whole[:, :1536], whole[:, 1536:], grad_gain
 
 
 def attend(packed, d_context, region):
@@ -107,7 +149,7 @@
     scaled_in = (normed * norm_gain).astype(jnp.bfloat16)
     shifted_in = shift_ahead(scaled_in)
     shifted_cot = shift_ahead(cotangent)
-    last_row = lax.axis_index("lat") == lax.axis_size("lat") - 1
+    last_row = lax.axis_index(LAT) == 7
     wrapped = jnp.logical_and(last_row, jnp.arange(height) >= height - WL // 2).astype(jnp.int32)
     region_grid = jnp.broadcast_to(wrapped[:, None, None], (height, breadth, 1))
     region_win = to_windows(region_grid)[:, :, 0]
@@ -146,6 +188,7 @@
 
 
 def solution(mesh):
-    in_specs = (P("lat", "lon", None), P(), P(), P(), P("lat", "lon", None))
-    out_specs = (P("lat", "lon", None), P("lat", "lon", None), P(), P(), P())
-    return jax.shard_map(local, mesh=mesh, in_specs=in_specs, out_specs=out_specs, check_vma=False)
+    fine = Mesh(mesh.devices.reshape(4, 2, 2, 8, 2), ALL)
+    in_specs = (P(LAT, LON, None), P(), P(), P(), P(LAT, LON, None))
+    out_specs = (P(LAT, LON, None), P(LAT, LON, None), P(), P(), P())
+    return jax.shard_map(local, mesh=fine, in_specs=in_specs, out_specs=out_specs, check_vma=False)

time: 380 us -> 210 us (0.55)
  waiting for transfers between devices: 181 us -> 33.9 us
  blocking collectives: 79.4 us -> 36.9 us
  starting transfers between devices: 16.1 us -> 31 us
  between operations: 14.4 us -> 1.12 us
  other arithmetic: 7.31 us -> 18.7 us
  local copies, waits for them, and re-layouts: 48.5 us -> 58.6 us
    psum x1 -> x0, waiting for transfers between devices: 172 us -> none  [sum_grads(): lax.psum((grad_items[0], grad_items[1], grad_items[2]), ('lat', 'lon'))]
    psum x1 -> x0, blocking collectives: 79.4 us -> none  [sum_grads(): lax.psum((grad_items[0], grad_items[1], grad_items[2]), ('lat', 'lon'))]
    all_to_all x0 -> x2, blocking collectives: none -> 36.9 us  [the longest x1 21.5 us: sum_grads(): pieces = lax.all_to_all(chunks, ('x', 'yh', 'yl'), 0, 0, tiled=True)]
    ppermute x0 -> x6, waiting for transfers between devices: none -> 15.5 us  [the longest x3 14.7 us: sum_grads(): arrived = lax.ppermute(total, ALL, z_swap(bit))]
    ppermute x0 -> x6, starting transfers between devices: none -> 14.4 us  [the longest x1 6.65 us: sum_grads(): arrived = lax.ppermute(half, ALL, core_swap())]
    ppermute x8, waiting for transfers between devices: 9.7 us -> 18.3 us  [passed_along(): lax.ppermute(value, axis, [(i, (i + by) % devices) for i in range(devices)])]
    convert_element_type x0 -> x8, other arithmetic: none -> 5.42 us  [the longest x1 2.41 us: sum_grads(): whole = whole.transpose(1, 0, 2).reshape(512, 2048).astype(jnp.float32)]
    convert_element_type x0 -> x1, local copies, waits for them, and re-layouts: none -> 5.35 us  [sum_grads(): whole = whole.transpose(1, 0, 2).reshape(512, 2048).astype(jnp.float32)]
  transfers between devices with their start and end apart: 9 -> 14, of which waited for: 5 -> 10; matrix products, arithmetic and copies ran while one was open for 3% -> 6% of each run, Pallas kernels for 0% -> 0%
where the time goes in v1:
time: 210 us; the launch traced here: 208 us
  local copies, waits for them, and re-layouts  58.6 us (28%)
  blocking collectives  36.9 us (18%)
  waiting for transfers between devices  33.9 us (16%)
  starting transfers between devices  31 us (15%)
  matrix products  27.9 us (13%)
  other arithmetic  18.7 us (9%)
    all_to_all x1, blocking collectives, sum_grads(): pieces = lax.all_to_all(chunks, ('x', 'yh', 'yl'), 0, 0, tiled=True)  21.5 us
    ppermute x8, waiting for transfers between devices, passed_along(): lax.ppermute(value, axis, [(i, (i + by) % devices) for i in range(devices)])  18.3 us
    ppermute x8, starting transfers between devices, passed_along(): lax.ppermute(value, axis, [(i, (i + by) % devices) for i in range(devices)])  16.5 us
    all_to_all x1, blocking collectives, sum_grads(): half = lax.all_to_all(spread, ('x', 'yh', 'yl'), 0, 0, tiled=True)  15.4 us
    unnamed x39, local copies, waits for them, and re-layouts  14.9 us
    ppermute x3, waiting for transfers between devices, sum_grads(): arrived = lax.ppermute(total, ALL, z_swap(bit))  14.7 us
    another operation x2, local copies, waits for them, and re-layouts, from_windows(): blocks = stacked.reshape(height // WL, breadth // WW, WL, WW, features)  6.67 us
    ppermute x1, starting transfers between devices, sum_grads(): arrived = lax.ppermute(half, ALL, core_swap())  6.65 us
  transfers between devices with their start and end apart: 14, of which 10 were waited for; matrix products, arithmetic and copies ran while one was open for 6% of the time, Pallas kernels for 0%

profile of v1, /device:TPU:1, one launch (start us, length us, event | category | flops | bytes accessed | tf_op | source)
XLA Modules:
  0.0 208.1 jit_solution(15331763401310896579)
XLA Ops:
  0.6 0.9 slice.84
  1.6 3.2 %collective-permute-start.4 = (bf16[6,6,512]{2,1,0:T(8,128)(2,1)S(1)}, bf16[6,6,512]{2,1,0:T(8,128)(2,1)S(1)}, u32[]{:S(2)}, u32[]{:S(2)}) collective-permute-start(bf16[6,6,512]{2,1,0:T(8,128)(2,1)S(1)} %slice.84), channel_id=1, source_target_pairs={{0,31},{1,0},{2,1},{3,2},{4,3},{5,4},{6,5},{7,6},{8,7},{9,8},{10,9... | collective-permute-start | bytes 110600 | tf_op jit(solution)/shard_map/ppermute | solution.py:17
  4.8 1.1 convert_reduce_fusion
  5.9 1.2 fusion.43
  7.1 1.1 fusion.38
  8.3 4.7 %collective-permute-start = (bf16[6,6,512]{2,1,0:T(8,128)(2,1)S(1)}, bf16[6,6,512]{2,1,0:T(8,128)(2,1)S(1)}, u32[]{:S(2)}, u32[]{:S(2)}) collective-permute-start(bf16[6,6,512]{2,1,0:T(8,128)(2,1)S(1)} %slice.97), channel_id=1, source_target_pairs={{0,31},{1,0},{2,1},{3,2},{4,3},{5,4},{6,5},{7,6},{8,7},{9,8},{10,9... | collective-permute-start | bytes 110600 | tf_op jit(solution)/shard_map/ppermute | solution.py:17
  12.9 1.0 slice.83
  14.1 4.9 %collective-permute-start.5 = (bf16[3,48,512]{2,1,0:T(8,128)(2,1)S(1)}, bf16[3,48,512]{2,1,0:T(8,128)(2,1)S(1)}, u32[]{:S(2)}, u32[]{:S(2)}) collective-permute-start(bf16[3,48,512]{2,1,0:T(8,128)(2,1)S(1)} %get-tuple-element.18), channel_id=1, source_target_pairs={{0,224},{32,0},{64,32},{96,64},{128,96},{160,128},{192,160},{224,1... | collective-permute-start | bytes 442376 | tf_op jit(solution)/shard_map/ppermute | solution.py:17
  20.3 1.3 collective-permute-done.5
  21.6 0.7 copy-done.6
  23.5 1.3 copy.41
  24.8 1.3 collective-permute-done.1
  26.1 0.9 pad_maximum_fusion.5
  27.1 0.7 copy-done.14
  27.8 1.5 convolution_convert_fusion.1
  29.3 1.3 reshape_reshape.24
  30.6 1.6 copy.33
  32.2 5.1 %reshape_reshape.25 = bf16[4,72,3,16,32]{4,3,2,0,1:T(8,128)(2,1)} reshape(bf16[1,4,6,12,1536]{4,1,3,2,0:T(4,128)(2,1)} %copy.33) | data formatting | bytes 1769472 | tf_op jit(solution)/shard_map/reshape;reshape | solution.py:105
  37.3 4.3 %fusion.83 = (bf16[4,72,1,16,32]{4,3,2,0,1:T(8,128)(2,1)}, bf16[4,72,1,16,32]{4,3,2,0,1:T(8,128)(2,1)}, bf16[4,72,1,16,32]{4,3,2,0,1:T(8,128)(2,1)S(1)}) fusion(bf16[4,72,3,16,32]{4,3,2,0,1:T(8,128)(2,1)} %reshape_reshape.25), kind=kLoop, calls=%fused_computation.110 | loop fusion | bytes 1769472 | tf_op jit(solution)/shard_map/slice | solution.py:106
  41.6 2.9 %copy.59 = bf16[4,72,1,16,32]{1,4,3,0,2:T(8,128)(2,1)} copy(bf16[4,72,1,16,32]{4,3,2,0,1:T(8,128)(2,1)} %get-tuple-element.14) | data formatting | bytes 589824
  44.5 2.9 %copy.58 = bf16[4,72,1,16,32]{1,4,3,0,2:T(8,128)(2,1)} copy(bf16[4,72,1,16,32]{4,3,2,0,1:T(8,128)(2,1)} %get-tuple-element.15) | data formatting | bytes 589824
  47.5 2.0 copy.60
  49.4 3.7 %fusion.84 = (f32[4,16,72]{2,1,0:T(8,128)S(1)}, f32[4,16,72,72]{2,3,1,0:T(8,128)}) fusion(pred[4,72,72]{1,2,0:T(8,128)(4,1)S(1)} %broadcast_compare_fusion, bf16[4,72,1,16,32]{1,4,3,0,2:T(8,128)(2,1)} %copy.60, bf16[4,72,1,16,32]{1,4,3,0,2:T(8,128)(2,1)} %copy.59), kind=kOutput, calls=%fused_computation.111 | convolution fusion | flops 22560840 | bytes 1956096 | tf_op jit(solution)/shard_map/sub | solution.py:117
  53.2 3.3 %fusion.19 = bf16[4,72,1,16,32]{1,4,3,0,2:T(8,128)(2,1)} fusion(bf16[4,72,16,32]{1,3,2,0:T(8,128)(2,1)S(1)} %copy.41, f32[4,16,72,72]{2,3,1,0:T(8,128)} %get-tuple-element.24, f32[4,16,72]{2,1,0:T(8,128)S(1)} %get-tuple-element.23), kind=kOutput, calls=%fused_computation.24 | convolution fusion | flops 22044672 | bytes 1935360 | tf_op jit(solution)/shard_map/bhqk,bqhd->bkhd/dot_general | solution.py:126
  56.5 1.3 fusion.18
  57.8 2.2 %fusion.54 = f32[4,16,72,72]{2,3,1,0:T(8,128)} fusion(bf16[4,72,16,32]{1,3,2,0:T(8,128)(2,1)S(1)} %copy.41, bf16[4,72,1,16,32]{1,4,3,0,2:T(8,128)(2,1)S(1)} %copy-done.5), kind=kOutput, calls=%fused_computation.67 | convolution fusion | flops 21233664 | bytes 1916928 | tf_op jit(solution)/shard_map/bqhd,bkhd->bhqk/dot_general | solution.py:125
  60.1 5.5 %fusion.23 = bf16[4,72,1,16,32]{1,4,3,0,2:T(8,128)(2,1)} fusion(f32[4,16,72,72]{2,3,1,0:T(8,128)} %fusion.54, bf16[4,72,1,16,32]{1,4,3,0,2:T(8,128)(2,1)S(1)} %copy-done.12, f32[4,16,72,72]{2,3,1,0:T(8,128)} %get-tuple-element.24, f32[4,16,72]{2,1,0:T(8,128)S(1)} %get-tuple-element.23), kind=kOutput, calls=%fused_computation.26 | convolution fusion | flops 23708232 | bytes 3262464 | tf_op jit(solution)/shard_map/bhqk,bkhd->bqhd/dot_general | solution.py:131
  65.6 5.4 %fusion.20 = bf16[4,72,1,16,32]{1,4,3,0,2:T(8,128)(2,1)} fusion(f32[4,16,72,72]{2,3,1,0:T(8,128)} %fusion.54, bf16[4,72,1,16,32]{1,4,3,0,2:T(8,128)(2,1)S(1)} %copy-done.11, f32[4,16,72,72]{2,3,1,0:T(8,128)} %get-tuple-element.24, f32[4,16,72]{2,1,0:T(8,128)S(1)} %get-tuple-element.23), kind=kOutput, calls=%fused_computation.25 | convolution fusion | flops 23708232 | bytes 3262464 | tf_op jit(solution)/shard_map/bhqk,bqhd->bkhd/dot_general | solution.py:134
  71.0 2.9 %copy.38 = bf16[4,72,16,32]{3,2,0,1:T(8,128)(2,1)S(1)} copy(bf16[4,72,16,32]{1,3,2,0:T(8,128)(2,1)} %fusion.18) | data formatting | bytes 589824 | tf_op jit(solution)/shard_map/convert_element_type | solution.py:122
  73.9 0.9 reshape_reshape.26
  75.0 0.7 copy-done.8
  75.7 1.3 convolution_convert_fusion.2
  77.0 1.7 pad_maximum_fusion.1
  78.7 4.0 %copy.46 = bf16[4,72,3,16,32]{4,3,2,0,1:T(8,128)(2,1)} copy(bf16[4,72,3,16,32]{1,4,3,0,2:T(8,128)(2,1)S(1)} %pad_maximum_fusion.1) | data formatting | bytes 1769472 | tf_op jit(solution)/shard_map/stack | solution.py:137
  82.7 5.8 %reshape_reshape.30 = bf16[1,4,6,12,1536]{4,1,3,2,0:T(4,128)(2,1)} reshape(bf16[4,72,3,16,32]{4,3,2,0,1:T(8,128)(2,1)} %copy.46) | data formatting | bytes 1769472 | tf_op jit(solution)/shard_map/reshape;reshape | solution.py:28
  88.5 1.4 copy.47
  89.8 1.1 reshape_reshape.31
  91.0 2.3 %convolution_convert_fusion = bf16[512,1536]{1,0:T(8,128)(2,1)S(1)} fusion(bf16[288,512]{1,0:T(8,128)(2,1)} %bitcast.124, bf16[288,1536]{1,0:T(8,128)(2,1)} %reshape_reshape.31), kind=kOutput, calls=%fused_computation.3 | convolution fusion | flops 453771264 | bytes 2752512 | tf_op jit(solution)/shard_map/td,tf->df/dot_general | solution.py:171
  93.9 2.0 collective-permute-start.8
  96.6 1.4 collective-permute-done.6
  98.1 2.0 collective-permute-start.7
  100.2 5.9 %collective-permute-done.7 = bf16[3,48,512]{2,1,0:T(8,128)(2,1)S(1)} collective-permute-done((bf16[3,48,512]{2,1,0:T(8,128)(2,1)S(1)}, bf16[3,48,512]{2,1,0:T(8,128)(2,1)S(1)}, u32[]{:S(2)}, u32[]{:S(2)}) %collective-permute-start.7) | collective-permute-done | bytes 147488 | tf_op jit(solution)/shard_map/ppermute | solution.py:17
  106.1 1.0 fusion.45
  107.2 5.6 %collective-permute-start.9 = (bf16[16,128]{1,0:T(8,128)(2,1)S(1)}, bf16[16,128]{1,0:T(8,128)(2,1)S(1)}, u32[]{:S(2)}, u32[]{:S(2)}) collective-permute-start(bf16[16,128]{1,0:T(8,128)(2,1)S(1)} %pad.5), channel_id=1, source_target_pairs={{0,1},{1,0},{2,3},{3,2},{4,5},{5,4},{6,7},{7,6},{8,9},{9,8},{10,11... | collective-permute-start | bytes 12296 | tf_op jit(solution)/shard_map/ppermute | solution.py:82
  112.7 0.8 collective-permute-done.9
  113.6 1.8 add_convert_fusion
  115.5 21.5 %all_to_all.10 = bf16[16,272,128]{2,1,0:T(8,128)(2,1)S(1)} all-to-all(bf16[16,272,128]{2,1,0:T(8,128)(2,1)S(1)} %pad_maximum_fusion.2), channel_id=1, replica_groups=mesh['x'=4,'yh'=2,'yl'=2,'z'=8,'c'=2] {'x','yh','yl'}, dimensions={0} | all-to-all | bytes 2228224 | tf_op jit(solution)/shard_map/all_to_all | solution.py:87
  137.3 3.1 %collective-permute-done.10 = bf16[272,128]{1,0:T(8,128)(2,1)S(1)} collective-permute-done((bf16[272,128]{1,0:T(8,128)(2,1)S(1)}, bf16[272,128]{1,0:T(8,128)(2,1)S(1)}, u32[]{:S(2)}, u32[]{:S(2)}) %collective-permute-start.10) | collective-permute-done | bytes 69664 | tf_op jit(solution)/shard_map/ppermute | solution.py:90
  140.5 4.5 %collective-permute-done.11 = bf16[272,128]{1,0:T(8,128)(2,1)S(1)} collective-permute-done((bf16[272,128]{1,0:T(8,128)(2,1)S(1)}, bf16[272,128]{1,0:T(8,128)(2,1)S(1)}, u32[]{:S(2)}, u32[]{:S(2)}) %collective-permute-start.11) | collective-permute-done | bytes 69664 | tf_op jit(solution)/shard_map/ppermute | solution.py:90
  145.2 7.1 %collective-permute-done.12 = bf16[272,128]{1,0:T(8,128)(2,1)S(1)} collective-permute-done((bf16[272,128]{1,0:T(8,128)(2,1)S(1)}, bf16[272,128]{1,0:T(8,128)(2,1)S(1)}, u32[]{:S(2)}, u32[]{:S(2)}) %collective-permute-start.12) | collective-permute-done | bytes 69664 | tf_op jit(solution)/shard_map/ppermute | solution.py:90
  152.4 15.4 %all_to_all.11 = bf16[16,272,128]{2,1,0:T(8,128)(2,1)S(1)} all-to-all(bf16[16,272,128]{2,1,0:T(8,128)(2,1)S(1)} %broadcast_in_dim.19), channel_id=1, replica_groups=mesh['x'=4,'yh'=2,'yl'=2,'z'=8,'c'=2] {'x','yh','yl'}, dimensions={0} | all-to-all | bytes 2228224 | tf_op jit(solution)/shard_map/all_to_all | solution.py:93
  167.8 6.7 %collective-permute-start.13 = (bf16[16,272,128]{2,1,0:T(8,128)(2,1)S(1)}, bf16[16,272,128]{2,1,0:T(8,128)(2,1)}, u32[]{:S(2)}, u32[]{:S(2)}) collective-permute-start(bf16[16,272,128]{2,1,0:T(8,128)(2,1)S(1)} %all_to_all.11), channel_id=1, source_target_pairs={{0,1},{1,0},{2,3},{3,2},{4,5},{5,4},{6,7},{7,6},{8,9},{9,8},{10,11... | collective-permute-start | bytes 3342344 | tf_op jit(solution)/shard_map/ppermute | solution.py:94
  174.9 1.9 collective-permute-done.2
  176.9 1.2 collective-permute-start.3
  178.1 6.5 %collective-permute-done.3 = bf16[3,48,512]{2,1,0:T(8,128)(2,1)S(1)} collective-permute-done((bf16[3,48,512]{2,1,0:T(8,128)(2,1)S(1)}, bf16[3,48,512]{2,1,0:T(8,128)(2,1)S(1)}, u32[]{:S(2)}, u32[]{:S(2)}) %collective-permute-start.3) | collective-permute-done | bytes 147488 | tf_op jit(solution)/shard_map/ppermute | solution.py:17
  184.5 2.2 %fusion.42 = (bf16[6,48,512]{2,1,0:T(8,128)(2,1)}, bf16[6,48,512]{2,1,0:T(8,128)(2,1)}) fusion(bf16[6,48,512]{2,1,0:T(8,128)(2,1)S(1)} %copy-done.2, bf16[6,48,512]{2,1,0:T(8,128)(2,1)} %get-tuple-element.13, bf16[6,48,512]{2,1,0:T(8,128)(2,1)} %param.9, f32[6,48]{1,0:T(8,128)S(1)} %get-tuple-element.25, f32[6,48]{1,0:T(8,128)S(1)} %get-tuple-element.26, ...), kind=kLoop, calls=%fused_computation.55 | loop fusion | flops 2949120 | bytes 1923584 | tf_op jit(solution)/shard_map/convert_element_type | solution.py:185
  186.7 1.4 broadcast_select_fusion
  188.8 1.3 slice_select_fusion
  190.3 2.4 %convert_bitcast_fusion = f32[512,16,128]{2,0,1:T(8,128)} fusion(bf16[16,512,128]{2,1,0:T(8,128)(2,1)S(1)} %bitcast.107), kind=kLoop, calls=%fused_computation.2 | loop fusion | flops 1048576 | bytes 6291456 | tf_op jit(solution)/shard_map/convert_element_type | solution.py:99
  192.7 5.3 %copy.50 = f32[512,16,128]{0,2,1:T(8,128)} copy(f32[512,16,128]{2,0,1:T(8,128)} %convert_bitcast_fusion) | data formatting | bytes 8388608 | tf_op jit(solution)/shard_map/convert_element_type | solution.py:99
  198.1 1.3 slice.117
  199.4 3.9 %slice.116 = f32[512,1536]{0,1:T(8,128)} slice(f32[512,2048]{0,1:T(8,128)} %bitcast.106), slice={[0:512], [0:1536]} | slice | bytes 6291456 | tf_op jit(solution)/shard_map/slice | solution.py:100
  203.2 3.5 %copy.51 = f32[512,1536]{1,0:T(8,128)} copy(f32[512,1536]{0,1:T(8,128)} %slice.116) | data formatting | bytes 6291456
  206.8 1.3 copy.52
  (79 shorter events, 6.3 us)
Async XLA Ops:
  0.6 27.2 %copy-start = (bf16[512,1536]{1,0:T(8,128)(2,1)S(1)}, bf16[512,1536]{1,0:T(8,128)(2,1)}, u32[]{:S(2)}) copy-start(bf16[512,1536]{1,0:T(8,128)(2,1)} %param.7) | copy-start | bytes 4718596
  1.6 20.7 %copy-start.3 = (bf16[512,512]{1,0:T(8,128)(2,1)S(1)}, bf16[512,512]{1,0:T(8,128)(2,1)}, u32[]{:S(2)}) copy-start(bf16[512,512]{1,0:T(8,128)(2,1)} %param.8) | copy-start | bytes 1572868
  1.6 12.5 %collective-permute-start.4 = (bf16[6,6,512]{2,1,0:T(8,128)(2,1)S(1)}, bf16[6,6,512]{2,1,0:T(8,128)(2,1)S(1)}, u32[]{:S(2)}, u32[]{:S(2)}) collective-permute-start(bf16[6,6,512]{2,1,0:T(8,128)(2,1)S(1)} %slice.84), channel_id=1, source_target_pairs={{0,31},{1,0},{2,1},{3,2},{4,3},{5,4},{6,5},{7,6},{8,7},{9,8},{10,9... | collective-permute-start | bytes 110600 | tf_op jit(solution)/shard_map/ppermute | solution.py:17
  8.3 10.9 %collective-permute-start = (bf16[6,6,512]{2,1,0:T(8,128)(2,1)S(1)}, bf16[6,6,512]{2,1,0:T(8,128)(2,1)S(1)}, u32[]{:S(2)}, u32[]{:S(2)}) collective-permute-start(bf16[6,6,512]{2,1,0:T(8,128)(2,1)S(1)} %slice.97), channel_id=1, source_target_pairs={{0,31},{1,0},{2,1},{3,2},{4,3},{5,4},{6,5},{7,6},{8,7},{9,8},{10,9... | collective-permute-start | bytes 110600 | tf_op jit(solution)/shard_map/ppermute | solution.py:17
  14.1 7.4 %collective-permute-start.5 = (bf16[3,48,512]{2,1,0:T(8,128)(2,1)S(1)}, bf16[3,48,512]{2,1,0:T(8,128)(2,1)S(1)}, u32[]{:S(2)}, u32[]{:S(2)}) collective-permute-start(bf16[3,48,512]{2,1,0:T(8,128)(2,1)S(1)} %get-tuple-element.18), channel_id=1, source_target_pairs={{0,224},{32,0},{64,32},{96,64},{128,96},{160,128},{192,160},{224,1... | collective-permute-start | bytes 442376 | tf_op jit(solution)/shard_map/ppermute | solution.py:17
  19.9 6.2 %collective-permute-start.1 = (bf16[3,48,512]{2,1,0:T(8,128)(2,1)}, bf16[3,48,512]{2,1,0:T(8,128)(2,1)}, u32[]{:S(2)}, u32[]{:S(2)}) collective-permute-start(bf16[3,48,512]{2,1,0:T(8,128)(2,1)} %get-tuple-element.20), channel_id=1, source_target_pairs={{0,224},{32,0},{64,32},{96,64},{128,96},{160,128},{192,160},{224,1... | collective-permute-start | bytes 442376 | tf_op jit(solution)/shard_map/ppermute | solution.py:17
  21.6 0.7 copy-start.6
  27.1 0.7 copy-start.14
  53.2 3.4 %copy-start.5 = (bf16[4,72,1,16,32]{1,4,3,0,2:T(8,128)(2,1)S(1)}, bf16[4,72,1,16,32]{1,4,3,0,2:T(8,128)(2,1)}, u32[]{:S(2)}) copy-start(bf16[4,72,1,16,32]{1,4,3,0,2:T(8,128)(2,1)} %copy.58) | copy-start | bytes 884740
  53.2 3.4 %copy-start.16 = (f32[4,16,72,72]{2,3,1,0:T(8,128)S(1)}, f32[4,16,72,72]{2,3,1,0:T(8,128)}, u32[]{:S(2)}) copy-start(f32[4,16,72,72]{2,3,1,0:T(8,128)} %get-tuple-element.24) | copy-start | bytes 3981316
  57.8 2.2 %copy-start.12 = (bf16[4,72,1,16,32]{1,4,3,0,2:T(8,128)(2,1)S(1)}, bf16[4,72,1,16,32]{1,4,3,0,2:T(8,128)(2,1)}, u32[]{:S(2)}) copy-start(bf16[4,72,1,16,32]{1,4,3,0,2:T(8,128)(2,1)} %copy.60) | copy-start | bytes 884740
  60.1 5.5 %copy-start.11 = (bf16[4,72,1,16,32]{1,4,3,0,2:T(8,128)(2,1)S(1)}, bf16[4,72,1,16,32]{1,4,3,0,2:T(8,128)(2,1)}, u32[]{:S(2)}) copy-start(bf16[4,72,1,16,32]{1,4,3,0,2:T(8,128)(2,1)} %copy.59) | copy-start | bytes 884740
  71.0 4.7 %copy-start.7 = (bf16[6,48,512]{2,1,0:T(8,128)(2,1)S(1)}, bf16[6,48,512]{2,1,0:T(8,128)(2,1)}, u32[]{:S(2)}) copy-start(bf16[6,48,512]{2,1,0:T(8,128)(2,1)} %copy-done.6) | copy-start | bytes 884740
  75.0 0.7 copy-start.8
  89.8 3.4 %copy-start.13 = (bf16[512,512]{1,0:T(8,128)(2,1)S(1)}, bf16[512,512]{1,0:T(8,128)(2,1)}, u32[]{:S(2)}) copy-start(bf16[512,512]{1,0:T(8,128)(2,1)} %convolution_convert_fusion.2) | copy-start | bytes 1572868
  93.2 2.6 %copy-start.10 = (bf16[288,1536]{1,0:T(8,128)(2,1)S(1)}, bf16[288,1536]{1,0:T(8,128)(2,1)}, u32[]{:S(2)}) copy-start(bf16[288,1536]{1,0:T(8,128)(2,1)} %reshape_reshape.31) | copy-start | bytes 2654212
  93.8 2.7 %copy-start.1 = (bf16[512,16,128]{2,0,1:T(8,128)(2,1)}, bf16[512,16,128]{2,0,1:T(8,128)(2,1)S(1)}, u32[]{:S(2)}) copy-start(bf16[512,16,128]{2,0,1:T(8,128)(2,1)S(1)} %copy_bitcast_fusion) | copy-start | bytes 6291460
  93.9 12.2 %copy-start.2 = (bf16[6,48,512]{2,1,0:T(8,128)(2,1)S(1)}, bf16[6,48,512]{2,1,0:T(8,128)(2,1)}, u32[]{:S(2)}) copy-start(bf16[6,48,512]{2,1,0:T(8,128)(2,1)} %param.5) | copy-start | bytes 884740
  93.9 12.2 %copy-start.15 = (f32[512]{0:T(512)S(1)}, f32[512]{0:T(512)}, u32[]{:S(2)}) copy-start(f32[512]{0:T(512)} %param.6) | copy-start | bytes 6148
  93.9 19.7 %collective-permute-start.8 = (bf16[4096,128]{1,0:T(8,128)(2,1)S(1)}, bf16[4096,128]{1,0:T(8,128)(2,1)}, u32[]{:S(2)}, u32[]{:S(2)}) collective-permute-start(bf16[4096,128]{1,0:T(8,128)(2,1)S(1)} %constant_dynamic-slice_fusion), channel_id=1, source_target_pairs={{0,1},{1,0},{2,3},{3,2},{4,5},{5,4},{6,7},{7,6},{8,9},{9,8},{10,11... | collective-permute-start | bytes 3145736 | tf_op jit(solution)/shard_map/ppermute | solution.py:79
  96.6 1.5 collective-permute-start.6
  98.1 8.0 %collective-permute-start.7 = (bf16[3,48,512]{2,1,0:T(8,128)(2,1)S(1)}, bf16[3,48,512]{2,1,0:T(8,128)(2,1)S(1)}, u32[]{:S(2)}, u32[]{:S(2)}) collective-permute-start(bf16[3,48,512]{2,1,0:T(8,128)(2,1)S(1)} %fusion.67), channel_id=1, source_target_pairs={{0,32},{32,64},{64,96},{96,128},{128,160},{160,192},{192,224},{224... | collective-permute-start | bytes 442376 | tf_op jit(solution)/shard_map/ppermute | solution.py:17
  107.2 6.4 %collective-permute-start.9 = (bf16[16,128]{1,0:T(8,128)(2,1)S(1)}, bf16[16,128]{1,0:T(8,128)(2,1)S(1)}, u32[]{:S(2)}, u32[]{:S(2)}) collective-permute-start(bf16[16,128]{1,0:T(8,128)(2,1)S(1)} %pad.5), channel_id=1, source_target_pairs={{0,1},{1,0},{2,3},{3,2},{4,5},{5,4},{6,7},{7,6},{8,9},{9,8},{10,11... | collective-permute-start | bytes 12296 | tf_op jit(solution)/shard_map/ppermute | solution.py:82
  137.1 37.4 %copy-start.4 = (bf16[512,512]{1,0:T(8,128)(2,1)S(1)}, bf16[512,512]{1,0:T(8,128)(2,1)}, u32[]{:S(2)}) copy-start(bf16[512,512]{1,0:T(8,128)(2,1)} %param.8) | copy-start | bytes 1572868
  137.2 37.3 %copy-start.9 = (bf16[288,512]{1,0:T(8,128)(2,1)S(1)}, bf16[288,512]{1,0:T(8,128)(2,1)}, u32[]{:S(2)}) copy-start(bf16[288,512]{1,0:T(8,128)(2,1)} %copy-done.8) | copy-start | bytes 884740
  137.2 3.2 %collective-permute-start.10 = (bf16[272,128]{1,0:T(8,128)(2,1)S(1)}, bf16[272,128]{1,0:T(8,128)(2,1)S(1)}, u32[]{:S(2)}, u32[]{:S(2)}) collective-permute-start(bf16[272,128]{1,0:T(8,128)(2,1)S(1)} %reduce_sum.82), channel_id=1, source_target_pairs={{0,2},{1,3},{2,0},{3,1},{4,6},{5,7},{6,4},{7,5},{8,10},{9,11},{10,... | collective-permute-start | bytes 208904 | tf_op jit(solution)/shard_map/ppermute | solution.py:90
  140.4 4.6 %collective-permute-start.11 = (bf16[272,128]{1,0:T(8,128)(2,1)S(1)}, bf16[272,128]{1,0:T(8,128)(2,1)S(1)}, u32[]{:S(2)}, u32[]{:S(2)}) collective-permute-start(bf16[272,128]{1,0:T(8,128)(2,1)S(1)} %add_convert_fusion.3), channel_id=1, source_target_pairs={{0,4},{1,5},{2,6},{3,7},{4,0},{5,1},{6,2},{7,3},{8,12},{9,13},{10,... | collective-permute-start | bytes 208904 | tf_op jit(solution)/shard_map/ppermute | solution.py:90
  145.1 7.2 %collective-permute-start.12 = (bf16[272,128]{1,0:T(8,128)(2,1)S(1)}, bf16[272,128]{1,0:T(8,128)(2,1)S(1)}, u32[]{:S(2)}, u32[]{:S(2)}) collective-permute-start(bf16[272,128]{1,0:T(8,128)(2,1)S(1)} %add_convert_fusion.2), channel_id=1, source_target_pairs={{0,8},{1,9},{2,10},{3,11},{4,12},{5,13},{6,14},{7,15},{8,0},{9,1},... | collective-permute-start | bytes 208904 | tf_op jit(solution)/shard_map/ppermute | solution.py:90
  167.8 18.9 %collective-permute-start.13 = (bf16[16,272,128]{2,1,0:T(8,128)(2,1)S(1)}, bf16[16,272,128]{2,1,0:T(8,128)(2,1)}, u32[]{:S(2)}, u32[]{:S(2)}) collective-permute-start(bf16[16,272,128]{2,1,0:T(8,128)(2,1)S(1)} %all_to_all.11), channel_id=1, source_target_pairs={{0,1},{1,0},{2,3},{3,2},{4,5},{5,4},{6,7},{7,6},{8,9},{9,8},{10,11... | collective-permute-start | bytes 3342344 | tf_op jit(solution)/shard_map/ppermute | solution.py:94
  174.8 2.0 collective-permute-start.2
  176.9 7.7 %collective-permute-start.3 = (bf16[3,48,512]{2,1,0:T(8,128)(2,1)S(1)}, bf16[3,48,512]{2,1,0:T(8,128)(2,1)S(1)}, u32[]{:S(2)}, u32[]{:S(2)}) collective-permute-start(bf16[3,48,512]{2,1,0:T(8,128)(2,1)S(1)} %fusion.69), channel_id=1, source_target_pairs={{0,32},{32,64},{64,96},{96,128},{128,160},{160,192},{192,224},{224... | collective-permute-start | bytes 442376 | tf_op jit(solution)/shard_map/ppermute | solution.py:17

commit v2 on v0

v2 whole, which is shorter than its diff:
```python
import functools

import jax
import jax.numpy as jnp
import numpy as np
from jax import lax
from jax.experimental import pallas as pl
from jax.experimental.pallas import tpu as pltpu
from jax.sharding import Mesh, PartitionSpec as P

ALL = ("x", "yh", "yl", "z", "c")
LAT = ("x", "yh")
LON = ("yl", "z", "c")
PLANE = ("x", "yh", "yl")
HEADS = 16
HS = 32
WL = 6
WW = 12
TILE = (6, 48)
D = 512
WINDOWS = 4
ROWS = 80
TOKENS = WINDOWS * ROWS
GROUP = 8
SPAN = GROUP * HS
EDGE = 16
HALF = 3 * TILE[1]
EDGES = 3 * EDGE
STRIP = 512 * 8
CHUNK = STRIP // 16
f32 = jnp.float32
bf16 = jnp.bfloat16
NT = (((1,), (1,)), ((), ()))
TN = (((0,), (0,)), ((), ()))


def gather_matrix():
    picks = np.zeros((TOKENS, 2 * HALF + 2 * EDGES), np.float32)
    for w in range(WINDOWS):
        for r in range(WL):
            for c in range(WW):
                col = w * WW + c + WW // 2
                below = r >= WL // 2
                line = r - WL // 2 if below else r
                if col < TILE[1]:
                    at = line * TILE[1] + col + (HALF if below else 0)
                else:
                    at = 2 * HALF + line * EDGE + col - TILE[1] + (EDGES if below else 0)
                picks[w * ROWS + r * WW + c, at] = 1.0
    return picks.astype(jnp.bfloat16)


def dot(a, b, dims=(((1,), (0,)), ((), ()))):
    return lax.dot_general(a, b, dims, preferred_element_type=f32)


def block_kernel(
    where_am_i,
    lat_ref, cot_ref, halo_lat_ref, halo_lon_ref, halo_cor_ref, gain_ref, w_qkv_ref, w_out_ref, picks_ref,
    own_ref, back_lat_ref, back_lon_ref, back_cor_ref, mine_ref, other_ref,
    scaled_s, normed_s, packed_s, dctx_s, ctx_s, dpacked_s, cot_s, latent_s,
):
    last_lat, core = where_am_i()
    picks = picks_ref[...]

    def gather(own, at):
        stack = jnp.concatenate(
            [own[HALF:, :], halo_lat_ref[at], halo_lon_ref[at], halo_cor_ref[at]], axis=0
        )
        return dot(picks, stack)

    latent = gather(lat_ref, 0)
    latent_s[...] = latent
    cot_s[...] = gather(cot_ref, 1).astype(bf16)
    centred = latent - jnp.mean(latent, axis=-1, keepdims=True)
    variance = jnp.mean(centred * centred, axis=-1, keepdims=True)
    recip_std = lax.rsqrt(variance + 1e-05)
    normed = centred * recip_std
    normed_s[...] = normed
    scaled_s[...] = (normed * gain_ref[...]).astype(bf16)
    packed_s[...] = dot(scaled_s[...], w_qkv_ref[...]).astype(bf16)
    dctx_s[...] = dot(cot_s[...], w_out_ref[...], NT).astype(bf16)

    scaling = HS ** (-0.5)
    key_at = lax.broadcasted_iota(jnp.int32, (ROWS, GROUP * ROWS), 0)
    lane = lax.broadcasted_iota(jnp.int32, (1, GROUP * ROWS), 1)
    query_at = lane
    for h in range(1, GROUP):
        query_at = query_at - jnp.where(lane >= h * ROWS, ROWS, 0)
    split = WL // 2 * WW
    differ = jnp.logical_and(last_lat, (key_at >= split) != (query_at >= split))
    excluded = jnp.logical_or(key_at >= WL * WW, differ)
    bias = jnp.where(excluded, -1e30, 0.0).astype(f32)
    head_of = lax.broadcasted_iota(jnp.int32, (GROUP, 1, SPAN), 2) // HS
    head = lax.broadcasted_iota(jnp.int32, (GROUP, 1, SPAN), 0)
    own_head = jnp.where(head_of == head, 1.0, 0.0).astype(f32)
    own_head_b = own_head.astype(bf16)

    def spread(rows):
        return (rows[None] * own_head_b).reshape(GROUP * ROWS, SPAN)

    def collect(rows):
        return jnp.sum(rows.reshape(GROUP, ROWS, SPAN) * own_head, axis=0).astype(bf16)

    for w in range(WINDOWS):
        for g in range(HEADS // GROUP):
            rows = slice(w * ROWS, (w + 1) * ROWS)
            at = [slice(b * D + g * SPAN, b * D + (g + 1) * SPAN) for b in range(3)]
            keys = packed_s[rows, at[1]]
            values = packed_s[rows, at[2]]
            queries = spread(packed_s[rows, at[0]])
            d_context = spread(dctx_s[rows, at[0]])
            scores = dot(keys, queries, NT) * (scaling * 1.4426950408889634) + bias
            expo = jnp.exp2(scores - jnp.max(scores, axis=0, keepdims=True))
            probs = expo * (1.0 / jnp.sum(expo, axis=0, keepdims=True))
            weights = probs.astype(bf16)
            d_weights = dot(values, d_context, NT)
            mean_d = jnp.sum(d_weights * probs, axis=0, keepdims=True)
            d_scaled = ((probs * scaling) * (d_weights - mean_d)).astype(bf16)
            ctx_s[rows, at[0]] = collect(dot(weights, values, TN))
            dpacked_s[rows, at[2]] = dot(weights, d_context).astype(bf16)
            dpacked_s[rows, at[0]] = collect(dot(d_scaled, keys, TN))
            dpacked_s[rows, at[1]] = dot(d_scaled, queries).astype(bf16)

    first = core == 0
    for strip in range(0, 8, 2):
        cols = slice(strip * 128, strip * 128 + 256)
        low = dot(scaled_s[...], dpacked_s[:, cols], TN)
        if strip < 4:
            high = dot(scaled_s[...], dpacked_s[:, 2 * D + strip * 128 : 2 * D + strip * 128 + 256], TN)
        else:
            high = dot(ctx_s[...], cot_s[:, strip * 128 - D : strip * 128 - D + 256], TN)
        keep = jnp.where(first, low, high).astype(bf16)
        give = jnp.where(first, high, low).astype(bf16)
        for k in range(2):
            to = slice((strip + k) * 512, (strip + k + 1) * 512)
            mine_ref[to, :] = keep[:, k * 128 : (k + 1) * 128]
            other_ref[to, :] = give[:, k * 128 : (k + 1) * 128]

    normed = normed_s[...]
    d_shifted = dot(dpacked_s[...], w_qkv_ref[...], NT).astype(bf16).astype(f32)
    grad_gain = jnp.sum(d_shifted * normed, axis=0, keepdims=True)
    gain_rows = jnp.concatenate(
        [grad_gain[:, k * 128 : (k + 1) * 128] for k in range(4)] + [jnp.zeros((12, 128), f32)], axis=0
    ).astype(bf16)
    mine_ref[STRIP:, :] = gain_rows
    other_ref[STRIP:, :] = gain_rows
    hidden = d_shifted * gain_ref[...]
    part = recip_std * (
        hidden
        - jnp.mean(hidden, axis=-1, keepdims=True)
        - normed * jnp.mean(hidden * normed, axis=-1, keepdims=True)
    )
    d_latent = (cot_s[...].astype(f32) + part).astype(bf16)
    attn = dot(ctx_s[...], w_out_ref[...]).astype(bf16).astype(f32)
    mixed = (latent_s[...] + attn).astype(bf16)
    for k, value in enumerate((mixed, d_latent)):
        moved = dot(picks, value, TN).astype(bf16)
        own_ref[k] = moved[:HALF]
        back_lat_ref[k] = moved[HALF : 2 * HALF]
        back_lon_ref[k] = moved[2 * HALF : 2 * HALF + EDGES]
        back_cor_ref[k] = moved[2 * HALF + EDGES :]


def here():
    return jnp.logical_and(lax.axis_index("x") == 3, lax.axis_index("yh") == 1), lax.axis_index("c")


def vmem_call(kernel, out_shapes, scratch, flops, moved, count):
    whole = pl.BlockSpec(memory_space=pltpu.VMEM)
    return pl.pallas_call(
        kernel,
        out_shape=out_shapes,
        in_specs=[whole] * count,
        out_specs=[whole] * len(out_shapes),
        scratch_shapes=scratch,
        compiler_params=pltpu.CompilerParams(vmem_limit_bytes=40 * 1024 * 1024),
        cost_estimate=pl.CostEstimate(flops=flops, bytes_accessed=moved, transcendentals=0),
    )


def shape(*dims, dtype=bf16):
    return jax.ShapeDtypeStruct(dims, dtype)


def block(where_am_i, latent, cot, halo_lat, halo_lon, halo_cor, gain, w_qkv, w_out):
    return vmem_call(
        functools.partial(block_kernel, where_am_i),
        [
            shape(2, HALF, D), shape(2, HALF, D), shape(2, EDGES, D), shape(2, EDGES, D),
            shape(STRIP + 16, 128), shape(STRIP + 16, 128),
        ],
        [
            pltpu.VMEM((TOKENS, D), bf16), pltpu.VMEM((TOKENS, D), f32), pltpu.VMEM((TOKENS, 3 * D), bf16),
            pltpu.VMEM((TOKENS, D), bf16), pltpu.VMEM((TOKENS, D), bf16), pltpu.VMEM((TOKENS, 3 * D), bf16),
            pltpu.VMEM((TOKENS, D), bf16), pltpu.VMEM((TOKENS, D), f32),
        ],
        6_000_000_000, 8_000_000, 9,
    )(latent, cot, halo_lat, halo_lon, halo_cor, gain, w_qkv, w_out, jnp.asarray(gather_matrix()))


def add_kernel(mine_ref, arrived_ref, chunks_ref):
    gain = (mine_ref[STRIP:, :].astype(f32) + arrived_ref[STRIP:, :].astype(f32)).astype(bf16)
    for k in range(16):
        at = slice(k * CHUNK, (k + 1) * CHUNK)
        chunks_ref[k, :CHUNK] = (mine_ref[at, :].astype(f32) + arrived_ref[at, :].astype(f32)).astype(bf16)
        chunks_ref[k, CHUNK:] = gain


def unpack_kernel(where_am_i, half_ref, arrived_ref, qkv_ref, out_ref, gain_ref):
    first = where_am_i()[1] == 0
    for k in range(16):
        ours = half_ref[k, :CHUNK].astype(f32)
        theirs = arrived_ref[k, :CHUNK].astype(f32)
        low = jnp.where(first, ours, theirs)
        high = jnp.where(first, theirs, ours)
        strip, rows = k // 2, slice(k % 2 * CHUNK, (k % 2 + 1) * CHUNK)
        qkv_ref[rows, strip * 128 : (strip + 1) * 128] = low
        if strip < 4:
            qkv_ref[rows, 2 * D + strip * 128 : 2 * D + (strip + 1) * 128] = high
        else:
            out_ref[rows, strip * 128 - D : (strip + 1) * 128 - D] = high
    gain = jnp.where(first, half_ref[0, CHUNK:].astype(f32), arrived_ref[0, CHUNK:].astype(f32))
    for k in range(4):
        gain_ref[:, k * 128 : (k + 1) * 128] = gain[k : k + 1, :]


def place_kernel(own_ref, lat_ref, lon_ref, cor_ref, mixed_ref, d_latent_ref):
    for k, out_ref in enumerate((mixed_ref, d_latent_ref)):
        for r in range(3):
            for first, body_ref, edge_ref in ((0, lat_ref, cor_ref), (HALF, own_ref, lon_ref)):
                at = r * TILE[1]
                edge = edge_ref[k, r * EDGE : (r + 1) * EDGE].astype(f32)
                body = body_ref[k, at : at + EDGE].astype(f32)
                out_ref[first + at : first + at + EDGE, :] = (body + edge).astype(bf16)
                out_ref[first + at + EDGE : first + at + TILE[1], :] = body_ref[k, at + EDGE : at + TILE[1]]


def shifted(lat_by, lon_by):
    pairs = []
    for i in range(256):
        lat, lon = i // 32, i % 32
        pairs.append((i, (lat + lat_by) % 8 * 32 + (lon + lon_by) % 32))
    return pairs


def swapped(bits):
    return [(i, i ^ bits) for i in range(256)]


def send(value, pairs):
    return lax.ppermute(value, ALL, pairs)


def sum_grads(mine, other):
    arrived = send(other, swapped(1))
    chunks = vmem_call(add_kernel, [shape(16, CHUNK + 16, 128)], [], 1_000_000, 4_000_000, 2)(mine, arrived)[0]
    pieces = lax.all_to_all(chunks, PLANE, 0, 0, tiled=True)
    total = jnp.sum(pieces.astype(f32), axis=0).astype(bf16)
    for bit in (2, 4, 8):
        total = (total.astype(f32) + send(total, swapped(bit)).astype(f32)).astype(bf16)
    spread = jnp.broadcast_to(total, (16, CHUNK + 16, 128))
    half = lax.all_to_all(spread, PLANE, 0, 0, tiled=True)
    arrived = send(half, swapped(1))
    grad_qkv, grad_out, grad_gain = vmem_call(
        functools.partial(unpack_kernel, here),
        [shape(D, 3 * D, dtype=f32), shape(D, D, dtype=f32), shape(1, D, dtype=f32)],
        [], 1_000_000, 6_000_000, 2,
    )(half, arrived)
    return grad_qkv, grad_out, grad_gain.reshape(D)


def local(latent, norm_gain, w_qkv, w_out, cotangent):
    both = jnp.stack([latent[:3], cotangent[:3]])
    halo_lat = send(both.reshape(2, HALF, D), shifted(-1, 0))
    halo_cor = send(both[:, :, :EDGE].reshape(2, EDGES, D), shifted(-1, -1))
    edge = jnp.stack([latent[3:, :EDGE], cotangent[3:, :EDGE]])
    halo_lon = send(edge.reshape(2, EDGES, D), shifted(0, -1))
    own, back_lat, back_lon, back_cor, mine, other = block(
        here, latent.reshape(-1, D), cotangent.reshape(-1, D), halo_lat, halo_lon, halo_cor,
        norm_gain.reshape(1, D), w_qkv, w_out,
    )
    grad_qkv, grad_out, grad_gain = sum_grads(mine, other)
    came_lat = send(back_lat, shifted(1, 0))
    came_lon = send(back_lon, shifted(0, 1))
    came_cor = send(back_cor, shifted(1, 1))
    mixed, d_latent = vmem_call(
        place_kernel, [shape(2 * HALF, D), shape(2 * HALF, D)], [], 1_000_000, 2_000_000, 4
    )(own, came_lat, came_lon, came_cor)
    return mixed.reshape(*TILE, D), d_latent.reshape(*TILE, D), grad_qkv, grad_out, grad_gain


def solution(mesh):
    fine = Mesh(mesh.devices.reshape(4, 2, 2, 8, 2), ALL)
    in_specs = (P(LAT, LON, None), P(), P(), P(), P(LAT, LON, None))
    out_specs = (P(LAT, LON, None), P(LAT, LON, None), P(), P(), P())
    return jax.shard_map(local, mesh=fine, in_specs=in_specs, out_specs=out_specs, check_vma=False)
```

time: 380 us -> 112 us (0.29)
  waiting for transfers between devices: 181 us -> 21.4 us
  local copies, waits for them, and re-layouts: 48.5 us -> 3.32 us
  blocking collectives: 79.4 us -> 37.2 us
  matrix products: 31.5 us -> 0 us
  starting transfers between devices: 16.1 us -> 37.7 us
  between operations: 14.4 us -> 0.75 us
  Pallas kernels: 0 us -> 11.4 us
  other arithmetic: 7.31 us -> 0.27 us
    psum x1 -> x0, waiting for transfers between devices: 172 us -> none  [sum_grads(): lax.psum((grad_items[0], grad_items[1], grad_items[2]), ('lat', 'lon'))]
    psum x1 -> x0, blocking collectives: 79.4 us -> none  [sum_grads(): lax.psum((grad_items[0], grad_items[1], grad_items[2]), ('lat', 'lon'))]
    all_to_all x0 -> x2, blocking collectives: none -> 37.2 us  [the longest x1 22 us: sum_grads(): pieces = lax.all_to_all(chunks, PLANE, 0, 0, tiled=True)]
    dot_general x11 -> x0, matrix products: 29 us -> none  [the longest x1 5.53 us: attend(): jnp.einsum('bhqk,bkhd->bqhd', d_scaled, key_rows, preferred_element_type=...]
    ppermute x8 -> x11, starting transfers between devices: 16.1 us -> 37.7 us  [send(): return lax.ppermute(value, ALL, pairs)]
    another operation x10 -> x1, local copies, waits for them, and re-layouts: 21 us -> 1.17 us  [local(): both = jnp.stack([latent[:3], cotangent[:3]])]
    unnamed x37 -> x12, local copies, waits for them, and re-layouts: 14.8 us -> 2 us
    ppermute x8 -> x11, waiting for transfers between devices: 9.7 us -> 21.4 us  [send(): return lax.ppermute(value, ALL, pairs)]
  transfers between devices with their start and end apart: 9 -> 11, of which waited for: 5 -> 6; matrix products, arithmetic and copies ran while one was open for 3% -> 0% of each run, Pallas kernels for 0% -> 1%
where the time goes in v2:
time: 112 us
  starting transfers between devices  37.7 us (34%)
  blocking collectives  37.2 us (33%)
  waiting for transfers between devices  21.4 us (19%)
  Pallas kernels  11.4 us (10%)
  local copies, waits for them, and re-layouts  3.32 us (3%)
    ppermute x11, starting transfers between devices, send(): return lax.ppermute(value, ALL, pairs)  37.7 us
    all_to_all x1, blocking collectives, sum_grads(): pieces = lax.all_to_all(chunks, PLANE, 0, 0, tiled=True)  22 us
    ppermute x11, waiting for transfers between devices, send(): return lax.ppermute(value, ALL, pairs)  21.4 us
    all_to_all x1, blocking collectives, sum_grads(): half = lax.all_to_all(spread, PLANE, 0, 0, tiled=True)  15.2 us
    pallas_call x1, Pallas kernels, block(): vmem_call(functools.partial(block_kernel, where_am_i), [shape(2, HALF, D)...  7.95 us
    pallas_call x1, Pallas kernels, sum_grads(): vmem_call(functools.partial(unpack_kernel, here), [shape(D, 3 * D, dtype=...  2.33 us
  transfers between devices with their start and end apart: 11, of which 6 were waited for; matrix products, arithmetic and copies ran while one was open for 0% of the time, Pallas kernels for 1%

profile of v2, /device:TPU:1, one launch (start us, length us, event | category | flops | bytes accessed | tf_op | source)
XLA Modules:
  0.0 112.0 jit_solution(9545178229910677738)
XLA Ops:
  0.6 0.0 copy-start.1
  0.6 0.0 copy-start
  0.7 0.0 copy-start.2
  0.7 0.0 copy-start.4
  0.7 1.2 %slice_bitcast_fusion = (bf16[1,3,48,512]{3,2,1,0:T(8,128)(2,1)S(1)}, bf16[3,48,512]{2,1,0:T(8,128)(2,1)S(1)}, bf16[3,48,512]{2,1,0:T(8,128)(2,1)S(1)}, bf16[1,3,48,512]{3,2,1,0:T(8,128)(2,1)S(1)}) fusion(bf16[6,48,512]{2,1,0:T(8,128)(2,1)} %param.10, bf16[6,48,512]{2,1,0:T(8,128)(2,1)} %param.6), kind=kLoop, calls=%fused_computation.6 | loop fusion | bytes 884736 | tf_op jit(solution)/shard_map/stack | solution.py:274
  1.9 6.0 %collective-permute-start = (bf16[2,144,512]{2,1,0:T(8,128)(2,1)S(1)}, bf16[2,144,512]{2,1,0:T(8,128)(2,1)S(1)}, u32[]{:S(2)}, u32[]{:S(2)}) collective-permute-start(bf16[2,144,512]{2,1,0:T(8,128)(2,1)S(1)} %pad_maximum_fusion), channel_id=1, source_target_pairs={{0,224},{1,225},{2,226},{3,227},{4,228},{5,229},{6,230},{7,231},{8... | collective-permute-start | bytes 884744 | tf_op jit(solution)/shard_map/ppermute | solution.py:252
  7.9 0.0 copy-done
  7.9 0.0 copy-done.1
  7.9 1.0 collective-permute-start.1
  9.0 6.6 %collective-permute-start.2 = (bf16[2,48,512]{2,1,0:T(8,128)(2,1)S(1)}, bf16[2,48,512]{2,1,0:T(8,128)(2,1)S(1)}, u32[]{:S(2)}, u32[]{:S(2)}) collective-permute-start(bf16[2,48,512]{2,1,0:T(8,128)(2,1)S(1)} %bitcast.22), channel_id=1, source_target_pairs={{0,255},{1,224},{2,225},{3,226},{4,227},{5,228},{6,229},{7,230},{8... | collective-permute-start | bytes 294920 | tf_op jit(solution)/shard_map/ppermute | solution.py:252
  15.6 0.0 collective-permute-done.1.halo_lon_ref
  15.6 1.6 %collective-permute-done.2.halo_cor_ref = bf16[2,48,512]{2,1,0:T(8,128)(2,1)S(1)} collective-permute-done((bf16[2,48,512]{2,1,0:T(8,128)(2,1)S(1)}, bf16[2,48,512]{2,1,0:T(8,128)(2,1)S(1)}, u32[]{:S(2)}, u32[]{:S(2)}) %collective-permute-start.2) | collective-permute-done | bytes 98336 | tf_op jit(solution)/shard_map/ppermute | solution.py:252
  17.3 0.0 collective-permute-done.halo_lat_ref
  17.3 0.0 copy-done.2
  17.3 0.0 copy-done.4
  17.3 0.0 copy-start.3
  17.3 1.0 copy-done.3
  18.3 0.0 copy-start.5
  18.3 0.9 copy-done.5
  19.3 8.0 %shard_map.101 = (bf16[2,144,512]{2,1,0:T(8,128)(2,1)S(1)}, bf16[2,144,512]{2,1,0:T(8,128)(2,1)S(1)}, bf16[2,48,512]{2,1,0:T(8,128)(2,1)S(1)}, bf16[2,48,512]{2,...) custom-call(bf16[288,512]{1,0:T(8,128)(2,1)S(1)} %bitcast.15, ...), custom_call_target="tpu_custom_call" | custom-call | flops 6000000000 | bytes 8000000 | tf_op jit(solution)/shard_map/pallas_call | solution.py:187
  27.2 2.6 %collective-permute-start.6 = (bf16[4112,128]{1,0:T(8,128)(2,1)S(1)}, bf16[4112,128]{1,0:T(8,128)(2,1)S(1)}, u32[]{:S(2)}, u32[]{:S(2)}) collective-permute-start(bf16[4112,128]{1,0:T(8,128)(2,1)S(1)} %get-tuple-element.23), channel_id=1, source_target_pairs={{0,1},{1,0},{2,3},{3,2},{4,5},{5,4},{6,7},{7,6},{8,9},{9,8},{10,11... | collective-permute-start | bytes 3158024 | tf_op jit(solution)/shard_map/ppermute | solution.py:252
  29.8 2.3 %collective-permute-done.6.arrived_ref = bf16[4112,128]{1,0:T(8,128)(2,1)S(1)} collective-permute-done((bf16[4112,128]{1,0:T(8,128)(2,1)S(1)}, bf16[4112,128]{1,0:T(8,128)(2,1)S(1)}, u32[]{:S(2)}, u32[]{:S(2)}) %collective-permute-start.6) | collective-permute-done | bytes 1052704 | tf_op jit(solution)/shard_map/ppermute | solution.py:252
  32.1 0.2 shard_map.103
  32.3 22.0 %all_to_all.10 = bf16[16,272,128]{2,1,0:T(8,128)(2,1)S(1)} all-to-all(bf16[16,272,128]{2,1,0:T(8,128)(2,1)S(1)} %shard_map.103), channel_id=1, replica_groups=mesh['x'=4,'yh'=2,'yl'=2,'z'=8,'c'=2] {'x','yh','yl'}, dimensions={0} | all-to-all | bytes 2228224 | tf_op jit(solution)/shard_map/all_to_all | solution.py:258
  54.3 0.2 reduce_sum.12
  54.4 1.4 %collective-permute-start.7 = (bf16[272,128]{1,0:T(8,128)(2,1)S(1)}, bf16[272,128]{1,0:T(8,128)(2,1)S(1)}, u32[]{:S(2)}, u32[]{:S(2)}) collective-permute-start(bf16[272,128]{1,0:T(8,128)(2,1)S(1)} %reduce_sum.12), channel_id=1, source_target_pairs={{0,2},{1,3},{2,0},{3,1},{4,6},{5,7},{6,4},{7,5},{8,10},{9,11},{10,... | collective-permute-start | bytes 208904 | tf_op jit(solution)/shard_map/ppermute | solution.py:252
  55.8 1.9 %collective-permute-done.7 = bf16[272,128]{1,0:T(8,128)(2,1)S(1)} collective-permute-done((bf16[272,128]{1,0:T(8,128)(2,1)S(1)}, bf16[272,128]{1,0:T(8,128)(2,1)S(1)}, u32[]{:S(2)}, u32[]{:S(2)}) %collective-permute-start.7) | collective-permute-done | bytes 69664 | tf_op jit(solution)/shard_map/ppermute | solution.py:252
  57.7 2.9 %collective-permute-start.8 = (bf16[272,128]{1,0:T(8,128)(2,1)S(1)}, bf16[272,128]{1,0:T(8,128)(2,1)S(1)}, u32[]{:S(2)}, u32[]{:S(2)}) collective-permute-start(bf16[272,128]{1,0:T(8,128)(2,1)S(1)} %add_convert_fusion.2), channel_id=1, source_target_pairs={{0,4},{1,5},{2,6},{3,7},{4,0},{5,1},{6,2},{7,3},{8,12},{9,13},{10,... | collective-permute-start | bytes 208904 | tf_op jit(solution)/shard_map/ppermute | solution.py:252
  60.6 1.7 %collective-permute-done.8 = bf16[272,128]{1,0:T(8,128)(2,1)S(1)} collective-permute-done((bf16[272,128]{1,0:T(8,128)(2,1)S(1)}, bf16[272,128]{1,0:T(8,128)(2,1)S(1)}, u32[]{:S(2)}, u32[]{:S(2)}) %collective-permute-start.8) | collective-permute-done | bytes 69664 | tf_op jit(solution)/shard_map/ppermute | solution.py:252
  62.3 7.1 %collective-permute-start.9 = (bf16[272,128]{1,0:T(8,128)(2,1)S(1)}, bf16[272,128]{1,0:T(8,128)(2,1)S(1)}, u32[]{:S(2)}, u32[]{:S(2)}) collective-permute-start(bf16[272,128]{1,0:T(8,128)(2,1)S(1)} %add_convert_fusion.1), channel_id=1, source_target_pairs={{0,8},{1,9},{2,10},{3,11},{4,12},{5,13},{6,14},{7,15},{8,0},{9,1},... | collective-permute-start | bytes 208904 | tf_op jit(solution)/shard_map/ppermute | solution.py:252
  69.4 2.0 %collective-permute-done.9 = bf16[272,128]{1,0:T(8,128)(2,1)S(1)} collective-permute-done((bf16[272,128]{1,0:T(8,128)(2,1)S(1)}, bf16[272,128]{1,0:T(8,128)(2,1)S(1)}, u32[]{:S(2)}, u32[]{:S(2)}) %collective-permute-start.9) | collective-permute-done | bytes 69664 | tf_op jit(solution)/shard_map/ppermute | solution.py:252
  71.4 0.1 broadcast_in_dim.3
  71.6 15.2 %all_to_all.11.half_ref = bf16[16,272,128]{2,1,0:T(8,128)(2,1)S(1)} all-to-all(bf16[16,272,128]{2,1,0:T(8,128)(2,1)S(1)} %broadcast_in_dim.3), channel_id=1, replica_groups=mesh['x'=4,'yh'=2,'yl'=2,'z'=8,'c'=2] {'x','yh','yl'}, dimensions={0} | all-to-all | bytes 2228224 | tf_op jit(solution)/shard_map/all_to_all | solution.py:263
  86.8 6.5 %collective-permute-start.10 = (bf16[16,272,128]{2,1,0:T(8,128)(2,1)S(1)}, bf16[16,272,128]{2,1,0:T(8,128)(2,1)S(1)}, u32[]{:S(2)}, u32[]{:S(2)}) collective-permute-start(bf16[16,272,128]{2,1,0:T(8,128)(2,1)S(1)} %all_to_all.11.half_ref), channel_id=1, source_target_pairs={{0,1},{1,0},{2,3},{3,2},{4,5},{5,4},{6,7},{7,6},{8,9},{9,8},{10,11... | collective-permute-start | bytes 3342344 | tf_op jit(solution)/shard_map/ppermute | solution.py:252
  93.3 1.1 collective-permute-start.3
  94.4 0.7 collective-permute-start.4
  95.1 1.8 %collective-permute-start.5 = (bf16[2,48,512]{2,1,0:T(8,128)(2,1)S(1)}, bf16[2,48,512]{2,1,0:T(8,128)(2,1)S(1)}, u32[]{:S(2)}, u32[]{:S(2)}) collective-permute-start(bf16[2,48,512]{2,1,0:T(8,128)(2,1)S(1)} %get-tuple-element.19), channel_id=1, source_target_pairs={{0,33},{1,34},{2,35},{3,36},{4,37},{5,38},{6,39},{7,40},{8,41},{9,... | collective-permute-start | bytes 294920 | tf_op jit(solution)/shard_map/ppermute | solution.py:252
  96.9 0.0 collective-permute-done.4.lon_ref
  96.9 11.9 %collective-permute-done.5.cor_ref = bf16[2,48,512]{2,1,0:T(8,128)(2,1)S(1)} collective-permute-done((bf16[2,48,512]{2,1,0:T(8,128)(2,1)S(1)}, bf16[2,48,512]{2,1,0:T(8,128)(2,1)S(1)}, u32[]{:S(2)}, u32[]{:S(2)}) %collective-permute-start.5) | collective-permute-done | bytes 98336 | tf_op jit(solution)/shard_map/ppermute | solution.py:252
  108.8 0.0 collective-permute-done.3.lat_ref
  108.8 0.9 shard_map.102
  109.7 0.0 collective-permute-done.10.arrived_ref
  109.7 2.3 %shard_map.104 = (f32[512,1536]{1,0:T(8,128)}, f32[512,512]{1,0:T(8,128)}, f32[1,512]{1,0:T(1,128)}) custom-call(bf16[16,272,128]{2,1,0:T(8,128)(2,1)S(1)} %all_to_all.11.half_ref, bf16[16,272,128]{2,1,0:T(8,128)(2,1)S(1)} %collective-permute-done.10.arrived_ref), custom_call_target="tpu_custom_call" | custom-call | flops 1000000 | bytes 6000000 | tf_op jit(solution)/shard_map/pallas_call | solution.py:265
  (8 shorter events, 0.1 us)
Async XLA Ops:
  0.6 7.3 %copy-start.1 = (bf16[6,48,512]{2,1,0:T(8,128)(2,1)S(1)}, bf16[6,48,512]{2,1,0:T(8,128)(2,1)}, u32[]{:S(2)}) copy-start(bf16[6,48,512]{2,1,0:T(8,128)(2,1)} %param.10) | copy-start | bytes 884740
  0.6 7.3 %copy-start = (bf16[6,48,512]{2,1,0:T(8,128)(2,1)S(1)}, bf16[6,48,512]{2,1,0:T(8,128)(2,1)}, u32[]{:S(2)}) copy-start(bf16[6,48,512]{2,1,0:T(8,128)(2,1)} %param.6) | copy-start | bytes 884740
  0.7 16.6 %copy-start.2 = (bf16[512,1536]{1,0:T(8,128)(2,1)S(1)}, bf16[512,1536]{1,0:T(8,128)(2,1)}, u32[]{:S(2)}) copy-start(bf16[512,1536]{1,0:T(8,128)(2,1)} %w_qkv_ref.1) | copy-start | bytes 4718596
  0.7 16.6 %copy-start.4 = (f32[512]{0:T(512)S(1)}, f32[512]{0:T(512)}, u32[]{:S(2)}) copy-start(f32[512]{0:T(512)} %param.7) | copy-start | bytes 6148
  1.9 15.4 %collective-permute-start = (bf16[2,144,512]{2,1,0:T(8,128)(2,1)S(1)}, bf16[2,144,512]{2,1,0:T(8,128)(2,1)S(1)}, u32[]{:S(2)}, u32[]{:S(2)}) collective-permute-start(bf16[2,144,512]{2,1,0:T(8,128)(2,1)S(1)} %pad_maximum_fusion), channel_id=1, source_target_pairs={{0,224},{1,225},{2,226},{3,227},{4,228},{5,229},{6,230},{7,231},{8... | collective-permute-start | bytes 884744 | tf_op jit(solution)/shard_map/ppermute | solution.py:252
  7.9 7.7 %collective-permute-start.1 = (bf16[2,48,512]{2,1,0:T(8,128)(2,1)S(1)}, bf16[2,48,512]{2,1,0:T(8,128)(2,1)S(1)}, u32[]{:S(2)}, u32[]{:S(2)}) collective-permute-start(bf16[2,48,512]{2,1,0:T(8,128)(2,1)S(1)} %pad_maximum_fusion.2), channel_id=1, source_target_pairs={{0,31},{1,0},{2,1},{3,2},{4,3},{5,4},{6,5},{7,6},{8,7},{9,8},{10,9... | collective-permute-start | bytes 294920 | tf_op jit(solution)/shard_map/ppermute | solution.py:252
  9.0 8.3 %collective-permute-start.2 = (bf16[2,48,512]{2,1,0:T(8,128)(2,1)S(1)}, bf16[2,48,512]{2,1,0:T(8,128)(2,1)S(1)}, u32[]{:S(2)}, u32[]{:S(2)}) collective-permute-start(bf16[2,48,512]{2,1,0:T(8,128)(2,1)S(1)} %bitcast.22), channel_id=1, source_target_pairs={{0,255},{1,224},{2,225},{3,226},{4,227},{5,228},{6,229},{7,230},{8... | collective-permute-start | bytes 294920 | tf_op jit(solution)/shard_map/ppermute | solution.py:252
  17.3 1.0 copy-start.3
  18.3 0.9 copy-start.5
  27.2 4.8 %collective-permute-start.6 = (bf16[4112,128]{1,0:T(8,128)(2,1)S(1)}, bf16[4112,128]{1,0:T(8,128)(2,1)S(1)}, u32[]{:S(2)}, u32[]{:S(2)}) collective-permute-start(bf16[4112,128]{1,0:T(8,128)(2,1)S(1)} %get-tuple-element.23), channel_id=1, source_target_pairs={{0,1},{1,0},{2,3},{3,2},{4,5},{5,4},{6,7},{7,6},{8,9},{9,8},{10,11... | collective-permute-start | bytes 3158024 | tf_op jit(solution)/shard_map/ppermute | solution.py:252
  54.4 3.2 %collective-permute-start.7 = (bf16[272,128]{1,0:T(8,128)(2,1)S(1)}, bf16[272,128]{1,0:T(8,128)(2,1)S(1)}, u32[]{:S(2)}, u32[]{:S(2)}) collective-permute-start(bf16[272,128]{1,0:T(8,128)(2,1)S(1)} %reduce_sum.12), channel_id=1, source_target_pairs={{0,2},{1,3},{2,0},{3,1},{4,6},{5,7},{6,4},{7,5},{8,10},{9,11},{10,... | collective-permute-start | bytes 208904 | tf_op jit(solution)/shard_map/ppermute | solution.py:252
  57.7 4.6 %collective-permute-start.8 = (bf16[272,128]{1,0:T(8,128)(2,1)S(1)}, bf16[272,128]{1,0:T(8,128)(2,1)S(1)}, u32[]{:S(2)}, u32[]{:S(2)}) collective-permute-start(bf16[272,128]{1,0:T(8,128)(2,1)S(1)} %add_convert_fusion.2), channel_id=1, source_target_pairs={{0,4},{1,5},{2,6},{3,7},{4,0},{5,1},{6,2},{7,3},{8,12},{9,13},{10,... | collective-permute-start | bytes 208904 | tf_op jit(solution)/shard_map/ppermute | solution.py:252
  62.3 9.1 %collective-permute-start.9 = (bf16[272,128]{1,0:T(8,128)(2,1)S(1)}, bf16[272,128]{1,0:T(8,128)(2,1)S(1)}, u32[]{:S(2)}, u32[]{:S(2)}) collective-permute-start(bf16[272,128]{1,0:T(8,128)(2,1)S(1)} %add_convert_fusion.1), channel_id=1, source_target_pairs={{0,8},{1,9},{2,10},{3,11},{4,12},{5,13},{6,14},{7,15},{8,0},{9,1},... | collective-permute-start | bytes 208904 | tf_op jit(solution)/shard_map/ppermute | solution.py:252
  86.8 22.9 %collective-permute-start.10 = (bf16[16,272,128]{2,1,0:T(8,128)(2,1)S(1)}, bf16[16,272,128]{2,1,0:T(8,128)(2,1)S(1)}, u32[]{:S(2)}, u32[]{:S(2)}) collective-permute-start(bf16[16,272,128]{2,1,0:T(8,128)(2,1)S(1)} %all_to_all.11.half_ref), channel_id=1, source_target_pairs={{0,1},{1,0},{2,3},{3,2},{4,5},{5,4},{6,7},{7,6},{8,9},{9,8},{10,11... | collective-permute-start | bytes 3342344 | tf_op jit(solution)/shard_map/ppermute | solution.py:252
  93.3 15.5 %collective-permute-start.3 = (bf16[2,144,512]{2,1,0:T(8,128)(2,1)S(1)}, bf16[2,144,512]{2,1,0:T(8,128)(2,1)S(1)}, u32[]{:S(2)}, u32[]{:S(2)}) collective-permute-start(bf16[2,144,512]{2,1,0:T(8,128)(2,1)S(1)} %get-tuple-element.17), channel_id=1, source_target_pairs={{0,32},{1,33},{2,34},{3,35},{4,36},{5,37},{6,38},{7,39},{8,40},{9,... | collective-permute-start | bytes 884744 | tf_op jit(solution)/shard_map/ppermute | solution.py:252
  94.4 2.5 %collective-permute-start.4 = (bf16[2,48,512]{2,1,0:T(8,128)(2,1)S(1)}, bf16[2,48,512]{2,1,0:T(8,128)(2,1)S(1)}, u32[]{:S(2)}, u32[]{:S(2)}) collective-permute-start(bf16[2,48,512]{2,1,0:T(8,128)(2,1)S(1)} %get-tuple-element.18), channel_id=1, source_target_pairs={{0,1},{1,2},{2,3},{3,4},{4,5},{5,6},{6,7},{7,8},{8,9},{9,10},{10,1... | collective-permute-start | bytes 294920 | tf_op jit(solution)/shard_map/ppermute | solution.py:252
  95.1 13.7 %collective-permute-start.5 = (bf16[2,48,512]{2,1,0:T(8,128)(2,1)S(1)}, bf16[2,48,512]{2,1,0:T(8,128)(2,1)S(1)}, u32[]{:S(2)}, u32[]{:S(2)}) collective-permute-start(bf16[2,48,512]{2,1,0:T(8,128)(2,1)S(1)} %get-tuple-element.19), channel_id=1, source_target_pairs={{0,33},{1,34},{2,35},{3,36},{4,37},{5,38},{6,39},{7,40},{8,41},{9,... | collective-permute-start | bytes 294920 | tf_op jit(solution)/shard_map/ppermute | solution.py:252

commit v3 on v2

v3 whole, which is shorter than its diff:
```python
import functools

import jax
import jax.numpy as jnp
from jax import lax
from jax.experimental import pallas as pl
from jax.experimental.pallas import tpu as pltpu
from jax.sharding import Mesh, PartitionSpec as P

ALL = ("x", "yh", "yl", "z", "c")
LAT = ("x", "yh")
LON = ("yl", "z", "c")
PLANE = ("x", "yh", "yl")
HEADS = 16
HS = 32
WL = 6
WW = 12
TILE = (6, 48)
D = 512
WINDOWS = 4
ROWS = 80
TOKENS = WINDOWS * ROWS
GROUP = 8
SPAN = GROUP * HS
EDGE = 16
HALF = 3 * TILE[1]
EDGES = 3 * EDGE
STRIP = 512 * 8
CHUNK = STRIP // 16
SUMMED = CHUNK + 16
BACK = HALF + EDGES
f32 = jnp.float32
bf16 = jnp.bfloat16
NT = (((1,), (1,)), ((), ()))
TN = (((0,), (0,)), ((), ()))


def dot(a, b, dims=(((1,), (0,)), ((), ()))):
    return lax.dot_general(a, b, dims, preferred_element_type=f32)


def norm(latent):
    centred = latent - jnp.mean(latent, axis=-1, keepdims=True)
    variance = jnp.mean(centred * centred, axis=-1, keepdims=True)
    recip_std = lax.rsqrt(variance + 1e-05)
    return centred * recip_std, recip_std


def picks_kernel(w_out_ref, picks_ref, w_out_s):
    w_out_s[...] = w_out_ref[...]
    def count(value, step, upto):
        return sum(jnp.where(value >= step * k, 1, 0) for k in range(1, upto))

    row = lax.broadcasted_iota(jnp.int32, (TOKENS, 128), 0)
    window = count(row, ROWS, WINDOWS)
    cell = row - window * ROWS
    line = count(cell, WW, WL)
    col = (window + 0) * WW + cell - line * WW + WW // 2
    below = line >= WL // 2
    line = jnp.where(below, line - WL // 2, line)
    inside = line * TILE[1] + col + jnp.where(below, HALF, 0)
    beyond = 2 * HALF + line * EDGE + col - TILE[1] + jnp.where(below, EDGES, 0)
    at = jnp.where(col < TILE[1], inside, beyond)
    at = jnp.where(cell < WL * WW, at, -1)
    lane = lax.broadcasted_iota(jnp.int32, (TOKENS, 128), 1)
    for k in range(3):
        picks_ref[:, k * 128 : (k + 1) * 128] = jnp.where(at == lane + k * 128, 1.0, 0.0).astype(bf16)


def attend_kernel(
    where_am_i,
    lat_ref, cot_ref, halo_lat_ref, halo_lon_ref, halo_cor_ref, gain_ref, w_qkv_ref, w_out_ref, picks_ref,
    mine_ref, other_ref, latent_s, cot_s, ctx_s, dpacked_s,
    scaled_s, packed_s, dctx_s,
):
    last_lat, core = where_am_i()
    picks = picks_ref[...]

    def gather(own, at):
        stack = jnp.concatenate(
            [own[HALF:, :], halo_lat_ref[at], halo_lon_ref[at], halo_cor_ref[at]], axis=0
        )
        return dot(picks, stack)

    latent = gather(lat_ref, 0)
    latent_s[...] = latent.astype(bf16)
    cot_s[...] = gather(cot_ref, 1).astype(bf16)
    normed, _ = norm(latent)
    scaled_s[...] = (normed * gain_ref[...]).astype(bf16)
    packed_s[...] = dot(scaled_s[...], w_qkv_ref[...]).astype(bf16)
    dctx_s[...] = dot(cot_s[...], w_out_ref[...], NT).astype(bf16)

    scaling = HS ** (-0.5)
    key_at = lax.broadcasted_iota(jnp.int32, (ROWS, GROUP * ROWS), 0)
    lane = lax.broadcasted_iota(jnp.int32, (1, GROUP * ROWS), 1)
    query_at = lane
    for h in range(1, GROUP):
        query_at = query_at - jnp.where(lane >= h * ROWS, ROWS, 0)
    split = WL // 2 * WW
    differ = jnp.logical_and(last_lat, (key_at >= split) != (query_at >= split))
    excluded = jnp.logical_or(key_at >= WL * WW, differ)
    bias = jnp.where(excluded, -1e30, 0.0).astype(f32)
    head_of = lax.broadcasted_iota(jnp.int32, (GROUP, 1, SPAN), 2) // HS
    head = lax.broadcasted_iota(jnp.int32, (GROUP, 1, SPAN), 0)
    own_head = jnp.where(head_of == head, 1.0, 0.0).astype(f32)
    own_head_b = own_head.astype(bf16)

    def spread(rows):
        return (rows[None] * own_head_b).reshape(GROUP * ROWS, SPAN)

    def collect(rows):
        return jnp.sum(rows.reshape(GROUP, ROWS, SPAN) * own_head, axis=0).astype(bf16)

    for w in range(WINDOWS):
        for g in range(HEADS // GROUP):
            rows = slice(w * ROWS, (w + 1) * ROWS)
            at = [slice(b * D + g * SPAN, b * D + (g + 1) * SPAN) for b in range(3)]
            keys = packed_s[rows, at[1]]
            values = packed_s[rows, at[2]]
            queries = spread(packed_s[rows, at[0]])
            d_context = spread(dctx_s[rows, at[0]])
            scores = dot(keys, queries, NT) * (scaling * 1.4426950408889634) + bias
            expo = jnp.exp2(scores - jnp.max(scores, axis=0, keepdims=True))
            probs = expo * (1.0 / jnp.sum(expo, axis=0, keepdims=True))
            weights = probs.astype(bf16)
            d_weights = dot(values, d_context, NT)
            mean_d = jnp.sum(d_weights * probs, axis=0, keepdims=True)
            d_scaled = ((probs * scaling) * (d_weights - mean_d)).astype(bf16)
            ctx_s[rows, at[0]] = collect(dot(weights, values, TN))
            dpacked_s[rows, at[2]] = dot(weights, d_context).astype(bf16)
            dpacked_s[rows, at[0]] = collect(dot(d_scaled, keys, TN))
            dpacked_s[rows, at[1]] = dot(d_scaled, queries).astype(bf16)

    first = core == 0
    for strip in range(0, 8, 2):
        cols = slice(strip * 128, strip * 128 + 256)
        low = dot(scaled_s[...], dpacked_s[:, cols], TN)
        if strip < 4:
            high = dot(scaled_s[...], dpacked_s[:, 2 * D + strip * 128 : 2 * D + strip * 128 + 256], TN)
        else:
            high = dot(ctx_s[...], cot_s[:, strip * 128 - D : strip * 128 - D + 256], TN)
        keep = jnp.where(first, low, high).astype(bf16)
        give = jnp.where(first, high, low).astype(bf16)
        for k in range(2):
            to = slice((strip + k) * 512, (strip + k + 1) * 512)
            mine_ref[to, :] = keep[:, k * 128 : (k + 1) * 128]
            other_ref[to, :] = give[:, k * 128 : (k + 1) * 128]


def finish_kernel(
    latent_ref, cot_ref, ctx_ref, dpacked_ref, gain_ref, w_qkv_ref, w_out_ref, picks_ref,
    own_ref, back_ref, back_lon_ref, gain_rows_ref,
):
    latent = latent_ref[...].astype(f32)
    normed, recip_std = norm(latent)
    d_shifted = dot(dpacked_ref[...], w_qkv_ref[...], NT).astype(bf16).astype(f32)
    grad_gain = jnp.sum(d_shifted * normed, axis=0, keepdims=True)
    gain_rows_ref[...] = jnp.concatenate(
        [grad_gain[:, k * 128 : (k + 1) * 128] for k in range(4)] + [jnp.zeros((12, 128), f32)], axis=0
    ).astype(bf16)
    hidden = d_shifted * gain_ref[...]
    part = recip_std * (
        hidden
        - jnp.mean(hidden, axis=-1, keepdims=True)
        - normed * jnp.mean(hidden * normed, axis=-1, keepdims=True)
    )
    d_latent = (cot_ref[...].astype(f32) + part).astype(bf16)
    attn = dot(ctx_ref[...], w_out_ref[...]).astype(bf16).astype(f32)
    mixed = (latent + attn).astype(bf16)
    picks = picks_ref[...]
    for k, value in enumerate((mixed, d_latent)):
        moved = dot(picks, value, TN).astype(bf16)
        own_ref[k] = moved[:HALF]
        back_ref[k, :HALF] = moved[HALF : 2 * HALF]
        back_ref[k, HALF:] = moved[2 * HALF + EDGES :]
        back_lon_ref[k] = moved[2 * HALF : 2 * HALF + EDGES]


def here():
    return jnp.logical_and(lax.axis_index("x") == 3, lax.axis_index("yh") == 1), lax.axis_index("c")


def vmem_call(kernel, out_shapes, scratch, flops, moved, count):
    whole = pl.BlockSpec(memory_space=pltpu.VMEM)
    return pl.pallas_call(
        kernel,
        out_shape=out_shapes,
        in_specs=[whole] * count,
        out_specs=[whole] * len(out_shapes),
        scratch_shapes=scratch,
        compiler_params=pltpu.CompilerParams(vmem_limit_bytes=40 * 1024 * 1024),
        cost_estimate=pl.CostEstimate(flops=flops, bytes_accessed=moved, transcendentals=0),
    )


def shape(*dims, dtype=bf16):
    return jax.ShapeDtypeStruct(dims, dtype)


def block(where_am_i, latent, cot, halo_lat, halo_lon, halo_cor, gain, w_qkv, w_out):
    picks, w_out = vmem_call(picks_kernel, [shape(TOKENS, 384), shape(D, D)], [], 1_000_000, 500_000, 1)(w_out)
    mine, other, latent_w, cot_w, ctx, dpacked = vmem_call(
        functools.partial(attend_kernel, where_am_i),
        [
            shape(STRIP, 128), shape(STRIP, 128),
            shape(TOKENS, D), shape(TOKENS, D), shape(TOKENS, D), shape(TOKENS, 3 * D),
        ],
        [
            pltpu.VMEM((TOKENS, D), bf16), pltpu.VMEM((TOKENS, 3 * D), bf16), pltpu.VMEM((TOKENS, D), bf16),
        ],
        5_000_000_000, 8_000_000, 9,
    )(latent, cot, halo_lat, halo_lon, halo_cor, gain, w_qkv, w_out, picks)
    own, back, back_lon, gain_rows = vmem_call(
        finish_kernel,
        [shape(2, HALF, D), shape(2, BACK, D), shape(2, EDGES, D), shape(16, 128)],
        [], 1_500_000_000, 4_000_000, 8,
    )(latent_w, cot_w, ctx, dpacked, gain, w_qkv, w_out, picks)
    return own, back, back_lon, mine, other, gain_rows


def add_kernel(mine_ref, arrived_ref, gain_ref, chunks_ref):
    for k in range(16):
        at = slice(k * CHUNK, (k + 1) * CHUNK)
        chunks_ref[k, :CHUNK] = (mine_ref[at, :].astype(f32) + arrived_ref[at, :].astype(f32)).astype(bf16)
        chunks_ref[k, CHUNK:] = gain_ref[...]


def spread_kernel(total_ref, arrived_ref, came_ref, back_lon_ref, spread_ref, edge_ref):
    total = (total_ref[...].astype(f32) + arrived_ref[...].astype(f32)).astype(bf16)
    for k in range(16):
        spread_ref[k] = total
    for k in range(2):
        edge_ref[k, :EDGES] = back_lon_ref[k]
        edge_ref[k, EDGES:] = came_ref[k, HALF:]


def unpack_kernel(where_am_i, side, half_ref, *refs):
    qkv_ref, out_ref = refs[-4 - side], refs[-3 - side]
    wide_s, sems = refs[-2:]
    core = where_am_i()[1]
    low = core == side

    def store(start):
        for block in range(4):
            cols = slice(block * 256, (block + 1) * 256)
            if start:
                for k in range(4 * block, 4 * block + 4):
                    at = slice(k // 2 * 128, (k // 2 + 1) * 128)
                    wide_s[k % 2 * CHUNK : (k % 2 + 1) * CHUNK, at] = half_ref[k, :CHUNK].astype(f32)

            def copy(ref, first):
                to = ref.at[:, first : first + 256]
                move = pltpu.make_async_copy(wide_s.at[:, cols], to, sems.at[block])
                move.start() if start else move.wait()

            pl.when(low)(lambda: copy(qkv_ref, block * 256))
            if block < 2:
                pl.when(jnp.logical_not(low))(lambda: copy(qkv_ref, 2 * D + block * 256))
            else:
                pl.when(jnp.logical_not(low))(lambda: copy(out_ref, block * 256 - D))

    store(True)
    if side:
        own_ref, gain_ref = refs[0], refs[-3]
        gain = half_ref[0, CHUNK:].astype(f32) + own_ref[0, CHUNK:].astype(f32)
        for k in range(4):
            gain_ref[:, k * 128 : (k + 1) * 128] = gain[k : k + 1, :]
    store(False)


def unpack(where_am_i, side, half, *rest):
    whole = pl.BlockSpec(memory_space=pltpu.VMEM)
    stay = pl.BlockSpec(memory_space=pltpu.HBM)
    outs = [shape(D, 3 * D, dtype=f32), shape(D, D, dtype=f32)]
    return pl.pallas_call(
        functools.partial(unpack_kernel, where_am_i, side),
        out_shape=outs + [shape(1, D, dtype=f32)] * side,
        in_specs=[whole] + [whole, stay, stay] * side,
        out_specs=[stay, stay] + [whole] * side,
        scratch_shapes=[pltpu.VMEM((D, 2 * D), f32), pltpu.SemaphoreType.DMA((4,))],
        input_output_aliases={2: 0, 3: 1} if side else {},
        compiler_params=pltpu.CompilerParams(vmem_limit_bytes=40 * 1024 * 1024),
        cost_estimate=pl.CostEstimate(flops=1_000_000, bytes_accessed=3_000_000, transcendentals=0),
    )(half, *rest)


def place_kernel(own_ref, came_ref, edge_ref, mixed_ref, d_latent_ref):
    for k, out_ref in enumerate((mixed_ref, d_latent_ref)):
        for r in range(3):
            at = r * TILE[1]
            for first, body_ref, edges in ((0, came_ref, EDGES), (HALF, own_ref, 0)):
                edge = edge_ref[k, edges + r * EDGE : edges + (r + 1) * EDGE].astype(f32)
                body = body_ref[k, at : at + EDGE].astype(f32)
                out_ref[first + at : first + at + EDGE, :] = (body + edge).astype(bf16)
                out_ref[first + at + EDGE : first + at + TILE[1], :] = body_ref[k, at + EDGE : at + TILE[1]]


def shifted(lat_by, lon_by):
    pairs = []
    for i in range(256):
        lat, lon = i // 32, i % 32
        pairs.append((i, (lat + lat_by) % 8 * 32 + (lon + lon_by) % 32))
    return pairs


def swapped(bits):
    return [(i, i ^ bits) for i in range(256)]


def send(value, pairs):
    return lax.ppermute(value, ALL, pairs)


def sum_and_return(own, back, back_lon, mine, other, gain_rows):
    arrived = send(other, swapped(1))
    chunks = vmem_call(
        add_kernel, [shape(16, SUMMED, 128)], [], 1_000_000, 4_000_000, 3
    )(mine, arrived, gain_rows)[0]
    pieces = lax.all_to_all(chunks, PLANE, 0, 0, tiled=True)
    total = jnp.sum(pieces.astype(f32), axis=0).astype(bf16)
    for bits in (2, 4):
        total = (total.astype(f32) + send(total, swapped(bits)).astype(f32)).astype(bf16)
    spread, edge = vmem_call(
        spread_kernel, [shape(16, SUMMED, 128), shape(2, 2 * EDGES, D)], [], 1_000_000, 3_000_000, 4
    )(total, send(total, swapped(12)), came := send(back, shifted(1, 0)), back_lon)
    half = lax.all_to_all(spread, PLANE, 0, 0, tiled=True)
    edge = send(edge, shifted(0, 1))
    half, edge = lax.optimization_barrier((half, edge))
    arrived = send(half, swapped(1))
    parts = unpack(here, 0, half)
    mixed, d_latent = vmem_call(
        place_kernel, [shape(2 * HALF, D), shape(2 * HALF, D)], [], 1_000_000, 2_000_000, 3
    )(own, came, edge)
    grad_qkv, grad_out, grad_gain = unpack(here, 1, arrived, half, *parts)
    return mixed.reshape(*TILE, D), d_latent.reshape(*TILE, D), grad_qkv, grad_out, grad_gain.reshape(D)


def local(latent, norm_gain, w_qkv, w_out, cotangent):
    both = jnp.stack([latent[:3], cotangent[:3]])
    halo_lat = send(both.reshape(2, HALF, D), shifted(-1, 0))
    halo_cor = send(both[:, :, :EDGE].reshape(2, EDGES, D), shifted(-1, -1))
    edge = jnp.stack([latent[3:, :EDGE], cotangent[3:, :EDGE]])
    halo_lon = send(edge.reshape(2, EDGES, D), shifted(0, -1))
    return sum_and_return(*block(
        here, latent.reshape(-1, D), cotangent.reshape(-1, D), halo_lat, halo_lon, halo_cor,
        norm_gain.reshape(1, D), w_qkv, w_out,
    ))


def solution(mesh):
    fine = Mesh(mesh.devices.reshape(4, 2, 2, 8, 2), ALL)
    in_specs = (P(LAT, LON, None), P(), P(), P(), P(LAT, LON, None))
    out_specs = (P(LAT, LON, None), P(LAT, LON, None), P(), P(), P())
    return jax.shard_map(local, mesh=fine, in_specs=in_specs, out_specs=out_specs, check_vma=False)
```

time: 112 us -> 97.5 us (0.87)
  blocking collectives: 37.2 us -> 22 us
  starting transfers between devices: 37.7 us -> 43.9 us
  waiting for transfers between devices: 21.4 us -> 15.3 us
  Pallas kernels: 11.4 us -> 13.9 us
  local copies, waits for them, and re-layouts: 3.32 us -> 1.15 us
    all_to_all x2 -> x1, blocking collectives: 37.2 us -> 22 us  [sum_and_return(): pieces = lax.all_to_all(chunks, PLANE, 0, 0, tiled=True)]
    ppermute x11 -> x10, waiting for transfers between devices: 21.4 us -> 9.36 us  [send(): return lax.ppermute(value, ALL, pairs)]
    all_to_all x0 -> x1, waiting for transfers between devices: none -> 5.9 us  [sum_and_return(): half = lax.all_to_all(spread, PLANE, 0, 0, tiled=True)]
    all_to_all x0 -> x1, starting transfers between devices: none -> 5 us  [sum_and_return(): half = lax.all_to_all(spread, PLANE, 0, 0, tiled=True)]
    pallas_call x4 -> x8, Pallas kernels: 11.4 us -> 13.9 us  [the longest x1 6.61 us: block(): vmem_call(functools.partial(attend_kernel, where_am_i), [shape(STRIP, 128...]
    unnamed x12 -> x10, local copies, waits for them, and re-layouts: 2 us -> 0.03 us
    ppermute x11 -> x10, starting transfers between devices: 37.7 us -> 38.8 us  [send(): return lax.ppermute(value, ALL, pairs)]
  transfers between devices with their start and end apart: 11 -> 11, of which waited for: 6 -> 9; matrix products, arithmetic and copies ran while one was open for 0% -> 0% of each run, Pallas kernels for 1% -> 4%
where the time goes in v3:
time: 97.5 us; the launch traced here: 97.3 us
  starting transfers between devices  43.9 us (45%)
  blocking collectives  22 us (23%)
  waiting for transfers between devices  15.3 us (16%)
  Pallas kernels  13.9 us (14%)
  local copies, waits for them, and re-layouts  1.15 us (1%)
    ppermute x10, starting transfers between devices, send(): return lax.ppermute(value, ALL, pairs)  38.8 us
    all_to_all x1, blocking collectives, sum_and_return(): pieces = lax.all_to_all(chunks, PLANE, 0, 0, tiled=True)  22 us
    ppermute x10, waiting for transfers between devices, send(): return lax.ppermute(value, ALL, pairs)  9.36 us
    pallas_call x1, Pallas kernels, block(): vmem_call(functools.partial(attend_kernel, where_am_i), [shape(STRIP, 128...  6.61 us
    all_to_all x1, waiting for transfers between devices, sum_and_return(): half = lax.all_to_all(spread, PLANE, 0, 0, tiled=True)  5.9 us
    all_to_all x1, starting transfers between devices, sum_and_return(): half = lax.all_to_all(spread, PLANE, 0, 0, tiled=True)  5 us
    pallas_call x2, Pallas kernels, unpack(): pl.pallas_call(functools.partial(unpack_kernel, where_am_i, side), out_sh...  3.4 us
  transfers between devices with their start and end apart: 11, of which 9 were waited for; matrix products, arithmetic and copies ran while one was open for 0% of the time, Pallas kernels for 4%

profile of v3, /device:TPU:1, one launch (start us, length us, event | category | flops | bytes accessed | tf_op | source)
XLA Modules:
  0.0 97.3 jit_solution(17609236943635378434)
XLA Ops:
  0.6 0.0 copy-start.2
  0.6 0.0 copy-start.1
  0.7 0.0 copy-start
  0.7 1.1 %slice_bitcast_fusion = (bf16[1,3,48,512]{3,2,1,0:T(8,128)(2,1)S(1)}, bf16[3,48,512]{2,1,0:T(8,128)(2,1)S(1)}, bf16[3,48,512]{2,1,0:T(8,128)(2,1)S(1)}, bf16[1,3,48,512]{3,2,1,0:T(8,128)(2,1)S(1)}) fusion(bf16[6,48,512]{2,1,0:T(8,128)(2,1)} %param.9, bf16[6,48,512]{2,1,0:T(8,128)(2,1)} %param.5), kind=kLoop, calls=%fused_computation.5 | loop fusion | bytes 884736 | tf_op jit(solution)/shard_map/stack | solution.py:339
  1.8 0.0 copy-start.3
  1.8 0.0 copy-start.4
  1.8 6.0 %collective-permute-start = (bf16[2,144,512]{2,1,0:T(8,128)(2,1)S(1)}, bf16[2,144,512]{2,1,0:T(8,128)(2,1)S(1)}, u32[]{:S(2)}, u32[]{:S(2)}) collective-permute-start(bf16[2,144,512]{2,1,0:T(8,128)(2,1)S(1)} %pad_maximum_fusion), channel_id=1, source_target_pairs={{0,224},{1,225},{2,226},{3,227},{4,228},{5,229},{6,230},{7,231},{8... | collective-permute-start | bytes 884744 | tf_op jit(solution)/shard_map/ppermute | solution.py:311
  7.9 0.0 copy-done.1
  7.9 0.0 copy-done.2
  7.9 1.0 %collective-permute-start.1 = (bf16[2,48,512]{2,1,0:T(8,128)(2,1)S(1)}, bf16[2,48,512]{2,1,0:T(8,128)(2,1)S(1)}, u32[]{:S(2)}, u32[]{:S(2)}) collective-permute-start(bf16[2,48,512]{2,1,0:T(8,128)(2,1)S(1)} %pad_maximum_fusion.2), channel_id=1, source_target_pairs={{0,31},{1,0},{2,1},{3,2},{4,3},{5,4},{6,5},{7,6},{8,7},{9,8},{10,9... | collective-permute-start | bytes 294920 | tf_op jit(solution)/shard_map/ppermute | solution.py:311
  9.0 6.6 %collective-permute-start.2 = (bf16[2,48,512]{2,1,0:T(8,128)(2,1)S(1)}, bf16[2,48,512]{2,1,0:T(8,128)(2,1)S(1)}, u32[]{:S(2)}, u32[]{:S(2)}) collective-permute-start(bf16[2,48,512]{2,1,0:T(8,128)(2,1)S(1)} %bitcast.23), channel_id=1, source_target_pairs={{0,255},{1,224},{2,225},{3,226},{4,227},{5,228},{6,229},{7,230},{8... | collective-permute-start | bytes 294920 | tf_op jit(solution)/shard_map/ppermute | solution.py:311
  15.6 0.0 copy-done
  15.6 0.1 shard_map.92
  15.7 0.0 collective-permute-done.1.halo_lon_ref
  15.7 1.5 %collective-permute-done.2.halo_cor_ref = bf16[2,48,512]{2,1,0:T(8,128)(2,1)S(1)} collective-permute-done((bf16[2,48,512]{2,1,0:T(8,128)(2,1)S(1)}, bf16[2,48,512]{2,1,0:T(8,128)(2,1)S(1)}, u32[]{:S(2)}, u32[]{:S(2)}) %collective-permute-start.2) | collective-permute-done | bytes 98336 | tf_op jit(solution)/shard_map/ppermute | solution.py:311
  17.2 0.0 collective-permute-done.halo_lat_ref
  17.2 0.0 copy-done.3
  17.2 0.0 copy-done.4
  17.2 6.6 %shard_map.93 = (bf16[4096,128]{1,0:T(8,128)(2,1)S(1)}, bf16[4096,128]{1,0:T(8,128)(2,1)S(1)}, bf16[320,512]{1,0:T(8,128)(2,1)S(1)}, bf16[320,512]{1,0:T(8,128)(...) custom-call(bf16[288,512]{1,0:T(8,128)(2,1)S(1)} %bitcast.15, bf16[288,512]{1,0:T(8,128)(2,1)S(1)} %bitcast.16, ...), custom_call_target="tpu_custom_call" | custom-call | flops 5000000000 | bytes 8000000 | tf_op jit(solution)/shard_map/pallas_call | solution.py:202
  23.9 2.6 %collective-permute-start.4 = (bf16[4096,128]{1,0:T(8,128)(2,1)S(1)}, bf16[4096,128]{1,0:T(8,128)(2,1)S(1)}, u32[]{:S(2)}, u32[]{:S(2)}) collective-permute-start(bf16[4096,128]{1,0:T(8,128)(2,1)S(1)} %get-tuple-element.37), channel_id=1, source_target_pairs={{0,1},{1,0},{2,3},{3,2},{4,5},{5,4},{6,7},{7,6},{8,9},{9,8},{10,11... | collective-permute-start | bytes 3145736 | tf_op jit(solution)/shard_map/ppermute | solution.py:311
  26.4 1.5 %shard_map.94 = (bf16[2,144,512]{2,1,0:T(8,128)(2,1)S(1)}, bf16[2,192,512]{2,1,0:T(8,128)(2,1)S(1)}, bf16[2,48,512]{2,1,0:T(8,128)(2,1)S(1)}, bf16[16,128]{1,0:T(8,128)(2,1)S(1)}) custom-call(bf16[320,512]{1,0:T(8,128)(2,1)S(1)} %get-tuple-element.30.latent_ref, bf16[320,512]{1,0:T(8,128)(2,1)S(1)} %get-tuple-element.31.cot_ref, ...), custom_call_target="tpu_custom_call" | custom-call | flops 1500000000 | bytes 4000000 | tf_op jit(solution)/shard_map/pallas_call | solution.py:213
  28.0 0.7 collective-permute-done.4.arrived_ref
  28.7 0.3 shard_map.95
  29.0 22.0 %all_to_all.10 = bf16[16,272,128]{2,1,0:T(8,128)(2,1)S(1)} all-to-all(bf16[16,272,128]{2,1,0:T(8,128)(2,1)S(1)} %shard_map.95), channel_id=1, replica_groups=mesh['x'=4,'yh'=2,'yl'=2,'z'=8,'c'=2] {'x','yh','yl'}, dimensions={0} | all-to-all | bytes 2228224 | tf_op jit(solution)/shard_map/all_to_all | solution.py:319
  51.0 0.2 reduce_sum.12
  51.1 1.4 %collective-permute-start.5 = (bf16[272,128]{1,0:T(8,128)(2,1)S(1)}, bf16[272,128]{1,0:T(8,128)(2,1)S(1)}, u32[]{:S(2)}, u32[]{:S(2)}) collective-permute-start(bf16[272,128]{1,0:T(8,128)(2,1)S(1)} %reduce_sum.12), channel_id=1, source_target_pairs={{0,2},{1,3},{2,0},{3,1},{4,6},{5,7},{6,4},{7,5},{8,10},{9,11},{10,... | collective-permute-start | bytes 208904 | tf_op jit(solution)/shard_map/ppermute | solution.py:311
  52.5 1.2 %collective-permute-start.3 = (bf16[2,192,512]{2,1,0:T(8,128)(2,1)S(1)}, bf16[2,192,512]{2,1,0:T(8,128)(2,1)S(1)}, u32[]{:S(2)}, u32[]{:S(2)}) collective-permute-start(bf16[2,192,512]{2,1,0:T(8,128)(2,1)S(1)} %get-tuple-element.35), channel_id=1, source_target_pairs={{0,32},{1,33},{2,34},{3,35},{4,36},{5,37},{6,38},{7,39},{8,40},{9,... | collective-permute-start | bytes 1179656 | tf_op jit(solution)/shard_map/ppermute | solution.py:311
  53.7 0.7 collective-permute-done.5
  54.4 2.9 %collective-permute-start.6 = (bf16[272,128]{1,0:T(8,128)(2,1)S(1)}, bf16[272,128]{1,0:T(8,128)(2,1)S(1)}, u32[]{:S(2)}, u32[]{:S(2)}) collective-permute-start(bf16[272,128]{1,0:T(8,128)(2,1)S(1)} %add_convert_fusion.1), channel_id=1, source_target_pairs={{0,4},{1,5},{2,6},{3,7},{4,0},{5,1},{6,2},{7,3},{8,12},{9,13},{10,... | collective-permute-start | bytes 208904 | tf_op jit(solution)/shard_map/ppermute | solution.py:311
  57.3 1.7 %collective-permute-done.6 = bf16[272,128]{1,0:T(8,128)(2,1)S(1)} collective-permute-done((bf16[272,128]{1,0:T(8,128)(2,1)S(1)}, bf16[272,128]{1,0:T(8,128)(2,1)S(1)}, u32[]{:S(2)}, u32[]{:S(2)}) %collective-permute-start.6) | collective-permute-done | bytes 69664 | tf_op jit(solution)/shard_map/ppermute | solution.py:311
  59.0 5.7 %collective-permute-start.7 = (bf16[272,128]{1,0:T(8,128)(2,1)S(1)}, bf16[272,128]{1,0:T(8,128)(2,1)S(1)}, u32[]{:S(2)}, u32[]{:S(2)}) collective-permute-start(bf16[272,128]{1,0:T(8,128)(2,1)S(1)} %add_convert_fusion.total_ref), channel_id=1, source_target_pairs={{0,12},{1,13},{2,14},{3,15},{4,8},{5,9},{6,10},{7,11},{8,4},{9,5},... | collective-permute-start | bytes 208904 | tf_op jit(solution)/shard_map/ppermute | solution.py:311
  64.7 0.1 collective-permute-done.3.came_ref
  64.7 1.9 %collective-permute-done.7.arrived_ref = bf16[272,128]{1,0:T(8,128)(2,1)S(1)} collective-permute-done((bf16[272,128]{1,0:T(8,128)(2,1)S(1)}, bf16[272,128]{1,0:T(8,128)(2,1)S(1)}, u32[]{:S(2)}, u32[]{:S(2)}) %collective-permute-start.7) | collective-permute-done | bytes 69664 | tf_op jit(solution)/shard_map/ppermute | solution.py:311
  66.7 1.1 %shard_map.96 = (bf16[16,272,128]{2,1,0:T(8,128)(2,1)}, bf16[2,96,512]{2,1,0:T(8,128)(2,1)S(1)}) custom-call(bf16[272,128]{1,0:T(8,128)(2,1)S(1)} %add_convert_fusion.total_ref, bf16[272,128]{1,0:T(8,128)(2,1)S(1)} %collective-permute-done.7.arrived_ref, bf16[2,192,512]{2,1,0:T(8,128)(2,1)S(1)} %collective-permute-done.3.came_ref, ...), custom_call_target="tpu_custom_call" | custom-call | flops 1000000 | bytes 3000000 | tf_op jit(solution)/shard_map/pallas_call | solution.py:323
  67.7 5.0 %all-to-all-start.1 = ((bf16[16,272,128]{2,1,0:T(8,128)(2,1)}), bf16[16,272,128]{2,1,0:T(8,128)(2,1)S(1)}, u32[]{:S(2)}, u32[]{:S(2)}) async-start(bf16[16,272,128]{2,1,0:T(8,128)(2,1)} %get-tuple-element.40), calls=%async_computation.1 | async-start | bytes 2228224 | tf_op jit(solution)/shard_map/all_to_all | solution.py:326
  72.8 5.3 %collective-permute-start.8 = (bf16[2,96,512]{2,1,0:T(8,128)(2,1)S(1)}, bf16[2,96,512]{2,1,0:T(8,128)(2,1)S(1)}, u32[]{:S(2)}, u32[]{:S(2)}) collective-permute-start(bf16[2,96,512]{2,1,0:T(8,128)(2,1)S(1)} %get-tuple-element.41), channel_id=1, source_target_pairs={{0,1},{1,2},{2,3},{3,4},{4,5},{5,6},{6,7},{7,8},{8,9},{9,10},{10,1... | collective-permute-start | bytes 589832 | tf_op jit(solution)/shard_map/ppermute | solution.py:311
  78.0 2.6 %collective-permute-done.8.edge_ref = bf16[2,96,512]{2,1,0:T(8,128)(2,1)S(1)} collective-permute-done((bf16[2,96,512]{2,1,0:T(8,128)(2,1)S(1)}, bf16[2,96,512]{2,1,0:T(8,128)(2,1)S(1)}, u32[]{:S(2)}, u32[]{:S(2)}) %collective-permute-start.8) | collective-permute-done | bytes 196640 | tf_op jit(solution)/shard_map/ppermute | solution.py:311
  80.7 5.9 %all-to-all-done.1.half_ref.refs_0_ = bf16[16,272,128]{2,1,0:T(8,128)(2,1)S(1)} async-done(((bf16[16,272,128]{2,1,0:T(8,128)(2,1)}), bf16[16,272,128]{2,1,0:T(8,128)(2,1)S(1)}, u32[]{:S(2)}, u32[]{:S(2)}) %all-to-all-start.1) | async-done | bytes 1114144 | tf_op jit(solution)/shard_map/all_to_all | solution.py:326
  86.6 6.2 %collective-permute-start.9 = (bf16[16,272,128]{2,1,0:T(8,128)(2,1)S(1)}, bf16[16,272,128]{2,1,0:T(8,128)(2,1)S(1)}, u32[]{:S(2)}, u32[]{:S(2)}) collective-permute-start(bf16[16,272,128]{2,1,0:T(8,128)(2,1)S(1)} %all-to-all-done.1.half_ref.refs_0_), channel_id=1, source_target_pairs={{0,1},{1,0},{2,3},{3,2},{4,5},{5,4},{6,7},{7,6},{8,9},{9,8},{10,11... | collective-permute-start | bytes 3342344 | tf_op jit(solution)/shard_map/ppermute | solution.py:311
  92.7 1.4 %shard_map.98 = (f32[512,1536]{1,0:T(8,128)}, f32[512,512]{1,0:T(8,128)}) custom-call(bf16[16,272,128]{2,1,0:T(8,128)(2,1)S(1)} %all-to-all-done.1.half_ref.refs_0_), custom_call_target="tpu_custom_call" | custom-call | flops 1000000 | bytes 3000000 | tf_op jit(solution)/shard_map/pallas_call | solution.py:275
  94.2 0.9 shard_map.97
  95.0 0.1 collective-permute-done.9.half_ref
  95.1 2.0 %shard_map.99 = (f32[512,1536]{1,0:T(8,128)}, f32[512,512]{1,0:T(8,128)}, f32[1,512]{1,0:T(1,128)}) custom-call(bf16[16,272,128]{2,1,0:T(8,128)(2,1)S(1)} %collective-permute-done.9.half_ref, bf16[16,272,128]{2,1,0:T(8,128)(2,1)S(1)} %all-to-all-done.1.half_ref.refs_0_, ...), custom_call_target="tpu_custom_call", output_to_operand_aliasing={{0}: (2, {}), {1}: (3, {})} | custom-call | flops 1000000 | bytes 3000000 | tf_op jit(solution)/shard_map/pallas_call | solution.py:275
  (7 shorter events, 0.1 us)
Async XLA Ops:
  0.6 7.2 %copy-start.2 = (bf16[6,48,512]{2,1,0:T(8,128)(2,1)S(1)}, bf16[6,48,512]{2,1,0:T(8,128)(2,1)}, u32[]{:S(2)}) copy-start(bf16[6,48,512]{2,1,0:T(8,128)(2,1)} %param.9) | copy-start | bytes 884740
  0.6 7.2 %copy-start.1 = (bf16[6,48,512]{2,1,0:T(8,128)(2,1)S(1)}, bf16[6,48,512]{2,1,0:T(8,128)(2,1)}, u32[]{:S(2)}) copy-start(bf16[6,48,512]{2,1,0:T(8,128)(2,1)} %param.5) | copy-start | bytes 884740
  0.7 14.9 %copy-start = (bf16[512,512]{1,0:T(8,128)(2,1)S(1)}, bf16[512,512]{1,0:T(8,128)(2,1)}, u32[]{:S(2)}) copy-start(bf16[512,512]{1,0:T(8,128)(2,1)} %w_out_ref.1) | copy-start | bytes 1572868
  1.8 15.5 %copy-start.3 = (bf16[512,1536]{1,0:T(8,128)(2,1)S(1)}, bf16[512,1536]{1,0:T(8,128)(2,1)}, u32[]{:S(2)}) copy-start(bf16[512,1536]{1,0:T(8,128)(2,1)} %w_qkv_ref.3) | copy-start | bytes 4718596
  1.8 15.4 %copy-start.4 = (f32[512]{0:T(512)S(1)}, f32[512]{0:T(512)}, u32[]{:S(2)}) copy-start(f32[512]{0:T(512)} %param.6) | copy-start | bytes 6148
  1.8 15.4 %collective-permute-start = (bf16[2,144,512]{2,1,0:T(8,128)(2,1)S(1)}, bf16[2,144,512]{2,1,0:T(8,128)(2,1)S(1)}, u32[]{:S(2)}, u32[]{:S(2)}) collective-permute-start(bf16[2,144,512]{2,1,0:T(8,128)(2,1)S(1)} %pad_maximum_fusion), channel_id=1, source_target_pairs={{0,224},{1,225},{2,226},{3,227},{4,228},{5,229},{6,230},{7,231},{8... | collective-permute-start | bytes 884744 | tf_op jit(solution)/shard_map/ppermute | solution.py:311
  7.9 7.8 %collective-permute-start.1 = (bf16[2,48,512]{2,1,0:T(8,128)(2,1)S(1)}, bf16[2,48,512]{2,1,0:T(8,128)(2,1)S(1)}, u32[]{:S(2)}, u32[]{:S(2)}) collective-permute-start(bf16[2,48,512]{2,1,0:T(8,128)(2,1)S(1)} %pad_maximum_fusion.2), channel_id=1, source_target_pairs={{0,31},{1,0},{2,1},{3,2},{4,3},{5,4},{6,5},{7,6},{8,7},{9,8},{10,9... | collective-permute-start | bytes 294920 | tf_op jit(solution)/shard_map/ppermute | solution.py:311
  9.0 8.3 %collective-permute-start.2 = (bf16[2,48,512]{2,1,0:T(8,128)(2,1)S(1)}, bf16[2,48,512]{2,1,0:T(8,128)(2,1)S(1)}, u32[]{:S(2)}, u32[]{:S(2)}) collective-permute-start(bf16[2,48,512]{2,1,0:T(8,128)(2,1)S(1)} %bitcast.23), channel_id=1, source_target_pairs={{0,255},{1,224},{2,225},{3,226},{4,227},{5,228},{6,229},{7,230},{8... | collective-permute-start | bytes 294920 | tf_op jit(solution)/shard_map/ppermute | solution.py:311
  23.9 4.8 %collective-permute-start.4 = (bf16[4096,128]{1,0:T(8,128)(2,1)S(1)}, bf16[4096,128]{1,0:T(8,128)(2,1)S(1)}, u32[]{:S(2)}, u32[]{:S(2)}) collective-permute-start(bf16[4096,128]{1,0:T(8,128)(2,1)S(1)} %get-tuple-element.37), channel_id=1, source_target_pairs={{0,1},{1,0},{2,3},{3,2},{4,5},{5,4},{6,7},{7,6},{8,9},{9,8},{10,11... | collective-permute-start | bytes 3145736 | tf_op jit(solution)/shard_map/ppermute | solution.py:311
  51.1 3.2 %collective-permute-start.5 = (bf16[272,128]{1,0:T(8,128)(2,1)S(1)}, bf16[272,128]{1,0:T(8,128)(2,1)S(1)}, u32[]{:S(2)}, u32[]{:S(2)}) collective-permute-start(bf16[272,128]{1,0:T(8,128)(2,1)S(1)} %reduce_sum.12), channel_id=1, source_target_pairs={{0,2},{1,3},{2,0},{3,1},{4,6},{5,7},{6,4},{7,5},{8,10},{9,11},{10,... | collective-permute-start | bytes 208904 | tf_op jit(solution)/shard_map/ppermute | solution.py:311
  52.5 12.3 %collective-permute-start.3 = (bf16[2,192,512]{2,1,0:T(8,128)(2,1)S(1)}, bf16[2,192,512]{2,1,0:T(8,128)(2,1)S(1)}, u32[]{:S(2)}, u32[]{:S(2)}) collective-permute-start(bf16[2,192,512]{2,1,0:T(8,128)(2,1)S(1)} %get-tuple-element.35), channel_id=1, source_target_pairs={{0,32},{1,33},{2,34},{3,35},{4,36},{5,37},{6,38},{7,39},{8,40},{9,... | collective-permute-start | bytes 1179656 | tf_op jit(solution)/shard_map/ppermute | solution.py:311
  54.4 4.6 %collective-permute-start.6 = (bf16[272,128]{1,0:T(8,128)(2,1)S(1)}, bf16[272,128]{1,0:T(8,128)(2,1)S(1)}, u32[]{:S(2)}, u32[]{:S(2)}) collective-permute-start(bf16[272,128]{1,0:T(8,128)(2,1)S(1)} %add_convert_fusion.1), channel_id=1, source_target_pairs={{0,4},{1,5},{2,6},{3,7},{4,0},{5,1},{6,2},{7,3},{8,12},{9,13},{10,... | collective-permute-start | bytes 208904 | tf_op jit(solution)/shard_map/ppermute | solution.py:311
  59.0 7.7 %collective-permute-start.7 = (bf16[272,128]{1,0:T(8,128)(2,1)S(1)}, bf16[272,128]{1,0:T(8,128)(2,1)S(1)}, u32[]{:S(2)}, u32[]{:S(2)}) collective-permute-start(bf16[272,128]{1,0:T(8,128)(2,1)S(1)} %add_convert_fusion.total_ref), channel_id=1, source_target_pairs={{0,12},{1,13},{2,14},{3,15},{4,8},{5,9},{6,10},{7,11},{8,4},{9,5},... | collective-permute-start | bytes 208904 | tf_op jit(solution)/shard_map/ppermute | solution.py:311
  67.7 18.8 %all-to-all-start.1 = ((bf16[16,272,128]{2,1,0:T(8,128)(2,1)}), bf16[16,272,128]{2,1,0:T(8,128)(2,1)S(1)}, u32[]{:S(2)}, u32[]{:S(2)}) async-start(bf16[16,272,128]{2,1,0:T(8,128)(2,1)} %get-tuple-element.40), calls=%async_computation.1 | async-start | bytes 2228224 | tf_op jit(solution)/shard_map/all_to_all | solution.py:326
  72.8 7.9 %collective-permute-start.8 = (bf16[2,96,512]{2,1,0:T(8,128)(2,1)S(1)}, bf16[2,96,512]{2,1,0:T(8,128)(2,1)S(1)}, u32[]{:S(2)}, u32[]{:S(2)}) collective-permute-start(bf16[2,96,512]{2,1,0:T(8,128)(2,1)S(1)} %get-tuple-element.41), channel_id=1, source_target_pairs={{0,1},{1,2},{2,3},{3,4},{4,5},{5,6},{6,7},{7,8},{8,9},{9,10},{10,1... | collective-permute-start | bytes 589832 | tf_op jit(solution)/shard_map/ppermute | solution.py:311
  86.6 8.6 %collective-permute-start.9 = (bf16[16,272,128]{2,1,0:T(8,128)(2,1)S(1)}, bf16[16,272,128]{2,1,0:T(8,128)(2,1)S(1)}, u32[]{:S(2)}, u32[]{:S(2)}) collective-permute-start(bf16[16,272,128]{2,1,0:T(8,128)(2,1)S(1)} %all-to-all-done.1.half_ref.refs_0_), channel_id=1, source_target_pairs={{0,1},{1,0},{2,3},{3,2},{4,5},{5,4},{6,7},{7,6},{8,9},{9,8},{10,11... | collective-permute-start | bytes 3342344 | tf_op jit(solution)/shard_map/ppermute | solution.py:311

commit v4 on v3

--- a/solution.py
+++ b/solution.py
@@ -22,12 +22,12 @@
 TOKENS = WINDOWS * ROWS
 GROUP = 8
 SPAN = GROUP * HS
-EDGE = 16
+EDGE = 8
 HALF = 3 * TILE[1]
 EDGES = 3 * EDGE
 STRIP = 512 * 8
 CHUNK = STRIP // 16
-SUMMED = CHUNK + 16
+SUMMED = CHUNK + 8
 BACK = HALF + EDGES
 f32 = jnp.float32
 bf16 = jnp.bfloat16
@@ -46,7 +46,8 @@
     return centred * recip_std, recip_std
 
 
-def picks_kernel(w_out_ref, picks_ref, w_out_s):
+def prepare_kernel(w_qkv_ref, w_out_ref, picks_ref, w_qkv_s, w_out_s):
+    w_qkv_s[...] = w_qkv_ref[...]
     w_out_s[...] = w_out_ref[...]
     def count(value, step, upto):
         return sum(jnp.where(value >= step * k, 1, 0) for k in range(1, upto))
@@ -67,18 +68,32 @@
         picks_ref[:, k * 128 : (k + 1) * 128] = jnp.where(at == lane + k * 128, 1.0, 0.0).astype(bf16)
 
 
+def weight_grads(side, scaled_ref, ctx_ref, cot_ref, dpacked_ref, to_ref):
+    for block in range(4):
+        if side and block > 1:
+            pair = ctx_ref[...], cot_ref[:, (block - 2) * 256 : (block - 1) * 256]
+        else:
+            first = side * 2 * D + block * 256
+            pair = scaled_ref[...], dpacked_ref[:, first : first + 256]
+        part = dot(*pair, TN).astype(bf16)
+        for k in range(2):
+            at = (2 * block + k) * D
+            to_ref[at : at + D, :] = part[:, k * 128 : (k + 1) * 128]
+
+
 def attend_kernel(
     where_am_i,
     lat_ref, cot_ref, halo_lat_ref, halo_lon_ref, halo_cor_ref, gain_ref, w_qkv_ref, w_out_ref, picks_ref,
-    mine_ref, other_ref, latent_s, cot_s, ctx_s, dpacked_s,
-    scaled_s, packed_s, dctx_s,
+    other_ref, latent_s, cot_s, ctx_s, dpacked_s, scaled_s,
+    packed_s, dctx_s,
 ):
     last_lat, core = where_am_i()
     picks = picks_ref[...]
 
     def gather(own, at):
         stack = jnp.concatenate(
-            [own[HALF:, :], halo_lat_ref[at], halo_lon_ref[at], halo_cor_ref[at]], axis=0
+            [own[HALF:, :], halo_lat_ref[at], halo_lon_ref[at], halo_cor_ref[at], jnp.zeros((48, D), bf16)],
+            axis=0,
         )
         return dot(picks, stack)
 
@@ -131,32 +146,24 @@
             dpacked_s[rows, at[0]] = collect(dot(d_scaled, keys, TN))
             dpacked_s[rows, at[1]] = dot(d_scaled, queries).astype(bf16)
 
-    first = core == 0
-    for strip in range(0, 8, 2):
-        cols = slice(strip * 128, strip * 128 + 256)
-        low = dot(scaled_s[...], dpacked_s[:, cols], TN)
-        if strip < 4:
-            high = dot(scaled_s[...], dpacked_s[:, 2 * D + strip * 128 : 2 * D + strip * 128 + 256], TN)
-        else:
-            high = dot(ctx_s[...], cot_s[:, strip * 128 - D : strip * 128 - D + 256], TN)
-        keep = jnp.where(first, low, high).astype(bf16)
-        give = jnp.where(first, high, low).astype(bf16)
-        for k in range(2):
-            to = slice((strip + k) * 512, (strip + k + 1) * 512)
-            mine_ref[to, :] = keep[:, k * 128 : (k + 1) * 128]
-            other_ref[to, :] = give[:, k * 128 : (k + 1) * 128]
+    pl.when(core == 1)(lambda: weight_grads(0, scaled_s, ctx_s, cot_s, dpacked_s, other_ref))
+    pl.when(core == 0)(lambda: weight_grads(1, scaled_s, ctx_s, cot_s, dpacked_s, other_ref))
 
 
 def finish_kernel(
-    latent_ref, cot_ref, ctx_ref, dpacked_ref, gain_ref, w_qkv_ref, w_out_ref, picks_ref,
-    own_ref, back_ref, back_lon_ref, gain_rows_ref,
+    where_am_i,
+    latent_ref, cot_ref, ctx_ref, dpacked_ref, scaled_ref, gain_ref, w_qkv_ref, w_out_ref, picks_ref,
+    own_ref, back_ref, back_lon_ref, gain_rows_ref, mine_ref,
 ):
+    core = where_am_i()[1]
+    pl.when(core == 0)(lambda: weight_grads(0, scaled_ref, ctx_ref, cot_ref, dpacked_ref, mine_ref))
+    pl.when(core == 1)(lambda: weight_grads(1, scaled_ref, ctx_ref, cot_ref, dpacked_ref, mine_ref))
     latent = latent_ref[...].astype(f32)
     normed, recip_std = norm(latent)
     d_shifted = dot(dpacked_ref[...], w_qkv_ref[...], NT).astype(bf16).astype(f32)
     grad_gain = jnp.sum(d_shifted * normed, axis=0, keepdims=True)
     gain_rows_ref[...] = jnp.concatenate(
-        [grad_gain[:, k * 128 : (k + 1) * 128] for k in range(4)] + [jnp.zeros((12, 128), f32)], axis=0
+        [grad_gain[:, k * 128 : (k + 1) * 128] for k in range(4)] + [jnp.zeros((4, 128), f32)], axis=0
     ).astype(bf16)
     hidden = d_shifted * gain_ref[...]
     part = recip_std * (
@@ -172,7 +179,7 @@
         moved = dot(picks, value, TN).astype(bf16)
         own_ref[k] = moved[:HALF]
         back_ref[k, :HALF] = moved[HALF : 2 * HALF]
-        back_ref[k, HALF:] = moved[2 * HALF + EDGES :]
+        back_ref[k, HALF:] = moved[2 * HALF + EDGES : 2 * HALF + 2 * EDGES]
         back_lon_ref[k] = moved[2 * HALF : 2 * HALF + EDGES]
 
 
@@ -180,7 +187,7 @@
     return jnp.logical_and(lax.axis_index("x") == 3, lax.axis_index("yh") == 1), lax.axis_index("c")
 
 
-def vmem_call(kernel, out_shapes, scratch, flops, moved, count):
+def vmem_call(kernel, out_shapes, scratch, flops, moved, count, mebibytes=12):
     whole = pl.BlockSpec(memory_space=pltpu.VMEM)
     return pl.pallas_call(
         kernel,
@@ -188,7 +195,7 @@
         in_specs=[whole] * count,
         out_specs=[whole] * len(out_shapes),
         scratch_shapes=scratch,
-        compiler_params=pltpu.CompilerParams(vmem_limit_bytes=40 * 1024 * 1024),
+        compiler_params=pltpu.CompilerParams(vmem_limit_bytes=mebibytes * 1024 * 1024),
         cost_estimate=pl.CostEstimate(flops=flops, bytes_accessed=moved, transcendentals=0),
     )
 
@@ -198,23 +205,23 @@
 
 
 def block(where_am_i, latent, cot, halo_lat, halo_lon, halo_cor, gain, w_qkv, w_out):
-    picks, w_out = vmem_call(picks_kernel, [shape(TOKENS, 384), shape(D, D)], [], 1_000_000, 500_000, 1)(w_out)
-    mine, other, latent_w, cot_w, ctx, dpacked = vmem_call(
+    picks, w_qkv, w_out = vmem_call(
+        prepare_kernel, [shape(TOKENS, 384), shape(D, 3 * D), shape(D, D)], [], 1_000_000, 4_000_000, 2
+    )(w_qkv, w_out)
+    other, *kept = vmem_call(
         functools.partial(attend_kernel, where_am_i),
         [
-            shape(STRIP, 128), shape(STRIP, 128),
-            shape(TOKENS, D), shape(TOKENS, D), shape(TOKENS, D), shape(TOKENS, 3 * D),
+            shape(STRIP, 128),
+            shape(TOKENS, D), shape(TOKENS, D), shape(TOKENS, D), shape(TOKENS, 3 * D), shape(TOKENS, D),
         ],
-        [
-            pltpu.VMEM((TOKENS, D), bf16), pltpu.VMEM((TOKENS, 3 * D), bf16), pltpu.VMEM((TOKENS, D), bf16),
-        ],
-        5_000_000_000, 8_000_000, 9,
+        [pltpu.VMEM((TOKENS, 3 * D), bf16), pltpu.VMEM((TOKENS, D), bf16)],
+        5_000_000_000, 8_000_000, 9, 32,
     )(latent, cot, halo_lat, halo_lon, halo_cor, gain, w_qkv, w_out, picks)
-    own, back, back_lon, gain_rows = vmem_call(
-        finish_kernel,
-        [shape(2, HALF, D), shape(2, BACK, D), shape(2, EDGES, D), shape(16, 128)],
-        [], 1_500_000_000, 4_000_000, 8,
-    )(latent_w, cot_w, ctx, dpacked, gain, w_qkv, w_out, picks)
+    own, back, back_lon, gain_rows, mine = vmem_call(
+        functools.partial(finish_kernel, where_am_i),
+        [shape(2, HALF, D), shape(2, BACK, D), shape(2, EDGES, D), shape(8, 128), shape(STRIP, 128)],
+        [], 1_500_000_000, 4_000_000, 9, 32,
+    )(*kept, gain, w_qkv, w_out, picks)
     return own, back, back_lon, mine, other, gain_rows
 
 
@@ -235,7 +242,7 @@
 
 
 def unpack_kernel(where_am_i, side, half_ref, *refs):
-    qkv_ref, out_ref = refs[-4 - side], refs[-3 - side]
+    qkv_ref, out_ref = refs[3:5] if side else refs[:2]
     wide_s, sems = refs[-2:]
     core = where_am_i()[1]
     low = core == side
@@ -259,13 +266,17 @@
             else:
                 pl.when(jnp.logical_not(low))(lambda: copy(out_ref, block * 256 - D))
 
-    store(True)
     if side:
-        own_ref, gain_ref = refs[0], refs[-3]
+        own_ref, gain_ref, gain_s, gain_sem = refs[0], refs[5], *refs[6:8]
         gain = half_ref[0, CHUNK:].astype(f32) + own_ref[0, CHUNK:].astype(f32)
         for k in range(4):
-            gain_ref[:, k * 128 : (k + 1) * 128] = gain[k : k + 1, :]
+            gain_s[:, k * 128 : (k + 1) * 128] = gain[k : k + 1, :]
+        move = pltpu.make_async_copy(gain_s, gain_ref, gain_sem)
+        move.start()
+    store(True)
     store(False)
+    if side:
+        move.wait()
 
 
 def unpack(where_am_i, side, half, *rest):
@@ -276,10 +287,11 @@
         functools.partial(unpack_kernel, where_am_i, side),
         out_shape=outs + [shape(1, D, dtype=f32)] * side,
         in_specs=[whole] + [whole, stay, stay] * side,
-        out_specs=[stay, stay] + [whole] * side,
-        scratch_shapes=[pltpu.VMEM((D, 2 * D), f32), pltpu.SemaphoreType.DMA((4,))],
+        out_specs=[stay] * (2 + side),
+        scratch_shapes=[pltpu.VMEM((1, D), f32), pltpu.SemaphoreType.DMA] * side
+        + [pltpu.VMEM((D, 2 * D), f32), pltpu.SemaphoreType.DMA((4,))],
         input_output_aliases={2: 0, 3: 1} if side else {},
-        compiler_params=pltpu.CompilerParams(vmem_limit_bytes=40 * 1024 * 1024),
+        compiler_params=pltpu.CompilerParams(vmem_limit_bytes=12 * 1024 * 1024),
         cost_estimate=pl.CostEstimate(flops=1_000_000, bytes_accessed=3_000_000, transcendentals=0),
     )(half, *rest)
 
@@ -320,9 +332,10 @@
     total = jnp.sum(pieces.astype(f32), axis=0).astype(bf16)
     for bits in (2, 4):
         total = (total.astype(f32) + send(total, swapped(bits)).astype(f32)).astype(bf16)
+    came = send(back, shifted(1, 0))
     spread, edge = vmem_call(
         spread_kernel, [shape(16, SUMMED, 128), shape(2, 2 * EDGES, D)], [], 1_000_000, 3_000_000, 4
-    )(total, send(total, swapped(12)), came := send(back, shifted(1, 0)), back_lon)
+    )(total, send(total, swapped(12)), came, back_lon)
     half = lax.all_to_all(spread, PLANE, 0, 0, tiled=True)
     edge = send(edge, shifted(0, 1))
     half, edge = lax.optimization_barrier((half, edge))

time: 97.5 us -> 94.5 us (0.969)
  starting transfers between devices: 43.9 us -> 37.3 us
  local copies, waits for them, and re-layouts: 1.15 us -> 3.7 us
    ppermute x10, starting transfers between devices: 38.8 us -> 33.6 us  [send(): return lax.ppermute(value, ALL, pairs)]
    unnamed x10, local copies, waits for them, and re-layouts: 0.03 us -> 1.81 us
    all_to_all x1, starting transfers between devices: 5 us -> 3.7 us  [sum_and_return(): half = lax.all_to_all(spread, PLANE, 0, 0, tiled=True)]
    pallas_call x2, Pallas kernels: 1.65 us -> 2.64 us  [the longest x1 2.47 us: block(): vmem_call(functools.partial(finish_kernel, where_am_i), [shape(2, HALF, D...]
  transfers between devices with their start and end apart: 11 -> 11, of which waited for: 9 -> 6; matrix products, arithmetic and copies ran while one was open for 0% -> 1% of each run, Pallas kernels for 4% -> 5%
where the time goes in v4:
time: 94.5 us; the launch traced here: 94.2 us
  starting transfers between devices  37.3 us (39%)
  blocking collectives  21.9 us (23%)
  waiting for transfers between devices  16.2 us (17%)
  Pallas kernels  13.9 us (15%)
  local copies, waits for them, and re-layouts  3.7 us (4%)
    ppermute x10, starting transfers between devices, send(): return lax.ppermute(value, ALL, pairs)  33.6 us
    all_to_all x1, blocking collectives, sum_and_return(): pieces = lax.all_to_all(chunks, PLANE, 0, 0, tiled=True)  21.9 us
    ppermute x10, waiting for transfers between devices, send(): return lax.ppermute(value, ALL, pairs)  10 us
    pallas_call x1, Pallas kernels, block(): vmem_call(functools.partial(attend_kernel, where_am_i), [shape(STRIP, 128...  6.25 us
    all_to_all x1, waiting for transfers between devices, sum_and_return(): half = lax.all_to_all(spread, PLANE, 0, 0, tiled=True)  6.13 us
    all_to_all x1, starting transfers between devices, sum_and_return(): half = lax.all_to_all(spread, PLANE, 0, 0, tiled=True)  3.7 us
    pallas_call x2, Pallas kernels, unpack(): pl.pallas_call(functools.partial(unpack_kernel, where_am_i, side), out_sh...  2.84 us
    pallas_call x1, Pallas kernels, block(): vmem_call(functools.partial(finish_kernel, where_am_i), [shape(2, HALF, D...  2.47 us
  transfers between devices with their start and end apart: 11, of which 6 were waited for; matrix products, arithmetic and copies ran while one was open for 1% of the time, Pallas kernels for 5%

profile of v4, /device:TPU:1, one launch (start us, length us, event | category | flops | bytes accessed | tf_op | source)
XLA Modules:
  0.0 94.2 jit_solution(14733794734038144050)
XLA Ops:
  0.6 0.0 copy-start.2
  0.6 0.0 copy-start
  0.7 1.2 %slice_bitcast_fusion.2 = (bf16[1,3,48,512]{3,2,1,0:T(8,128)(2,1)S(1)}, bf16[3,48,512]{2,1,0:T(8,128)(2,1)S(1)}, bf16[3,48,512]{2,1,0:T(8,128)(2,1)S(1)}, bf16[1,3,48,512]{3,2,1,0:T(8,128)(2,1)S(1)}) fusion(bf16[6,48,512]{2,1,0:T(8,128)(2,1)} %param.9, bf16[6,48,512]{2,1,0:T(8,128)(2,1)} %param.5), kind=kLoop, calls=%fused_computation.8 | loop fusion | bytes 884736 | tf_op jit(solution)/shard_map/stack | solution.py:352
  1.8 6.0 %collective-permute-start = (bf16[2,144,512]{2,1,0:T(8,128)(2,1)S(1)}, bf16[2,144,512]{2,1,0:T(8,128)(2,1)S(1)}, u32[]{:S(2)}, u32[]{:S(2)}) collective-permute-start(bf16[2,144,512]{2,1,0:T(8,128)(2,1)S(1)} %pad_maximum_fusion), channel_id=1, source_target_pairs={{0,224},{1,225},{2,226},{3,227},{4,228},{5,229},{6,230},{7,231},{8... | collective-permute-start | bytes 884744 | tf_op jit(solution)/shard_map/ppermute | solution.py:323
  7.9 0.0 copy-done.2
  7.9 0.7 slice_bitcast_fusion
  8.6 1.0 %collective-permute-start.1 = (bf16[2,24,512]{2,1,0:T(8,128)(2,1)S(1)}, bf16[2,24,512]{2,1,0:T(8,128)(2,1)S(1)}, u32[]{:S(2)}, u32[]{:S(2)}) collective-permute-start(bf16[2,24,512]{2,1,0:T(8,128)(2,1)S(1)} %pad_maximum_fusion.2), channel_id=1, source_target_pairs={{0,31},{1,0},{2,1},{3,2},{4,3},{5,4},{6,5},{7,6},{8,7},{9,8},{10,9... | collective-permute-start | bytes 147464 | tf_op jit(solution)/shard_map/ppermute | solution.py:323
  9.7 6.6 %collective-permute-start.2 = (bf16[2,24,512]{2,1,0:T(8,128)(2,1)S(1)}, bf16[2,24,512]{2,1,0:T(8,128)(2,1)S(1)}, u32[]{:S(2)}, u32[]{:S(2)}) collective-permute-start(bf16[2,24,512]{2,1,0:T(8,128)(2,1)S(1)} %fusion), channel_id=1, source_target_pairs={{0,255},{1,224},{2,225},{3,226},{4,227},{5,228},{6,229},{7,230},{8... | collective-permute-start | bytes 147464 | tf_op jit(solution)/shard_map/ppermute | solution.py:323
  16.2 0.0 copy-done
  16.2 0.0 copy-start.1
  16.2 1.0 %copy-done.1 = bf16[512,512]{1,0:T(8,128)(2,1)S(1)} copy-done((bf16[512,512]{1,0:T(8,128)(2,1)S(1)}, bf16[512,512]{1,0:T(8,128)(2,1)}, u32[]{:S(2)}) %copy-start.1) | copy-done | bytes 524312
  17.3 0.0 copy-start.3
  17.3 0.0 copy-start.4
  17.3 0.2 shard_map.92
  17.5 0.0 collective-permute-done.1.halo_lon_ref
  17.5 0.0 collective-permute-done.2.halo_cor_ref
  17.5 0.0 collective-permute-done.halo_lat_ref
  17.5 0.8 copy-done.3
  18.2 0.0 copy-done.4
  18.2 6.2 %shard_map.93 = (bf16[4096,128]{1,0:T(8,128)(2,1)S(1)}, bf16[320,512]{1,0:T(8,128)(2,1)S(1)}, bf16[320,512]{1,0:T(8,128)(2,1)S(1)}, bf16[320,512]{1,0:T(8,128)(2...) custom-call(bf16[288,512]{1,0:T(8,128)(2,1)S(1)} %bitcast.18, bf16[288,512]{1,0:T(8,128)(2,1)S(1)} %bitcast.19, ...), custom_call_target="tpu_custom_call" | custom-call | flops 5000000000 | bytes 8000000 | tf_op jit(solution)/shard_map/pallas_call | solution.py:211
  24.5 1.7 %collective-permute-start.4 = (bf16[4096,128]{1,0:T(8,128)(2,1)S(1)}, bf16[4096,128]{1,0:T(8,128)(2,1)S(1)}, u32[]{:S(2)}, u32[]{:S(2)}) collective-permute-start(bf16[4096,128]{1,0:T(8,128)(2,1)S(1)} %get-tuple-element.41), channel_id=1, source_target_pairs={{0,1},{1,0},{2,3},{3,2},{4,5},{5,4},{6,7},{7,6},{8,9},{9,8},{10,11... | collective-permute-start | bytes 3145736 | tf_op jit(solution)/shard_map/ppermute | solution.py:323
  26.2 2.5 %shard_map.94 = (bf16[2,144,512]{2,1,0:T(8,128)(2,1)S(1)}, bf16[2,168,512]{2,1,0:T(8,128)(2,1)S(1)}, bf16[2,24,512]{2,1,0:T(8,128)(2,1)S(1)}, bf16[8,128]{1,0:T(8,128)(2,1)S(1)}, bf16[4096,128]{1,0:T(8,128)(2,1)S(1)}) custom-call(bf16[320,512]{1,0:T(8,128)(2,1)S(1)} %get-tuple-element.33.latent_ref, bf16[320,512]{1,0:T(8,128)(2,1)S(1)} %get-tuple-element.34.cot_ref, ...), custom_call_target="tpu_custom_call" | custom-call | flops 1500000000 | bytes 4000000 | tf_op jit(solution)/shard_map/pallas_call | solution.py:220
  28.6 0.0 collective-permute-done.4.arrived_ref
  28.6 0.2 shard_map.95
  28.9 21.9 %all_to_all.10 = bf16[16,264,128]{2,1,0:T(8,128)(2,1)S(1)} all-to-all(bf16[16,264,128]{2,1,0:T(8,128)(2,1)S(1)} %shard_map.95), channel_id=1, replica_groups=mesh['x'=4,'yh'=2,'yl'=2,'z'=8,'c'=2] {'x','yh','yl'}, dimensions={0} | all-to-all | bytes 2162688 | tf_op jit(solution)/shard_map/all_to_all | solution.py:331
  50.8 0.1 reduce_sum.12
  51.0 0.2 collective-permute-start.5
  51.2 3.0 %collective-permute-done.5 = bf16[264,128]{1,0:T(8,128)(2,1)S(1)} collective-permute-done((bf16[264,128]{1,0:T(8,128)(2,1)S(1)}, bf16[264,128]{1,0:T(8,128)(2,1)S(1)}, u32[]{:S(2)}, u32[]{:S(2)}) %collective-permute-start.5) | collective-permute-done | bytes 67616 | tf_op jit(solution)/shard_map/ppermute | solution.py:323
  54.2 1.7 %collective-permute-start.6 = (bf16[264,128]{1,0:T(8,128)(2,1)S(1)}, bf16[264,128]{1,0:T(8,128)(2,1)S(1)}, u32[]{:S(2)}, u32[]{:S(2)}) collective-permute-start(bf16[264,128]{1,0:T(8,128)(2,1)S(1)} %add_convert_fusion.1), channel_id=1, source_target_pairs={{0,4},{1,5},{2,6},{3,7},{4,0},{5,1},{6,2},{7,3},{8,12},{9,13},{10,... | collective-permute-start | bytes 202760 | tf_op jit(solution)/shard_map/ppermute | solution.py:323
  56.0 1.2 %collective-permute-start.3 = (bf16[2,168,512]{2,1,0:T(8,128)(2,1)S(1)}, bf16[2,168,512]{2,1,0:T(8,128)(2,1)S(1)}, u32[]{:S(2)}, u32[]{:S(2)}) collective-permute-start(bf16[2,168,512]{2,1,0:T(8,128)(2,1)S(1)} %get-tuple-element.39), channel_id=1, source_target_pairs={{0,32},{1,33},{2,34},{3,35},{4,36},{5,37},{6,38},{7,39},{8,40},{9,... | collective-permute-start | bytes 1032200 | tf_op jit(solution)/shard_map/ppermute | solution.py:323
  57.1 1.9 %collective-permute-done.6 = bf16[264,128]{1,0:T(8,128)(2,1)S(1)} collective-permute-done((bf16[264,128]{1,0:T(8,128)(2,1)S(1)}, bf16[264,128]{1,0:T(8,128)(2,1)S(1)}, u32[]{:S(2)}, u32[]{:S(2)}) %collective-permute-start.6) | collective-permute-done | bytes 67616 | tf_op jit(solution)/shard_map/ppermute | solution.py:323
  59.1 3.9 %collective-permute-start.7 = (bf16[264,128]{1,0:T(8,128)(2,1)S(1)}, bf16[264,128]{1,0:T(8,128)(2,1)S(1)}, u32[]{:S(2)}, u32[]{:S(2)}) collective-permute-start(bf16[264,128]{1,0:T(8,128)(2,1)S(1)} %add_convert_fusion.total_ref), channel_id=1, source_target_pairs={{0,12},{1,13},{2,14},{3,15},{4,8},{5,9},{6,10},{7,11},{8,4},{9,5},... | collective-permute-start | bytes 202760 | tf_op jit(solution)/shard_map/ppermute | solution.py:323
  63.0 3.3 %collective-permute-done.3.came_ref = bf16[2,168,512]{2,1,0:T(8,128)(2,1)S(1)} collective-permute-done((bf16[2,168,512]{2,1,0:T(8,128)(2,1)S(1)}, bf16[2,168,512]{2,1,0:T(8,128)(2,1)S(1)}, u32[]{:S(2)}, u32[]{:S(2)}) %collective-permute-start.3) | collective-permute-done | bytes 344096 | tf_op jit(solution)/shard_map/ppermute | solution.py:323
  66.4 0.0 collective-permute-done.7.arrived_ref
  66.4 1.1 %shard_map.96 = (bf16[16,264,128]{2,1,0:T(8,128)(2,1)}, bf16[2,48,512]{2,1,0:T(8,128)(2,1)S(1)}) custom-call(bf16[264,128]{1,0:T(8,128)(2,1)S(1)} %add_convert_fusion.total_ref, bf16[264,128]{1,0:T(8,128)(2,1)S(1)} %collective-permute-done.7.arrived_ref, bf16[2,168,512]{2,1,0:T(8,128)(2,1)S(1)} %collective-permute-done.3.came_ref, ...), custom_call_target="tpu_custom_call" | custom-call | flops 1000000 | bytes 3000000 | tf_op jit(solution)/shard_map/pallas_call | solution.py:336
  67.4 3.7 %all-to-all-start.1 = ((bf16[16,264,128]{2,1,0:T(8,128)(2,1)}), bf16[16,264,128]{2,1,0:T(8,128)(2,1)S(1)}, u32[]{:S(2)}, u32[]{:S(2)}) async-start(bf16[16,264,128]{2,1,0:T(8,128)(2,1)} %get-tuple-element.44), calls=%async_computation.1 | async-start | bytes 2162688 | tf_op jit(solution)/shard_map/all_to_all | solution.py:339
  71.1 5.1 %collective-permute-start.8 = (bf16[2,48,512]{2,1,0:T(8,128)(2,1)S(1)}, bf16[2,48,512]{2,1,0:T(8,128)(2,1)S(1)}, u32[]{:S(2)}, u32[]{:S(2)}) collective-permute-start(bf16[2,48,512]{2,1,0:T(8,128)(2,1)S(1)} %get-tuple-element.45), channel_id=1, source_target_pairs={{0,1},{1,2},{2,3},{3,4},{4,5},{5,6},{6,7},{7,8},{8,9},{9,10},{10,1... | collective-permute-start | bytes 294920 | tf_op jit(solution)/shard_map/ppermute | solution.py:323
  76.2 1.6 %collective-permute-done.8.edge_ref = bf16[2,48,512]{2,1,0:T(8,128)(2,1)S(1)} collective-permute-done((bf16[2,48,512]{2,1,0:T(8,128)(2,1)S(1)}, bf16[2,48,512]{2,1,0:T(8,128)(2,1)S(1)}, u32[]{:S(2)}, u32[]{:S(2)}) %collective-permute-start.8) | collective-permute-done | bytes 98336 | tf_op jit(solution)/shard_map/ppermute | solution.py:323
  77.9 6.1 %all-to-all-done.1.half_ref.refs_0_ = bf16[16,264,128]{2,1,0:T(8,128)(2,1)S(1)} async-done(((bf16[16,264,128]{2,1,0:T(8,128)(2,1)}), bf16[16,264,128]{2,1,0:T(8,128)(2,1)S(1)}, u32[]{:S(2)}, u32[]{:S(2)}) %all-to-all-start.1) | async-done | bytes 1081376 | tf_op jit(solution)/shard_map/all_to_all | solution.py:339
  84.0 6.2 %collective-permute-start.9 = (bf16[16,264,128]{2,1,0:T(8,128)(2,1)S(1)}, bf16[16,264,128]{2,1,0:T(8,128)(2,1)S(1)}, u32[]{:S(2)}, u32[]{:S(2)}) collective-permute-start(bf16[16,264,128]{2,1,0:T(8,128)(2,1)S(1)} %all-to-all-done.1.half_ref.refs_0_), channel_id=1, source_target_pairs={{0,1},{1,0},{2,3},{3,2},{4,5},{5,4},{6,7},{7,6},{8,9},{9,8},{10,11... | collective-permute-start | bytes 3244040 | tf_op jit(solution)/shard_map/ppermute | solution.py:323
  90.2 1.4 %shard_map.98 = (f32[512,1536]{1,0:T(8,128)}, f32[512,512]{1,0:T(8,128)}) custom-call(bf16[16,264,128]{2,1,0:T(8,128)(2,1)S(1)} %all-to-all-done.1.half_ref.refs_0_), custom_call_target="tpu_custom_call" | custom-call | flops 1000000 | bytes 3000000 | tf_op jit(solution)/shard_map/pallas_call | solution.py:286
  91.7 0.9 shard_map.97
  92.5 0.1 collective-permute-done.9.half_ref
  92.6 1.4 %shard_map.99 = (f32[512,1536]{1,0:T(8,128)}, f32[512,512]{1,0:T(8,128)}, f32[1,512]{1,0:T(1,128)}) custom-call(bf16[16,264,128]{2,1,0:T(8,128)(2,1)S(1)} %collective-permute-done.9.half_ref, bf16[16,264,128]{2,1,0:T(8,128)(2,1)S(1)} %all-to-all-done.1.half_ref.refs_0_, ...), custom_call_target="tpu_custom_call", output_to_operand_aliasing={{0}: (2, {}), {1}: (3, {})} | custom-call | flops 1000000 | bytes 3000000 | tf_op jit(solution)/shard_map/pallas_call | solution.py:286
  (5 shorter events, 0.1 us)
Async XLA Ops:
  0.6 7.2 %copy-start.2 = (bf16[6,48,512]{2,1,0:T(8,128)(2,1)S(1)}, bf16[6,48,512]{2,1,0:T(8,128)(2,1)}, u32[]{:S(2)}) copy-start(bf16[6,48,512]{2,1,0:T(8,128)(2,1)} %param.5) | copy-start | bytes 884740
  0.6 15.6 %copy-start = (bf16[512,1536]{1,0:T(8,128)(2,1)S(1)}, bf16[512,1536]{1,0:T(8,128)(2,1)}, u32[]{:S(2)}) copy-start(bf16[512,1536]{1,0:T(8,128)(2,1)} %w_qkv_ref.1) | copy-start | bytes 4718596
  1.8 15.6 %collective-permute-start = (bf16[2,144,512]{2,1,0:T(8,128)(2,1)S(1)}, bf16[2,144,512]{2,1,0:T(8,128)(2,1)S(1)}, u32[]{:S(2)}, u32[]{:S(2)}) collective-permute-start(bf16[2,144,512]{2,1,0:T(8,128)(2,1)S(1)} %pad_maximum_fusion), channel_id=1, source_target_pairs={{0,224},{1,225},{2,226},{3,227},{4,228},{5,229},{6,230},{7,231},{8... | collective-permute-start | bytes 884744 | tf_op jit(solution)/shard_map/ppermute | solution.py:323
  8.6 8.8 %collective-permute-start.1 = (bf16[2,24,512]{2,1,0:T(8,128)(2,1)S(1)}, bf16[2,24,512]{2,1,0:T(8,128)(2,1)S(1)}, u32[]{:S(2)}, u32[]{:S(2)}) collective-permute-start(bf16[2,24,512]{2,1,0:T(8,128)(2,1)S(1)} %pad_maximum_fusion.2), channel_id=1, source_target_pairs={{0,31},{1,0},{2,1},{3,2},{4,3},{5,4},{6,5},{7,6},{8,7},{9,8},{10,9... | collective-permute-start | bytes 147464 | tf_op jit(solution)/shard_map/ppermute | solution.py:323
  9.7 7.8 %collective-permute-start.2 = (bf16[2,24,512]{2,1,0:T(8,128)(2,1)S(1)}, bf16[2,24,512]{2,1,0:T(8,128)(2,1)S(1)}, u32[]{:S(2)}, u32[]{:S(2)}) collective-permute-start(bf16[2,24,512]{2,1,0:T(8,128)(2,1)S(1)} %fusion), channel_id=1, source_target_pairs={{0,255},{1,224},{2,225},{3,226},{4,227},{5,228},{6,229},{7,230},{8... | collective-permute-start | bytes 147464 | tf_op jit(solution)/shard_map/ppermute | solution.py:323
  16.2 1.0 %copy-start.1 = (bf16[512,512]{1,0:T(8,128)(2,1)S(1)}, bf16[512,512]{1,0:T(8,128)(2,1)}, u32[]{:S(2)}) copy-start(bf16[512,512]{1,0:T(8,128)(2,1)} %w_out_ref.1) | copy-start | bytes 1572868
  17.3 1.0 %copy-start.3 = (bf16[6,48,512]{2,1,0:T(8,128)(2,1)S(1)}, bf16[6,48,512]{2,1,0:T(8,128)(2,1)}, u32[]{:S(2)}) copy-start(bf16[6,48,512]{2,1,0:T(8,128)(2,1)} %param.9) | copy-start | bytes 884740
  17.3 1.0 %copy-start.4 = (f32[512]{0:T(512)S(1)}, f32[512]{0:T(512)}, u32[]{:S(2)}) copy-start(f32[512]{0:T(512)} %param.6) | copy-start | bytes 6148
  24.5 4.1 %collective-permute-start.4 = (bf16[4096,128]{1,0:T(8,128)(2,1)S(1)}, bf16[4096,128]{1,0:T(8,128)(2,1)S(1)}, u32[]{:S(2)}, u32[]{:S(2)}) collective-permute-start(bf16[4096,128]{1,0:T(8,128)(2,1)S(1)} %get-tuple-element.41), channel_id=1, source_target_pairs={{0,1},{1,0},{2,3},{3,2},{4,5},{5,4},{6,7},{7,6},{8,9},{9,8},{10,11... | collective-permute-start | bytes 3145736 | tf_op jit(solution)/shard_map/ppermute | solution.py:323
  51.0 3.2 %collective-permute-start.5 = (bf16[264,128]{1,0:T(8,128)(2,1)S(1)}, bf16[264,128]{1,0:T(8,128)(2,1)S(1)}, u32[]{:S(2)}, u32[]{:S(2)}) collective-permute-start(bf16[264,128]{1,0:T(8,128)(2,1)S(1)} %reduce_sum.12), channel_id=1, source_target_pairs={{0,2},{1,3},{2,0},{3,1},{4,6},{5,7},{6,4},{7,5},{8,10},{9,11},{10,... | collective-permute-start | bytes 202760 | tf_op jit(solution)/shard_map/ppermute | solution.py:323
  54.2 4.8 %collective-permute-start.6 = (bf16[264,128]{1,0:T(8,128)(2,1)S(1)}, bf16[264,128]{1,0:T(8,128)(2,1)S(1)}, u32[]{:S(2)}, u32[]{:S(2)}) collective-permute-start(bf16[264,128]{1,0:T(8,128)(2,1)S(1)} %add_convert_fusion.1), channel_id=1, source_target_pairs={{0,4},{1,5},{2,6},{3,7},{4,0},{5,1},{6,2},{7,3},{8,12},{9,13},{10,... | collective-permute-start | bytes 202760 | tf_op jit(solution)/shard_map/ppermute | solution.py:323
  56.0 10.4 %collective-permute-start.3 = (bf16[2,168,512]{2,1,0:T(8,128)(2,1)S(1)}, bf16[2,168,512]{2,1,0:T(8,128)(2,1)S(1)}, u32[]{:S(2)}, u32[]{:S(2)}) collective-permute-start(bf16[2,168,512]{2,1,0:T(8,128)(2,1)S(1)} %get-tuple-element.39), channel_id=1, source_target_pairs={{0,32},{1,33},{2,34},{3,35},{4,36},{5,37},{6,38},{7,39},{8,40},{9,... | collective-permute-start | bytes 1032200 | tf_op jit(solution)/shard_map/ppermute | solution.py:323
  59.1 7.3 %collective-permute-start.7 = (bf16[264,128]{1,0:T(8,128)(2,1)S(1)}, bf16[264,128]{1,0:T(8,128)(2,1)S(1)}, u32[]{:S(2)}, u32[]{:S(2)}) collective-permute-start(bf16[264,128]{1,0:T(8,128)(2,1)S(1)} %add_convert_fusion.total_ref), channel_id=1, source_target_pairs={{0,12},{1,13},{2,14},{3,15},{4,8},{5,9},{6,10},{7,11},{8,4},{9,5},... | collective-permute-start | bytes 202760 | tf_op jit(solution)/shard_map/ppermute | solution.py:323
  67.4 16.6 %all-to-all-start.1 = ((bf16[16,264,128]{2,1,0:T(8,128)(2,1)}), bf16[16,264,128]{2,1,0:T(8,128)(2,1)S(1)}, u32[]{:S(2)}, u32[]{:S(2)}) async-start(bf16[16,264,128]{2,1,0:T(8,128)(2,1)} %get-tuple-element.44), calls=%async_computation.1 | async-start | bytes 2162688 | tf_op jit(solution)/shard_map/all_to_all | solution.py:339
  71.1 6.7 %collective-permute-start.8 = (bf16[2,48,512]{2,1,0:T(8,128)(2,1)S(1)}, bf16[2,48,512]{2,1,0:T(8,128)(2,1)S(1)}, u32[]{:S(2)}, u32[]{:S(2)}) collective-permute-start(bf16[2,48,512]{2,1,0:T(8,128)(2,1)S(1)} %get-tuple-element.45), channel_id=1, source_target_pairs={{0,1},{1,2},{2,3},{3,4},{4,5},{5,6},{6,7},{7,8},{8,9},{9,10},{10,1... | collective-permute-start | bytes 294920 | tf_op jit(solution)/shard_map/ppermute | solution.py:323
  84.0 8.6 %collective-permute-start.9 = (bf16[16,264,128]{2,1,0:T(8,128)(2,1)S(1)}, bf16[16,264,128]{2,1,0:T(8,128)(2,1)S(1)}, u32[]{:S(2)}, u32[]{:S(2)}) collective-permute-start(bf16[16,264,128]{2,1,0:T(8,128)(2,1)S(1)} %all-to-all-done.1.half_ref.refs_0_), channel_id=1, source_target_pairs={{0,1},{1,0},{2,3},{3,2},{4,5},{5,4},{6,7},{7,6},{8,9},{9,8},{10,11... | collective-permute-start | bytes 3244040 | tf_op jit(solution)/shard_map/ppermute | solution.py:323

commit v5 on v4

--- a/solution.py
+++ b/solution.py
@@ -7,10 +7,10 @@
 from jax.experimental.pallas import tpu as pltpu
 from jax.sharding import Mesh, PartitionSpec as P
 
-ALL = ("x", "yh", "yl", "z", "c")
-LAT = ("x", "yh")
-LON = ("yl", "z", "c")
-PLANE = ("x", "yh", "yl")
+ALL = ("xh", "xl", "yh", "yl", "zh", "zm", "zl", "c")
+LAT = ALL[:3]
+LON = ALL[3:]
+BOX = ("xl", "yh", "yl", "zl")
 HEADS = 16
 HS = 32
 WL = 6
@@ -46,6 +46,14 @@
     return centred * recip_std, recip_std
 
 
+def edges_kernel(rows_ref, edge_ref, to_cor_ref, to_lon_ref):
+    for k in range(2):
+        for r in range(3):
+            at = slice(r * EDGE, (r + 1) * EDGE)
+            to_cor_ref[k, at] = rows_ref[k, r, :EDGE]
+            to_lon_ref[k, at] = edge_ref[k, r, :EDGE]
+
+
 def prepare_kernel(w_qkv_ref, w_out_ref, picks_ref, w_qkv_s, w_out_s):
     w_qkv_s[...] = w_qkv_ref[...]
     w_out_s[...] = w_out_ref[...]
@@ -126,25 +134,33 @@
     def collect(rows):
         return jnp.sum(rows.reshape(GROUP, ROWS, SPAN) * own_head, axis=0).astype(bf16)
 
-    for w in range(WINDOWS):
-        for g in range(HEADS // GROUP):
-            rows = slice(w * ROWS, (w + 1) * ROWS)
-            at = [slice(b * D + g * SPAN, b * D + (g + 1) * SPAN) for b in range(3)]
-            keys = packed_s[rows, at[1]]
-            values = packed_s[rows, at[2]]
-            queries = spread(packed_s[rows, at[0]])
-            d_context = spread(dctx_s[rows, at[0]])
-            scores = dot(keys, queries, NT) * (scaling * 1.4426950408889634) + bias
-            expo = jnp.exp2(scores - jnp.max(scores, axis=0, keepdims=True))
-            probs = expo * (1.0 / jnp.sum(expo, axis=0, keepdims=True))
-            weights = probs.astype(bf16)
-            d_weights = dot(values, d_context, NT)
-            mean_d = jnp.sum(d_weights * probs, axis=0, keepdims=True)
-            d_scaled = ((probs * scaling) * (d_weights - mean_d)).astype(bf16)
-            ctx_s[rows, at[0]] = collect(dot(weights, values, TN))
-            dpacked_s[rows, at[2]] = dot(weights, d_context).astype(bf16)
-            dpacked_s[rows, at[0]] = collect(dot(d_scaled, keys, TN))
-            dpacked_s[rows, at[1]] = dot(d_scaled, queries).astype(bf16)
+    def begin(w, g):
+        rows = slice(w * ROWS, (w + 1) * ROWS)
+        at = [slice(b * D + g * SPAN, b * D + (g + 1) * SPAN) for b in range(3)]
+        keys = packed_s[rows, at[1]]
+        values = packed_s[rows, at[2]]
+        queries = spread(packed_s[rows, at[0]])
+        d_context = spread(dctx_s[rows, at[0]])
+        return rows, at, keys, values, queries, d_context, dot(keys, queries, NT), dot(values, d_context, NT)
+
+    def end(rows, at, keys, values, queries, d_context, scores, d_weights):
+        scores = scores * (scaling * 1.4426950408889634) + bias
+        expo = jnp.exp2(scores - jnp.max(scores, axis=0, keepdims=True))
+        probs = expo * (1.0 / jnp.sum(expo, axis=0, keepdims=True))
+        weights = probs.astype(bf16)
+        mean_d = jnp.sum(d_weights * probs, axis=0, keepdims=True)
+        d_scaled = ((probs * scaling) * (d_weights - mean_d)).astype(bf16)
+        ctx_s[rows, at[0]] = collect(dot(weights, values, TN))
+        dpacked_s[rows, at[2]] = dot(weights, d_context).astype(bf16)
+        dpacked_s[rows, at[0]] = collect(dot(d_scaled, keys, TN))
+        dpacked_s[rows, at[1]] = dot(d_scaled, queries).astype(bf16)
+
+    todo = [(w, g) for w in range(WINDOWS) for g in range(HEADS // GROUP)]
+    begun = begin(*todo[0])
+    for k in range(1, len(todo) + 1):
+        later = begin(*todo[k]) if k < len(todo) else None
+        end(*begun)
+        begun = later
 
     pl.when(core == 1)(lambda: weight_grads(0, scaled_s, ctx_s, cot_s, dpacked_s, other_ref))
     pl.when(core == 0)(lambda: weight_grads(1, scaled_s, ctx_s, cot_s, dpacked_s, other_ref))
@@ -184,7 +200,12 @@
 
 
 def here():
-    return jnp.logical_and(lax.axis_index("x") == 3, lax.axis_index("yh") == 1), lax.axis_index("c")
+    last_lat = lax.axis_index("xh") + lax.axis_index("xl") + lax.axis_index("yh") == 3
+    return last_lat, lax.axis_index("c")
+
+
+def moved_chunk(k):
+    return lax.rem(k + 8 * lax.axis_index("xh"), 16)
 
 
 def vmem_call(kernel, out_shapes, scratch, flops, moved, count, mebibytes=12):
@@ -228,14 +249,12 @@
 def add_kernel(mine_ref, arrived_ref, gain_ref, chunks_ref):
     for k in range(16):
         at = slice(k * CHUNK, (k + 1) * CHUNK)
-        chunks_ref[k, :CHUNK] = (mine_ref[at, :].astype(f32) + arrived_ref[at, :].astype(f32)).astype(bf16)
-        chunks_ref[k, CHUNK:] = gain_ref[...]
-
-
-def spread_kernel(total_ref, arrived_ref, came_ref, back_lon_ref, spread_ref, edge_ref):
-    total = (total_ref[...].astype(f32) + arrived_ref[...].astype(f32)).astype(bf16)
-    for k in range(16):
-        spread_ref[k] = total
+        to = moved_chunk(k)
+        chunks_ref[to, :CHUNK] = (mine_ref[at, :].astype(f32) + arrived_ref[at, :].astype(f32)).astype(bf16)
+        chunks_ref[to, CHUNK:] = gain_ref[...]
+
+
+def edge_kernel(came_ref, back_lon_ref, edge_ref):
     for k in range(2):
         edge_ref[k, :EDGES] = back_lon_ref[k]
         edge_ref[k, EDGES:] = came_ref[k, HALF:]
@@ -253,7 +272,7 @@
             if start:
                 for k in range(4 * block, 4 * block + 4):
                     at = slice(k // 2 * 128, (k // 2 + 1) * 128)
-                    wide_s[k % 2 * CHUNK : (k % 2 + 1) * CHUNK, at] = half_ref[k, :CHUNK].astype(f32)
+                    wide_s[k % 2 * CHUNK : (k % 2 + 1) * CHUNK, at] = half_ref[moved_chunk(k), :CHUNK].astype(f32)
 
             def copy(ref, first):
                 to = ref.at[:, first : first + 256]
@@ -268,7 +287,8 @@
 
     if side:
         own_ref, gain_ref, gain_s, gain_sem = refs[0], refs[5], *refs[6:8]
-        gain = half_ref[0, CHUNK:].astype(f32) + own_ref[0, CHUNK:].astype(f32)
+        at = moved_chunk(0)
+        gain = half_ref[at, CHUNK:].astype(f32) + own_ref[at, CHUNK:].astype(f32)
         for k in range(4):
             gain_s[:, k * 128 : (k + 1) * 128] = gain[k : k + 1, :]
         move = pltpu.make_async_copy(gain_s, gain_ref, gain_sem)
@@ -328,22 +348,21 @@
     chunks = vmem_call(
         add_kernel, [shape(16, SUMMED, 128)], [], 1_000_000, 4_000_000, 3
     )(mine, arrived, gain_rows)[0]
-    pieces = lax.all_to_all(chunks, PLANE, 0, 0, tiled=True)
+    pieces = lax.all_to_all(chunks, BOX, 0, 0, tiled=True)
     total = jnp.sum(pieces.astype(f32), axis=0).astype(bf16)
-    for bits in (2, 4):
+    for bits in (192, 4, 12):
         total = (total.astype(f32) + send(total, swapped(bits)).astype(f32)).astype(bf16)
     came = send(back, shifted(1, 0))
-    spread, edge = vmem_call(
-        spread_kernel, [shape(16, SUMMED, 128), shape(2, 2 * EDGES, D)], [], 1_000_000, 3_000_000, 4
-    )(total, send(total, swapped(12)), came, back_lon)
-    half = lax.all_to_all(spread, PLANE, 0, 0, tiled=True)
+    edge = vmem_call(edge_kernel, [shape(2, 2 * EDGES, D)], [], 1_000_000, 1_000_000, 2)(came, back_lon)[0]
+    total, edge = lax.optimization_barrier((total, edge))
+    half = lax.all_to_all(jnp.broadcast_to(total, (16, SUMMED, 128)), BOX, 0, 0, tiled=True)
     edge = send(edge, shifted(0, 1))
-    half, edge = lax.optimization_barrier((half, edge))
-    arrived = send(half, swapped(1))
-    parts = unpack(here, 0, half)
     mixed, d_latent = vmem_call(
         place_kernel, [shape(2 * HALF, D), shape(2 * HALF, D)], [], 1_000_000, 2_000_000, 3
     )(own, came, edge)
+    half, mixed, d_latent = lax.optimization_barrier((half, mixed, d_latent))
+    arrived = send(half, swapped(1))
+    parts = unpack(here, 0, half)
     grad_qkv, grad_out, grad_gain = unpack(here, 1, arrived, half, *parts)
     return mixed.reshape(*TILE, D), d_latent.reshape(*TILE, D), grad_qkv, grad_out, grad_gain.reshape(D)
 
@@ -351,9 +370,12 @@
 def local(latent, norm_gain, w_qkv, w_out, cotangent):
     both = jnp.stack([latent[:3], cotangent[:3]])
     halo_lat = send(both.reshape(2, HALF, D), shifted(-1, 0))
-    halo_cor = send(both[:, :, :EDGE].reshape(2, EDGES, D), shifted(-1, -1))
-    edge = jnp.stack([latent[3:, :EDGE], cotangent[3:, :EDGE]])
-    halo_lon = send(edge.reshape(2, EDGES, D), shifted(0, -1))
+    edge = jnp.stack([latent[3:, :16], cotangent[3:, :16]])
+    to_cor, to_lon = vmem_call(
+        edges_kernel, [shape(2, EDGES, D), shape(2, EDGES, D)], [], 1_000_000, 500_000, 2
+    )(both, edge)
+    halo_cor = send(to_cor, shifted(-1, -1))
+    halo_lon = send(to_lon, shifted(0, -1))
     return sum_and_return(*block(
         here, latent.reshape(-1, D), cotangent.reshape(-1, D), halo_lat, halo_lon, halo_cor,
         norm_gain.reshape(1, D), w_qkv, w_out,
@@ -361,7 +383,7 @@
 
 
 def solution(mesh):
-    fine = Mesh(mesh.devices.reshape(4, 2, 2, 8, 2), ALL)
+    fine = Mesh(mesh.devices.reshape((2,) * 8), ALL)
     in_specs = (P(LAT, LON, None), P(), P(), P(), P(LAT, LON, None))
     out_specs = (P(LAT, LON, None), P(LAT, LON, None), P(), P(), P())
     return jax.shard_map(local, mesh=fine, in_specs=in_specs, out_specs=out_specs, check_vma=False)

time: 94.5 us -> 91.7 us (0.970)
  blocking collectives: 21.9 us -> 19 us
  waiting for transfers between devices: 16.2 us -> 18.5 us
  Pallas kernels: 13.9 us -> 12.1 us
  local copies, waits for them, and re-layouts: 3.7 us -> 2.26 us
  starting transfers between devices: 37.3 us -> 38.4 us
    ppermute x10, waiting for transfers between devices: 10 us -> 13.9 us  [send(): return lax.ppermute(value, ALL, pairs)]
    all_to_all x1, blocking collectives: 21.9 us -> 19 us  [sum_and_return(): pieces = lax.all_to_all(chunks, BOX, 0, 0, tiled=True)]
    unnamed x10, local copies, waits for them, and re-layouts: 1.81 us -> 0.03 us
    all_to_all x1, waiting for transfers between devices: 6.13 us -> 4.64 us  [sum_and_return(): lax.all_to_all(jnp.broadcast_to(total, (16, SUMMED, 128)), BOX, 0, 0, til...]
    broadcast_in_dim x0 -> x1, local copies, waits for them, and re-layouts: none -> 1.12 us  [sum_and_return(): jnp.broadcast_to(total, (16, SUMMED, 128))]
    ppermute x10, starting transfers between devices: 33.6 us -> 34.7 us  [send(): return lax.ppermute(value, ALL, pairs)]
    pallas_call x1 -> x2, Pallas kernels: 1.06 us -> 0.02 us  [the longest x1 0.01 us: local(): vmem_call(edges_kernel, [shape(2, EDGES, D), shape(2, EDGES, D)], [], 100...]
  transfers between devices with their start and end apart: 11 -> 11, of which waited for: 6 -> 7; matrix products, arithmetic and copies ran while one was open for 1% -> 0% of each run, Pallas kernels for 5% -> 5%
where the time goes in v5:
time: 91.7 us; the launch traced here: 91.5 us
  starting transfers between devices  38.4 us (42%)
  blocking collectives  19 us (21%)
  waiting for transfers between devices  18.5 us (20%)
  Pallas kernels  12.1 us (13%)
  local copies, waits for them, and re-layouts  2.26 us (2%)
  between operations  0.97 us (1%)
    ppermute x10, starting transfers between devices, send(): return lax.ppermute(value, ALL, pairs)  34.7 us
    all_to_all x1, blocking collectives, sum_and_return(): pieces = lax.all_to_all(chunks, BOX, 0, 0, tiled=True)  19 us
    ppermute x10, waiting for transfers between devices, send(): return lax.ppermute(value, ALL, pairs)  13.9 us
    pallas_call x1, Pallas kernels, block(): vmem_call(functools.partial(attend_kernel, where_am_i), [shape(STRIP, 128...  5.67 us
    all_to_all x1, waiting for transfers between devices, sum_and_return(): lax.all_to_all(jnp.broadcast_to(total, (16, SUMMED, 128)), BOX, 0, 0, til...  4.64 us
    all_to_all x1, starting transfers between devices, sum_and_return(): lax.all_to_all(jnp.broadcast_to(total, (16, SUMMED, 128)), BOX, 0, 0, til...  3.7 us
    pallas_call x2, Pallas kernels, unpack(): pl.pallas_call(functools.partial(unpack_kernel, where_am_i, side), out_sh...  2.84 us
    pallas_call x1, Pallas kernels, block(): vmem_call(functools.partial(finish_kernel, where_am_i), [shape(2, HALF, D...  2.29 us
  transfers between devices with their start and end apart: 11, of which 7 were waited for; matrix products, arithmetic and copies ran while one was open for 0% of the time, Pallas kernels for 5%

profile of v5, /device:TPU:1, one launch (start us, length us, event | category | flops | bytes accessed | tf_op | source)
XLA Modules:
  0.0 91.5 jit_solution(4023462487366154429)
XLA Ops:
  0.6 0.0 copy-start.3
  0.6 0.0 copy-start.2
  0.7 0.0 copy-start.1
  0.7 1.1 %slice_bitcast_fusion.2 = (bf16[1,3,48,512]{3,2,1,0:T(8,128)(2,1)S(1)}, bf16[3,48,512]{2,1,0:T(8,128)(2,1)S(1)}, bf16[3,48,512]{2,1,0:T(8,128)(2,1)S(1)}, bf16[1,3,48,512]{3,2,1,0:T(8,128)(2,1)S(1)}) fusion(bf16[6,48,512]{2,1,0:T(8,128)(2,1)} %param.9, bf16[6,48,512]{2,1,0:T(8,128)(2,1)} %param.5), kind=kLoop, calls=%fused_computation.8 | loop fusion | bytes 884736 | tf_op jit(solution)/shard_map/stack | solution.py:371
  1.8 0.0 copy-start
  1.8 6.0 %collective-permute-start = (bf16[2,144,512]{2,1,0:T(8,128)(2,1)S(1)}, bf16[2,144,512]{2,1,0:T(8,128)(2,1)S(1)}, u32[]{:S(2)}, u32[]{:S(2)}) collective-permute-start(bf16[2,144,512]{2,1,0:T(8,128)(2,1)S(1)} %pad_maximum_fusion), channel_id=1, source_target_pairs={{0,224},{1,225},{2,226},{3,227},{4,228},{5,229},{6,230},{7,231},{8... | collective-permute-start | bytes 884744 | tf_op jit(solution)/shard_map/ppermute | solution.py:343
  7.8 0.0 copy-done.3
  7.8 0.0 copy-done.2
  7.9 0.0 copy-start.4
  8.0 1.0 %collective-permute-start.1 = (bf16[2,24,512]{2,1,0:T(8,128)(2,1)S(1)}, bf16[2,24,512]{2,1,0:T(8,128)(2,1)S(1)}, u32[]{:S(2)}, u32[]{:S(2)}) collective-permute-start(bf16[2,24,512]{2,1,0:T(8,128)(2,1)S(1)} %get-tuple-element.33), channel_id=1, source_target_pairs={{0,31},{1,0},{2,1},{3,2},{4,3},{5,4},{6,5},{7,6},{8,7},{9,8},{10,9... | collective-permute-start | bytes 147464 | tf_op jit(solution)/shard_map/ppermute | solution.py:343
  9.0 6.6 %collective-permute-start.2 = (bf16[2,24,512]{2,1,0:T(8,128)(2,1)S(1)}, bf16[2,24,512]{2,1,0:T(8,128)(2,1)S(1)}, u32[]{:S(2)}, u32[]{:S(2)}) collective-permute-start(bf16[2,24,512]{2,1,0:T(8,128)(2,1)S(1)} %get-tuple-element.34), channel_id=1, source_target_pairs={{0,255},{1,224},{2,225},{3,226},{4,227},{5,228},{6,229},{7,230},{8... | collective-permute-start | bytes 147464 | tf_op jit(solution)/shard_map/ppermute | solution.py:343
  15.6 0.0 copy-done.1
  15.6 0.0 copy-done
  15.6 0.2 shard_map.93
  15.7 0.0 collective-permute-done.1.halo_lon_ref
  15.7 1.0 %collective-permute-done.2.halo_cor_ref = bf16[2,24,512]{2,1,0:T(8,128)(2,1)S(1)} collective-permute-done((bf16[2,24,512]{2,1,0:T(8,128)(2,1)S(1)}, bf16[2,24,512]{2,1,0:T(8,128)(2,1)S(1)}, u32[]{:S(2)}, u32[]{:S(2)}) %collective-permute-start.2) | collective-permute-done | bytes 49184 | tf_op jit(solution)/shard_map/ppermute | solution.py:343
  16.7 0.0 collective-permute-done.halo_lat_ref
  16.7 0.0 copy-done.4
  16.7 5.7 %shard_map.94 = (bf16[4096,128]{1,0:T(8,128)(2,1)S(1)}, bf16[320,512]{1,0:T(8,128)(2,1)S(1)}, bf16[320,512]{1,0:T(8,128)(2,1)S(1)}, bf16[320,512]{1,0:T(8,128)(2...) custom-call(bf16[288,512]{1,0:T(8,128)(2,1)S(1)} %bitcast.16, bf16[288,512]{1,0:T(8,128)(2,1)S(1)} %bitcast.17, ...), custom_call_target="tpu_custom_call" | custom-call | flops 5000000000 | bytes 8000000 | tf_op jit(solution)/shard_map/pallas_call | solution.py:232
  22.4 2.5 %collective-permute-start.3 = (bf16[4096,128]{1,0:T(8,128)(2,1)S(1)}, bf16[4096,128]{1,0:T(8,128)(2,1)S(1)}, u32[]{:S(2)}, u32[]{:S(2)}) collective-permute-start(bf16[4096,128]{1,0:T(8,128)(2,1)S(1)} %get-tuple-element.44), channel_id=1, source_target_pairs={{0,1},{1,0},{2,3},{3,2},{4,5},{5,4},{6,7},{7,6},{8,9},{9,8},{10,11... | collective-permute-start | bytes 3145736 | tf_op jit(solution)/shard_map/ppermute | solution.py:343
  24.9 2.3 %shard_map.95 = (bf16[2,144,512]{2,1,0:T(8,128)(2,1)S(1)}, bf16[2,168,512]{2,1,0:T(8,128)(2,1)S(1)}, bf16[2,24,512]{2,1,0:T(8,128)(2,1)S(1)}, bf16[8,128]{1,0:T(8,128)(2,1)S(1)}, bf16[4096,128]{1,0:T(8,128)(2,1)S(1)}) custom-call(bf16[320,512]{1,0:T(8,128)(2,1)S(1)} %get-tuple-element.38.latent_ref, bf16[320,512]{1,0:T(8,128)(2,1)S(1)} %get-tuple-element.39.cot_ref, ...), custom_call_target="tpu_custom_call" | custom-call | flops 1500000000 | bytes 4000000 | tf_op jit(solution)/shard_map/pallas_call | solution.py:241
  27.2 0.0 collective-permute-done.3.arrived_ref
  27.2 0.2 shard_map.96
  27.5 19.0 %all_to_all.10 = bf16[16,264,128]{2,1,0:T(8,128)(2,1)S(1)} all-to-all(bf16[16,264,128]{2,1,0:T(8,128)(2,1)S(1)} %shard_map.96), channel_id=1, replica_groups=mesh['xh'=2,'xl'=2,'yh'=2,'yl'=2,'zh'=2,'zm'=2,'zl'=2,'c'=2] {'xl','yh',..., dimensions={0} | all-to-all | bytes 2162688 | tf_op jit(solution)/shard_map/all_to_all | solution.py:351
  46.4 0.1 reduce_sum.12
  46.6 3.3 %collective-permute-start.4 = (bf16[264,128]{1,0:T(8,128)(2,1)S(1)}, bf16[264,128]{1,0:T(8,128)(2,1)S(1)}, u32[]{:S(2)}, u32[]{:S(2)}) collective-permute-start(bf16[264,128]{1,0:T(8,128)(2,1)S(1)} %reduce_sum.12), channel_id=1, source_target_pairs={{0,192},{1,193},{2,194},{3,195},{4,196},{5,197},{6,198},{7,199},{8... | collective-permute-start | bytes 202760 | tf_op jit(solution)/shard_map/ppermute | solution.py:343
  49.9 1.7 %collective-permute-done.4 = bf16[264,128]{1,0:T(8,128)(2,1)S(1)} collective-permute-done((bf16[264,128]{1,0:T(8,128)(2,1)S(1)}, bf16[264,128]{1,0:T(8,128)(2,1)S(1)}, u32[]{:S(2)}, u32[]{:S(2)}) %collective-permute-start.4) | collective-permute-done | bytes 67616 | tf_op jit(solution)/shard_map/ppermute | solution.py:343
  51.6 3.1 %collective-permute-start.5 = (bf16[264,128]{1,0:T(8,128)(2,1)S(1)}, bf16[264,128]{1,0:T(8,128)(2,1)S(1)}, u32[]{:S(2)}, u32[]{:S(2)}) collective-permute-start(bf16[264,128]{1,0:T(8,128)(2,1)S(1)} %add_convert_fusion.2), channel_id=1, source_target_pairs={{0,4},{1,5},{2,6},{3,7},{4,0},{5,1},{6,2},{7,3},{8,12},{9,13},{10,... | collective-permute-start | bytes 202760 | tf_op jit(solution)/shard_map/ppermute | solution.py:343
  54.6 1.0 %collective-permute-start.7 = (bf16[2,168,512]{2,1,0:T(8,128)(2,1)S(1)}, bf16[2,168,512]{2,1,0:T(8,128)(2,1)S(1)}, u32[]{:S(2)}, u32[]{:S(2)}) collective-permute-start(bf16[2,168,512]{2,1,0:T(8,128)(2,1)S(1)} %get-tuple-element.46), channel_id=1, source_target_pairs={{0,32},{1,33},{2,34},{3,35},{4,36},{5,37},{6,38},{7,39},{8,40},{9,... | collective-permute-start | bytes 1032200 | tf_op jit(solution)/shard_map/ppermute | solution.py:343
  55.7 1.4 %collective-permute-done.5 = bf16[264,128]{1,0:T(8,128)(2,1)S(1)} collective-permute-done((bf16[264,128]{1,0:T(8,128)(2,1)S(1)}, bf16[264,128]{1,0:T(8,128)(2,1)S(1)}, u32[]{:S(2)}, u32[]{:S(2)}) %collective-permute-start.5) | collective-permute-done | bytes 67616 | tf_op jit(solution)/shard_map/ppermute | solution.py:343
  57.1 4.5 %collective-permute-start.6 = (bf16[264,128]{1,0:T(8,128)(2,1)S(1)}, bf16[264,128]{1,0:T(8,128)(2,1)S(1)}, u32[]{:S(2)}, u32[]{:S(2)}) collective-permute-start(bf16[264,128]{1,0:T(8,128)(2,1)S(1)} %add_convert_fusion.1), channel_id=1, source_target_pairs={{0,12},{1,13},{2,14},{3,15},{4,8},{5,9},{6,10},{7,11},{8,4},{9,5},... | collective-permute-start | bytes 202760 | tf_op jit(solution)/shard_map/ppermute | solution.py:343
  61.5 3.5 %collective-permute-done.7.came_ref = bf16[2,168,512]{2,1,0:T(8,128)(2,1)S(1)} collective-permute-done((bf16[2,168,512]{2,1,0:T(8,128)(2,1)S(1)}, bf16[2,168,512]{2,1,0:T(8,128)(2,1)S(1)}, u32[]{:S(2)}, u32[]{:S(2)}) %collective-permute-start.7) | collective-permute-done | bytes 344096 | tf_op jit(solution)/shard_map/ppermute | solution.py:343
  65.0 0.0 collective-permute-done.6
  65.1 1.1 %broadcast_in_dim.3 = bf16[16,264,128]{2,1,0:T(8,128)(2,1)} broadcast(bf16[264,128]{1,0:T(8,128)(2,1)S(1)} %add_convert_fusion), dimensions={1,2} | broadcast | bytes 1148928 | tf_op jit(solution)/shard_map/broadcast_in_dim | solution.py:358
  66.2 3.7 %all-to-all-start.1 = ((bf16[16,264,128]{2,1,0:T(8,128)(2,1)}), bf16[16,264,128]{2,1,0:T(8,128)(2,1)S(1)}, u32[]{:S(2)}, u32[]{:S(2)}) async-start(bf16[16,264,128]{2,1,0:T(8,128)(2,1)} %broadcast_in_dim.3), calls=%async_computation.1 | async-start | bytes 2162688 | tf_op jit(solution)/shard_map/all_to_all | solution.py:358
  69.9 5.1 %collective-permute-start.8 = (bf16[2,48,512]{2,1,0:T(8,128)(2,1)S(1)}, bf16[2,48,512]{2,1,0:T(8,128)(2,1)S(1)}, u32[]{:S(2)}, u32[]{:S(2)}) collective-permute-start(bf16[2,48,512]{2,1,0:T(8,128)(2,1)S(1)} %shard_map.97), channel_id=1, source_target_pairs={{0,1},{1,2},{2,3},{3,4},{4,5},{5,6},{6,7},{7,8},{8,9},{9,10},{10,1... | collective-permute-start | bytes 294920 | tf_op jit(solution)/shard_map/ppermute | solution.py:343
  75.0 5.4 %collective-permute-done.8.edge_ref = bf16[2,48,512]{2,1,0:T(8,128)(2,1)S(1)} collective-permute-done((bf16[2,48,512]{2,1,0:T(8,128)(2,1)S(1)}, bf16[2,48,512]{2,1,0:T(8,128)(2,1)S(1)}, u32[]{:S(2)}, u32[]{:S(2)}) %collective-permute-start.8) | collective-permute-done | bytes 98336 | tf_op jit(solution)/shard_map/ppermute | solution.py:343
  80.4 0.9 shard_map.98
  81.3 4.6 %all-to-all-done.1.half_ref.refs_0_ = bf16[16,264,128]{2,1,0:T(8,128)(2,1)S(1)} async-done(((bf16[16,264,128]{2,1,0:T(8,128)(2,1)}), bf16[16,264,128]{2,1,0:T(8,128)(2,1)S(1)}, u32[]{:S(2)}, u32[]{:S(2)}) %all-to-all-start.1) | async-done | bytes 1081376 | tf_op jit(solution)/shard_map/all_to_all | solution.py:358
  85.9 1.7 %collective-permute-start.9 = (bf16[16,264,128]{2,1,0:T(8,128)(2,1)S(1)}, bf16[16,264,128]{2,1,0:T(8,128)(2,1)S(1)}, u32[]{:S(2)}, u32[]{:S(2)}) collective-permute-start(bf16[16,264,128]{2,1,0:T(8,128)(2,1)S(1)} %all-to-all-done.1.half_ref.refs_0_), channel_id=1, source_target_pairs={{0,1},{1,0},{2,3},{3,2},{4,5},{5,4},{6,7},{7,6},{8,9},{9,8},{10,11... | collective-permute-start | bytes 3244040 | tf_op jit(solution)/shard_map/ppermute | solution.py:343
  87.6 1.4 %shard_map.99 = (f32[512,1536]{1,0:T(8,128)}, f32[512,512]{1,0:T(8,128)}) custom-call(bf16[16,264,128]{2,1,0:T(8,128)(2,1)S(1)} %all-to-all-done.1.half_ref.refs_0_), custom_call_target="tpu_custom_call" | custom-call | flops 1000000 | bytes 3000000 | tf_op jit(solution)/shard_map/pallas_call | solution.py:306
  89.0 0.9 collective-permute-done.9.half_ref
  89.9 1.4 %shard_map.100 = (f32[512,1536]{1,0:T(8,128)}, f32[512,512]{1,0:T(8,128)}, f32[1,512]{1,0:T(1,128)}) custom-call(bf16[16,264,128]{2,1,0:T(8,128)(2,1)S(1)} %collective-permute-done.9.half_ref, bf16[16,264,128]{2,1,0:T(8,128)(2,1)S(1)} %all-to-all-done.1.half_ref.refs_0_, ...), custom_call_target="tpu_custom_call", output_to_operand_aliasing={{0}: (2, {}), {1}: (3, {})} | custom-call | flops 1000000 | bytes 3000000 | tf_op jit(solution)/shard_map/pallas_call | solution.py:306
  (9 shorter events, 0.2 us)
Async XLA Ops:
  0.6 7.2 %copy-start.3 = (bf16[6,48,512]{2,1,0:T(8,128)(2,1)S(1)}, bf16[6,48,512]{2,1,0:T(8,128)(2,1)}, u32[]{:S(2)}) copy-start(bf16[6,48,512]{2,1,0:T(8,128)(2,1)} %param.9) | copy-start | bytes 884740
  0.6 7.2 %copy-start.2 = (bf16[6,48,512]{2,1,0:T(8,128)(2,1)S(1)}, bf16[6,48,512]{2,1,0:T(8,128)(2,1)}, u32[]{:S(2)}) copy-start(bf16[6,48,512]{2,1,0:T(8,128)(2,1)} %param.5) | copy-start | bytes 884740
  0.7 14.9 %copy-start.1 = (bf16[512,512]{1,0:T(8,128)(2,1)S(1)}, bf16[512,512]{1,0:T(8,128)(2,1)}, u32[]{:S(2)}) copy-start(bf16[512,512]{1,0:T(8,128)(2,1)} %w_out_ref.1) | copy-start | bytes 1572868
  1.8 13.8 %copy-start = (bf16[512,1536]{1,0:T(8,128)(2,1)S(1)}, bf16[512,1536]{1,0:T(8,128)(2,1)}, u32[]{:S(2)}) copy-start(bf16[512,1536]{1,0:T(8,128)(2,1)} %w_qkv_ref.1) | copy-start | bytes 4718596
  1.8 14.9 %collective-permute-start = (bf16[2,144,512]{2,1,0:T(8,128)(2,1)S(1)}, bf16[2,144,512]{2,1,0:T(8,128)(2,1)S(1)}, u32[]{:S(2)}, u32[]{:S(2)}) collective-permute-start(bf16[2,144,512]{2,1,0:T(8,128)(2,1)S(1)} %pad_maximum_fusion), channel_id=1, source_target_pairs={{0,224},{1,225},{2,226},{3,227},{4,228},{5,229},{6,230},{7,231},{8... | collective-permute-start | bytes 884744 | tf_op jit(solution)/shard_map/ppermute | solution.py:343
  7.9 8.8 %copy-start.4 = (f32[512]{0:T(512)S(1)}, f32[512]{0:T(512)}, u32[]{:S(2)}) copy-start(f32[512]{0:T(512)} %param.6) | copy-start | bytes 6148
  8.0 7.8 %collective-permute-start.1 = (bf16[2,24,512]{2,1,0:T(8,128)(2,1)S(1)}, bf16[2,24,512]{2,1,0:T(8,128)(2,1)S(1)}, u32[]{:S(2)}, u32[]{:S(2)}) collective-permute-start(bf16[2,24,512]{2,1,0:T(8,128)(2,1)S(1)} %get-tuple-element.33), channel_id=1, source_target_pairs={{0,31},{1,0},{2,1},{3,2},{4,3},{5,4},{6,5},{7,6},{8,7},{9,8},{10,9... | collective-permute-start | bytes 147464 | tf_op jit(solution)/shard_map/ppermute | solution.py:343
  9.0 7.8 %collective-permute-start.2 = (bf16[2,24,512]{2,1,0:T(8,128)(2,1)S(1)}, bf16[2,24,512]{2,1,0:T(8,128)(2,1)S(1)}, u32[]{:S(2)}, u32[]{:S(2)}) collective-permute-start(bf16[2,24,512]{2,1,0:T(8,128)(2,1)S(1)} %get-tuple-element.34), channel_id=1, source_target_pairs={{0,255},{1,224},{2,225},{3,226},{4,227},{5,228},{6,229},{7,230},{8... | collective-permute-start | bytes 147464 | tf_op jit(solution)/shard_map/ppermute | solution.py:343
  22.4 4.8 %collective-permute-start.3 = (bf16[4096,128]{1,0:T(8,128)(2,1)S(1)}, bf16[4096,128]{1,0:T(8,128)(2,1)S(1)}, u32[]{:S(2)}, u32[]{:S(2)}) collective-permute-start(bf16[4096,128]{1,0:T(8,128)(2,1)S(1)} %get-tuple-element.44), channel_id=1, source_target_pairs={{0,1},{1,0},{2,3},{3,2},{4,5},{5,4},{6,7},{7,6},{8,9},{9,8},{10,11... | collective-permute-start | bytes 3145736 | tf_op jit(solution)/shard_map/ppermute | solution.py:343
  46.6 5.0 %collective-permute-start.4 = (bf16[264,128]{1,0:T(8,128)(2,1)S(1)}, bf16[264,128]{1,0:T(8,128)(2,1)S(1)}, u32[]{:S(2)}, u32[]{:S(2)}) collective-permute-start(bf16[264,128]{1,0:T(8,128)(2,1)S(1)} %reduce_sum.12), channel_id=1, source_target_pairs={{0,192},{1,193},{2,194},{3,195},{4,196},{5,197},{6,198},{7,199},{8... | collective-permute-start | bytes 202760 | tf_op jit(solution)/shard_map/ppermute | solution.py:343
  51.6 5.5 %collective-permute-start.5 = (bf16[264,128]{1,0:T(8,128)(2,1)S(1)}, bf16[264,128]{1,0:T(8,128)(2,1)S(1)}, u32[]{:S(2)}, u32[]{:S(2)}) collective-permute-start(bf16[264,128]{1,0:T(8,128)(2,1)S(1)} %add_convert_fusion.2), channel_id=1, source_target_pairs={{0,4},{1,5},{2,6},{3,7},{4,0},{5,1},{6,2},{7,3},{8,12},{9,13},{10,... | collective-permute-start | bytes 202760 | tf_op jit(solution)/shard_map/ppermute | solution.py:343
  54.6 10.4 %collective-permute-start.7 = (bf16[2,168,512]{2,1,0:T(8,128)(2,1)S(1)}, bf16[2,168,512]{2,1,0:T(8,128)(2,1)S(1)}, u32[]{:S(2)}, u32[]{:S(2)}) collective-permute-start(bf16[2,168,512]{2,1,0:T(8,128)(2,1)S(1)} %get-tuple-element.46), channel_id=1, source_target_pairs={{0,32},{1,33},{2,34},{3,35},{4,36},{5,37},{6,38},{7,39},{8,40},{9,... | collective-permute-start | bytes 1032200 | tf_op jit(solution)/shard_map/ppermute | solution.py:343
  57.1 8.0 %collective-permute-start.6 = (bf16[264,128]{1,0:T(8,128)(2,1)S(1)}, bf16[264,128]{1,0:T(8,128)(2,1)S(1)}, u32[]{:S(2)}, u32[]{:S(2)}) collective-permute-start(bf16[264,128]{1,0:T(8,128)(2,1)S(1)} %add_convert_fusion.1), channel_id=1, source_target_pairs={{0,12},{1,13},{2,14},{3,15},{4,8},{5,9},{6,10},{7,11},{8,4},{9,5},... | collective-permute-start | bytes 202760 | tf_op jit(solution)/shard_map/ppermute | solution.py:343
  66.2 19.7 %all-to-all-start.1 = ((bf16[16,264,128]{2,1,0:T(8,128)(2,1)}), bf16[16,264,128]{2,1,0:T(8,128)(2,1)S(1)}, u32[]{:S(2)}, u32[]{:S(2)}) async-start(bf16[16,264,128]{2,1,0:T(8,128)(2,1)} %broadcast_in_dim.3), calls=%async_computation.1 | async-start | bytes 2162688 | tf_op jit(solution)/shard_map/all_to_all | solution.py:358
  69.9 10.5 %collective-permute-start.8 = (bf16[2,48,512]{2,1,0:T(8,128)(2,1)S(1)}, bf16[2,48,512]{2,1,0:T(8,128)(2,1)S(1)}, u32[]{:S(2)}, u32[]{:S(2)}) collective-permute-start(bf16[2,48,512]{2,1,0:T(8,128)(2,1)S(1)} %shard_map.97), channel_id=1, source_target_pairs={{0,1},{1,2},{2,3},{3,4},{4,5},{5,6},{6,7},{7,8},{8,9},{9,10},{10,1... | collective-permute-start | bytes 294920 | tf_op jit(solution)/shard_map/ppermute | solution.py:343
  85.9 4.0 %collective-permute-start.9 = (bf16[16,264,128]{2,1,0:T(8,128)(2,1)S(1)}, bf16[16,264,128]{2,1,0:T(8,128)(2,1)S(1)}, u32[]{:S(2)}, u32[]{:S(2)}) collective-permute-start(bf16[16,264,128]{2,1,0:T(8,128)(2,1)S(1)} %all-to-all-done.1.half_ref.refs_0_), channel_id=1, source_target_pairs={{0,1},{1,0},{2,3},{3,2},{4,5},{5,4},{6,7},{7,6},{8,9},{9,8},{10,11... | collective-permute-start | bytes 3244040 | tf_op jit(solution)/shard_map/ppermute | solution.py:343

commit v6 on v5

--- a/solution.py
+++ b/solution.py
@@ -166,14 +166,12 @@
     pl.when(core == 0)(lambda: weight_grads(1, scaled_s, ctx_s, cot_s, dpacked_s, other_ref))
 
 
-def finish_kernel(
-    where_am_i,
+def finish(
+    side,
     latent_ref, cot_ref, ctx_ref, dpacked_ref, scaled_ref, gain_ref, w_qkv_ref, w_out_ref, picks_ref,
     own_ref, back_ref, back_lon_ref, gain_rows_ref, mine_ref,
 ):
-    core = where_am_i()[1]
-    pl.when(core == 0)(lambda: weight_grads(0, scaled_ref, ctx_ref, cot_ref, dpacked_ref, mine_ref))
-    pl.when(core == 1)(lambda: weight_grads(1, scaled_ref, ctx_ref, cot_ref, dpacked_ref, mine_ref))
+    weight_grads(side, scaled_ref, ctx_ref, cot_ref, dpacked_ref, mine_ref)
     latent = latent_ref[...].astype(f32)
     normed, recip_std = norm(latent)
     d_shifted = dot(dpacked_ref[...], w_qkv_ref[...], NT).astype(bf16).astype(f32)
@@ -199,6 +197,10 @@
         back_lon_ref[k] = moved[2 * HALF : 2 * HALF + EDGES]
 
 
+def finish_kernel(where_am_i, *refs):
+    pl.when(where_am_i()[1] == 1)(lambda: finish(1, *refs))
+
+
 def here():
     last_lat = lax.axis_index("xh") + lax.axis_index("xl") + lax.axis_index("yh") == 3
     return last_lat, lax.axis_index("c")
@@ -223,6 +225,9 @@
 
 def shape(*dims, dtype=bf16):
     return jax.ShapeDtypeStruct(dims, dtype)
+
+
+FINISHED = [shape(2, HALF, D), shape(2, BACK, D), shape(2, EDGES, D), shape(8, 128), shape(STRIP, 128)]
 
 
 def block(where_am_i, latent, cot, halo_lat, halo_lon, halo_cor, gain, w_qkv, w_out):
@@ -238,20 +243,48 @@
         [pltpu.VMEM((TOKENS, 3 * D), bf16), pltpu.VMEM((TOKENS, D), bf16)],
         5_000_000_000, 8_000_000, 9, 32,
     )(latent, cot, halo_lat, halo_lon, halo_cor, gain, w_qkv, w_out, picks)
-    own, back, back_lon, gain_rows, mine = vmem_call(
-        functools.partial(finish_kernel, where_am_i),
-        [shape(2, HALF, D), shape(2, BACK, D), shape(2, EDGES, D), shape(8, 128), shape(STRIP, 128)],
-        [], 1_500_000_000, 4_000_000, 9, 32,
-    )(*kept, gain, w_qkv, w_out, picks)
-    return own, back, back_lon, mine, other, gain_rows
-
-
-def add_kernel(mine_ref, arrived_ref, gain_ref, chunks_ref):
-    for k in range(16):
-        at = slice(k * CHUNK, (k + 1) * CHUNK)
-        to = moved_chunk(k)
-        chunks_ref[to, :CHUNK] = (mine_ref[at, :].astype(f32) + arrived_ref[at, :].astype(f32)).astype(bf16)
-        chunks_ref[to, CHUNK:] = gain_ref[...]
+    operands = (*kept, gain, w_qkv, w_out, picks)
+    finished = vmem_call(
+        functools.partial(finish_kernel, where_am_i), FINISHED, [], 1_500_000_000, 4_000_000, 9, 24
+    )(*operands)
+    return other, operands, finished
+
+
+def add_kernel(where_am_i, arrived_ref, *refs):
+    operands, early, outs = refs[:9], refs[9:14], refs[14:17]
+    chunks_ref, gain_s, mine_s = refs[17:]
+    core = where_am_i()[1]
+
+    def add_to_arrived(gain_ref, mine_ref):
+        for k in range(16):
+            at = slice(k * CHUNK, (k + 1) * CHUNK)
+            to = moved_chunk(k)
+            chunks_ref[to, :CHUNK] = (mine_ref[at, :].astype(f32) + arrived_ref[at, :].astype(f32)).astype(bf16)
+            chunks_ref[to, CHUNK:] = gain_ref[...]
+
+    @pl.when(core == 0)
+    def _():
+        finish(0, *operands, *outs, gain_s, mine_s)
+        add_to_arrived(gain_s, mine_s)
+
+    @pl.when(core == 1)
+    def _():
+        add_to_arrived(*early[3:])
+        for out_ref, early_ref in zip(outs, early):
+            out_ref[...] = early_ref[...]
+
+
+def add(where_am_i, arrived, operands, finished):
+    whole = pl.BlockSpec(memory_space=pltpu.VMEM)
+    return pl.pallas_call(
+        functools.partial(add_kernel, where_am_i),
+        out_shape=FINISHED[:3] + [shape(16, SUMMED, 128)],
+        in_specs=[whole] * 15,
+        out_specs=[whole] * 4,
+        scratch_shapes=[pltpu.VMEM((8, 128), bf16), pltpu.VMEM((STRIP, 128), bf16)],
+        compiler_params=pltpu.CompilerParams(vmem_limit_bytes=24 * 1024 * 1024),
+        cost_estimate=pl.CostEstimate(flops=1_500_000_000, bytes_accessed=4_000_000, transcendentals=0),
+    )(arrived, *operands, *finished)
 
 
 def edge_kernel(came_ref, back_lon_ref, edge_ref):
@@ -343,11 +376,9 @@
     return lax.ppermute(value, ALL, pairs)
 
 
-def sum_and_return(own, back, back_lon, mine, other, gain_rows):
+def sum_and_return(other, operands, finished):
     arrived = send(other, swapped(1))
-    chunks = vmem_call(
-        add_kernel, [shape(16, SUMMED, 128)], [], 1_000_000, 4_000_000, 3
-    )(mine, arrived, gain_rows)[0]
+    own, back, back_lon, chunks = add(here, arrived, operands, finished)
     pieces = lax.all_to_all(chunks, BOX, 0, 0, tiled=True)
     total = jnp.sum(pieces.astype(f32), axis=0).astype(bf16)
     for bits in (192, 4, 12):

time: 91.7 us -> 89.4 us (0.975)
  waiting for transfers between devices: 18.5 us -> 10.2 us
  starting transfers between devices: 38.4 us -> 46.5 us
  blocking collectives: 19 us -> 17 us
    ppermute x10, starting transfers between devices: 34.7 us -> 42.8 us  [send(): return lax.ppermute(value, ALL, pairs)]
    all_to_all x1, waiting for transfers between devices: 4.64 us -> 0.01 us  [sum_and_return(): lax.all_to_all(jnp.broadcast_to(total, (16, SUMMED, 128)), BOX, 0, 0, til...]
    ppermute x10, waiting for transfers between devices: 13.9 us -> 10.2 us  [send(): return lax.ppermute(value, ALL, pairs)]
    all_to_all x1, blocking collectives: 19 us -> 17 us  [sum_and_return(): pieces = lax.all_to_all(chunks, BOX, 0, 0, tiled=True)]
where the time goes in v6:
time: 89.4 us; the launch traced here: 89.2 us
  starting transfers between devices  46.5 us (52%)
  blocking collectives  17 us (19%)
  Pallas kernels  12 us (13%)
  waiting for transfers between devices  10.2 us (11%)
  local copies, waits for them, and re-layouts  2.26 us (3%)
  between operations  0.96 us (1%)
    ppermute x10, starting transfers between devices, send(): return lax.ppermute(value, ALL, pairs)  42.8 us
    all_to_all x1, blocking collectives, sum_and_return(): pieces = lax.all_to_all(chunks, BOX, 0, 0, tiled=True)  17 us
    ppermute x10, waiting for transfers between devices, send(): return lax.ppermute(value, ALL, pairs)  10.2 us
    pallas_call x1, Pallas kernels, block(): vmem_call(functools.partial(attend_kernel, where_am_i), [shape(STRIP, 128...  5.69 us
    all_to_all x1, starting transfers between devices, sum_and_return(): lax.all_to_all(jnp.broadcast_to(total, (16, SUMMED, 128)), BOX, 0, 0, til...  3.7 us
    pallas_call x2, Pallas kernels, unpack(): pl.pallas_call(functools.partial(unpack_kernel, where_am_i, side), out_sh...  2.84 us
    pallas_call x1, Pallas kernels, block(): vmem_call(functools.partial(finish_kernel, where_am_i), FINISHED, [], 150...  2.09 us
  transfers between devices with their start and end apart: 11, of which 7 were waited for; matrix products, arithmetic and copies ran while one was open for 0% of the time, Pallas kernels for 5%

profile of v6, /device:TPU:1, one launch (start us, length us, event | category | flops | bytes accessed | tf_op | source)
XLA Modules:
  0.0 89.2 jit_solution(18064910377998852791)
XLA Ops:
  0.6 0.0 copy-start.3
  0.6 0.0 copy-start.2
  0.7 0.0 copy-start.1
  0.7 1.1 %slice_bitcast_fusion.2 = (bf16[1,3,48,512]{3,2,1,0:T(8,128)(2,1)S(1)}, bf16[3,48,512]{2,1,0:T(8,128)(2,1)S(1)}, bf16[3,48,512]{2,1,0:T(8,128)(2,1)S(1)}, bf16[1,3,48,512]{3,2,1,0:T(8,128)(2,1)S(1)}) fusion(bf16[6,48,512]{2,1,0:T(8,128)(2,1)} %param.9, bf16[6,48,512]{2,1,0:T(8,128)(2,1)} %param.5), kind=kLoop, calls=%fused_computation.8 | loop fusion | bytes 884736 | tf_op jit(solution)/shard_map/stack | solution.py:402
  1.8 0.0 copy-start
  1.8 6.0 %collective-permute-start = (bf16[2,144,512]{2,1,0:T(8,128)(2,1)S(1)}, bf16[2,144,512]{2,1,0:T(8,128)(2,1)S(1)}, u32[]{:S(2)}, u32[]{:S(2)}) collective-permute-start(bf16[2,144,512]{2,1,0:T(8,128)(2,1)S(1)} %pad_maximum_fusion), channel_id=1, source_target_pairs={{0,224},{1,225},{2,226},{3,227},{4,228},{5,229},{6,230},{7,231},{8... | collective-permute-start | bytes 884744 | tf_op jit(solution)/shard_map/ppermute | solution.py:376
  7.8 0.0 copy-done.3
  7.8 0.0 copy-done.2
  7.9 0.0 copy-start.4
  8.0 1.0 %collective-permute-start.1 = (bf16[2,24,512]{2,1,0:T(8,128)(2,1)S(1)}, bf16[2,24,512]{2,1,0:T(8,128)(2,1)S(1)}, u32[]{:S(2)}, u32[]{:S(2)}) collective-permute-start(bf16[2,24,512]{2,1,0:T(8,128)(2,1)S(1)} %get-tuple-element.37), channel_id=1, source_target_pairs={{0,31},{1,0},{2,1},{3,2},{4,3},{5,4},{6,5},{7,6},{8,7},{9,8},{10,9... | collective-permute-start | bytes 147464 | tf_op jit(solution)/shard_map/ppermute | solution.py:376
  9.0 6.6 %collective-permute-start.2 = (bf16[2,24,512]{2,1,0:T(8,128)(2,1)S(1)}, bf16[2,24,512]{2,1,0:T(8,128)(2,1)S(1)}, u32[]{:S(2)}, u32[]{:S(2)}) collective-permute-start(bf16[2,24,512]{2,1,0:T(8,128)(2,1)S(1)} %get-tuple-element.38), channel_id=1, source_target_pairs={{0,255},{1,224},{2,225},{3,226},{4,227},{5,228},{6,229},{7,230},{8... | collective-permute-start | bytes 147464 | tf_op jit(solution)/shard_map/ppermute | solution.py:376
  15.6 0.0 copy-done.1
  15.6 0.0 copy-done
  15.6 0.2 shard_map.93
  15.7 0.0 collective-permute-done.1.halo_lon_ref
  15.7 1.0 %collective-permute-done.2.halo_cor_ref = bf16[2,24,512]{2,1,0:T(8,128)(2,1)S(1)} collective-permute-done((bf16[2,24,512]{2,1,0:T(8,128)(2,1)S(1)}, bf16[2,24,512]{2,1,0:T(8,128)(2,1)S(1)}, u32[]{:S(2)}, u32[]{:S(2)}) %collective-permute-start.2) | collective-permute-done | bytes 49184 | tf_op jit(solution)/shard_map/ppermute | solution.py:376
  16.7 0.0 collective-permute-done.halo_lat_ref
  16.7 0.0 copy-done.4
  16.7 5.7 %shard_map.94 = (bf16[4096,128]{1,0:T(8,128)(2,1)S(1)}, bf16[320,512]{1,0:T(8,128)(2,1)S(1)}, bf16[320,512]{1,0:T(8,128)(2,1)S(1)}, bf16[320,512]{1,0:T(8,128)(2...) custom-call(bf16[288,512]{1,0:T(8,128)(2,1)S(1)} %bitcast.16, bf16[288,512]{1,0:T(8,128)(2,1)S(1)} %bitcast.17, ...), custom_call_target="tpu_custom_call" | custom-call | flops 5000000000 | bytes 8000000 | tf_op jit(solution)/shard_map/pallas_call | solution.py:237
  22.4 2.5 %collective-permute-start.3 = (bf16[4096,128]{1,0:T(8,128)(2,1)S(1)}, bf16[4096,128]{1,0:T(8,128)(2,1)S(1)}, u32[]{:S(2)}, u32[]{:S(2)}) collective-permute-start(bf16[4096,128]{1,0:T(8,128)(2,1)S(1)} %get-tuple-element.42), channel_id=1, source_target_pairs={{0,1},{1,0},{2,3},{3,2},{4,5},{5,4},{6,7},{7,6},{8,9},{9,8},{10,11... | collective-permute-start | bytes 3145736 | tf_op jit(solution)/shard_map/ppermute | solution.py:376
  24.9 2.1 %shard_map.95 = (bf16[2,144,512]{2,1,0:T(8,128)(2,1)S(1)}, bf16[2,168,512]{2,1,0:T(8,128)(2,1)S(1)}, bf16[2,24,512]{2,1,0:T(8,128)(2,1)S(1)}, bf16[8,128]{1,0:T(8,128)(2,1)S(1)}, bf16[4096,128]{1,0:T(8,128)(2,1)S(1)}) custom-call(bf16[320,512]{1,0:T(8,128)(2,1)S(1)} %get-tuple-element.43.refs_0_, bf16[320,512]{1,0:T(8,128)(2,1)S(1)} %get-tuple-element.44.refs_1_, ...), custom_call_target="tpu_custom_call" | custom-call | flops 1500000000 | bytes 4000000 | tf_op jit(solution)/shard_map/pallas_call | solution.py:247
  27.0 0.2 collective-permute-done.3.arrived_ref
  27.2 0.3 shard_map.96
  27.5 17.0 %all_to_all.10 = bf16[16,264,128]{2,1,0:T(8,128)(2,1)S(1)} all-to-all(bf16[16,264,128]{2,1,0:T(8,128)(2,1)S(1)} %get-tuple-element.53), channel_id=1, replica_groups=mesh['xh'=2,'xl'=2,'yh'=2,'yl'=2,'zh'=2,'zm'=2,'zl'=2,'c'=2] {'xl','yh',..., dimensions={0} | all-to-all | bytes 2162688 | tf_op jit(solution)/shard_map/all_to_all | solution.py:382
  44.6 0.1 reduce_sum.12
  44.7 2.9 %collective-permute-start.4 = (bf16[264,128]{1,0:T(8,128)(2,1)S(1)}, bf16[264,128]{1,0:T(8,128)(2,1)S(1)}, u32[]{:S(2)}, u32[]{:S(2)}) collective-permute-start(bf16[264,128]{1,0:T(8,128)(2,1)S(1)} %reduce_sum.12), channel_id=1, source_target_pairs={{0,192},{1,193},{2,194},{3,195},{4,196},{5,197},{6,198},{7,199},{8... | collective-permute-start | bytes 202760 | tf_op jit(solution)/shard_map/ppermute | solution.py:376
  47.6 1.7 %collective-permute-done.4 = bf16[264,128]{1,0:T(8,128)(2,1)S(1)} collective-permute-done((bf16[264,128]{1,0:T(8,128)(2,1)S(1)}, bf16[264,128]{1,0:T(8,128)(2,1)S(1)}, u32[]{:S(2)}, u32[]{:S(2)}) %collective-permute-start.4) | collective-permute-done | bytes 67616 | tf_op jit(solution)/shard_map/ppermute | solution.py:376
  49.3 3.1 %collective-permute-start.5 = (bf16[264,128]{1,0:T(8,128)(2,1)S(1)}, bf16[264,128]{1,0:T(8,128)(2,1)S(1)}, u32[]{:S(2)}, u32[]{:S(2)}) collective-permute-start(bf16[264,128]{1,0:T(8,128)(2,1)S(1)} %add_convert_fusion.2), channel_id=1, source_target_pairs={{0,4},{1,5},{2,6},{3,7},{4,0},{5,1},{6,2},{7,3},{8,12},{9,13},{10,... | collective-permute-start | bytes 202760 | tf_op jit(solution)/shard_map/ppermute | solution.py:376
  52.4 1.2 %collective-permute-start.7 = (bf16[2,168,512]{2,1,0:T(8,128)(2,1)S(1)}, bf16[2,168,512]{2,1,0:T(8,128)(2,1)S(1)}, u32[]{:S(2)}, u32[]{:S(2)}) collective-permute-start(bf16[2,168,512]{2,1,0:T(8,128)(2,1)S(1)} %get-tuple-element.54), channel_id=1, source_target_pairs={{0,32},{1,33},{2,34},{3,35},{4,36},{5,37},{6,38},{7,39},{8,40},{9,... | collective-permute-start | bytes 1032200 | tf_op jit(solution)/shard_map/ppermute | solution.py:376
  53.6 1.2 %collective-permute-done.5 = bf16[264,128]{1,0:T(8,128)(2,1)S(1)} collective-permute-done((bf16[264,128]{1,0:T(8,128)(2,1)S(1)}, bf16[264,128]{1,0:T(8,128)(2,1)S(1)}, u32[]{:S(2)}, u32[]{:S(2)}) %collective-permute-start.5) | collective-permute-done | bytes 67616 | tf_op jit(solution)/shard_map/ppermute | solution.py:376
  54.8 4.7 %collective-permute-start.6 = (bf16[264,128]{1,0:T(8,128)(2,1)S(1)}, bf16[264,128]{1,0:T(8,128)(2,1)S(1)}, u32[]{:S(2)}, u32[]{:S(2)}) collective-permute-start(bf16[264,128]{1,0:T(8,128)(2,1)S(1)} %add_convert_fusion.1), channel_id=1, source_target_pairs={{0,12},{1,13},{2,14},{3,15},{4,8},{5,9},{6,10},{7,11},{8,4},{9,5},... | collective-permute-start | bytes 202760 | tf_op jit(solution)/shard_map/ppermute | solution.py:376
  59.4 2.6 %collective-permute-done.7.came_ref = bf16[2,168,512]{2,1,0:T(8,128)(2,1)S(1)} collective-permute-done((bf16[2,168,512]{2,1,0:T(8,128)(2,1)S(1)}, bf16[2,168,512]{2,1,0:T(8,128)(2,1)S(1)}, u32[]{:S(2)}, u32[]{:S(2)}) %collective-permute-start.7) | collective-permute-done | bytes 344096 | tf_op jit(solution)/shard_map/ppermute | solution.py:376
  62.1 0.0 collective-permute-done.6
  62.1 1.1 %broadcast_in_dim.3 = bf16[16,264,128]{2,1,0:T(8,128)(2,1)} broadcast(bf16[264,128]{1,0:T(8,128)(2,1)S(1)} %add_convert_fusion), dimensions={1,2} | broadcast | bytes 1148928 | tf_op jit(solution)/shard_map/broadcast_in_dim | solution.py:389
  63.2 3.7 %all-to-all-start.1 = ((bf16[16,264,128]{2,1,0:T(8,128)(2,1)}), bf16[16,264,128]{2,1,0:T(8,128)(2,1)S(1)}, u32[]{:S(2)}, u32[]{:S(2)}) async-start(bf16[16,264,128]{2,1,0:T(8,128)(2,1)} %broadcast_in_dim.3), calls=%async_computation.1 | async-start | bytes 2162688 | tf_op jit(solution)/shard_map/all_to_all | solution.py:389
  66.9 7.8 %collective-permute-start.8 = (bf16[2,48,512]{2,1,0:T(8,128)(2,1)S(1)}, bf16[2,48,512]{2,1,0:T(8,128)(2,1)S(1)}, u32[]{:S(2)}, u32[]{:S(2)}) collective-permute-start(bf16[2,48,512]{2,1,0:T(8,128)(2,1)S(1)} %shard_map.97), channel_id=1, source_target_pairs={{0,1},{1,2},{2,3},{3,4},{4,5},{5,6},{6,7},{7,8},{8,9},{9,10},{10,1... | collective-permute-start | bytes 294920 | tf_op jit(solution)/shard_map/ppermute | solution.py:376
  74.7 2.6 %collective-permute-done.8.edge_ref = bf16[2,48,512]{2,1,0:T(8,128)(2,1)S(1)} collective-permute-done((bf16[2,48,512]{2,1,0:T(8,128)(2,1)S(1)}, bf16[2,48,512]{2,1,0:T(8,128)(2,1)S(1)}, u32[]{:S(2)}, u32[]{:S(2)}) %collective-permute-start.8) | collective-permute-done | bytes 98336 | tf_op jit(solution)/shard_map/ppermute | solution.py:376
  77.3 0.9 shard_map.98
  78.2 0.0 all-to-all-done.1.half_ref.refs_0_
  78.2 7.1 %collective-permute-start.9 = (bf16[16,264,128]{2,1,0:T(8,128)(2,1)S(1)}, bf16[16,264,128]{2,1,0:T(8,128)(2,1)S(1)}, u32[]{:S(2)}, u32[]{:S(2)}) collective-permute-start(bf16[16,264,128]{2,1,0:T(8,128)(2,1)S(1)} %all-to-all-done.1.half_ref.refs_0_), channel_id=1, source_target_pairs={{0,1},{1,0},{2,3},{3,2},{4,5},{5,4},{6,7},{7,6},{8,9},{9,8},{10,11... | collective-permute-start | bytes 3244040 | tf_op jit(solution)/shard_map/ppermute | solution.py:376
  85.3 1.4 %shard_map.99 = (f32[512,1536]{1,0:T(8,128)}, f32[512,512]{1,0:T(8,128)}) custom-call(bf16[16,264,128]{2,1,0:T(8,128)(2,1)S(1)} %all-to-all-done.1.half_ref.refs_0_), custom_call_target="tpu_custom_call" | custom-call | flops 1000000 | bytes 3000000 | tf_op jit(solution)/shard_map/pallas_call | solution.py:339
  86.7 0.9 %collective-permute-done.9.half_ref = bf16[16,264,128]{2,1,0:T(8,128)(2,1)S(1)} collective-permute-done((bf16[16,264,128]{2,1,0:T(8,128)(2,1)S(1)}, bf16[16,264,128]{2,1,0:T(8,128)(2,1)S(1)}, u32[]{:S(2)}, u32[]{:S(2)}) %collective-permute-start.9) | collective-permute-done | bytes 1081376 | tf_op jit(solution)/shard_map/ppermute | solution.py:376
  87.6 1.4 %shard_map.100 = (f32[512,1536]{1,0:T(8,128)}, f32[512,512]{1,0:T(8,128)}, f32[1,512]{1,0:T(1,128)}) custom-call(bf16[16,264,128]{2,1,0:T(8,128)(2,1)S(1)} %collective-permute-done.9.half_ref, bf16[16,264,128]{2,1,0:T(8,128)(2,1)S(1)} %all-to-all-done.1.half_ref.refs_0_, ...), custom_call_target="tpu_custom_call", output_to_operand_aliasing={{0}: (2, {}), {1}: (3, {})} | custom-call | flops 1000000 | bytes 3000000 | tf_op jit(solution)/shard_map/pallas_call | solution.py:339
  (9 shorter events, 0.2 us)
Async XLA Ops:
  0.6 7.2 %copy-start.3 = (bf16[6,48,512]{2,1,0:T(8,128)(2,1)S(1)}, bf16[6,48,512]{2,1,0:T(8,128)(2,1)}, u32[]{:S(2)}) copy-start(bf16[6,48,512]{2,1,0:T(8,128)(2,1)} %param.9) | copy-start | bytes 884740
  0.6 7.2 %copy-start.2 = (bf16[6,48,512]{2,1,0:T(8,128)(2,1)S(1)}, bf16[6,48,512]{2,1,0:T(8,128)(2,1)}, u32[]{:S(2)}) copy-start(bf16[6,48,512]{2,1,0:T(8,128)(2,1)} %param.5) | copy-start | bytes 884740
  0.7 14.9 %copy-start.1 = (bf16[512,512]{1,0:T(8,128)(2,1)S(1)}, bf16[512,512]{1,0:T(8,128)(2,1)}, u32[]{:S(2)}) copy-start(bf16[512,512]{1,0:T(8,128)(2,1)} %w_out_ref.1) | copy-start | bytes 1572868
  1.8 13.8 %copy-start = (bf16[512,1536]{1,0:T(8,128)(2,1)S(1)}, bf16[512,1536]{1,0:T(8,128)(2,1)}, u32[]{:S(2)}) copy-start(bf16[512,1536]{1,0:T(8,128)(2,1)} %w_qkv_ref.1) | copy-start | bytes 4718596
  1.8 14.9 %collective-permute-start = (bf16[2,144,512]{2,1,0:T(8,128)(2,1)S(1)}, bf16[2,144,512]{2,1,0:T(8,128)(2,1)S(1)}, u32[]{:S(2)}, u32[]{:S(2)}) collective-permute-start(bf16[2,144,512]{2,1,0:T(8,128)(2,1)S(1)} %pad_maximum_fusion), channel_id=1, source_target_pairs={{0,224},{1,225},{2,226},{3,227},{4,228},{5,229},{6,230},{7,231},{8... | collective-permute-start | bytes 884744 | tf_op jit(solution)/shard_map/ppermute | solution.py:376
  7.9 8.8 %copy-start.4 = (f32[512]{0:T(512)S(1)}, f32[512]{0:T(512)}, u32[]{:S(2)}) copy-start(f32[512]{0:T(512)} %param.6) | copy-start | bytes 6148
  8.0 7.8 %collective-permute-start.1 = (bf16[2,24,512]{2,1,0:T(8,128)(2,1)S(1)}, bf16[2,24,512]{2,1,0:T(8,128)(2,1)S(1)}, u32[]{:S(2)}, u32[]{:S(2)}) collective-permute-start(bf16[2,24,512]{2,1,0:T(8,128)(2,1)S(1)} %get-tuple-element.37), channel_id=1, source_target_pairs={{0,31},{1,0},{2,1},{3,2},{4,3},{5,4},{6,5},{7,6},{8,7},{9,8},{10,9... | collective-permute-start | bytes 147464 | tf_op jit(solution)/shard_map/ppermute | solution.py:376
  9.0 7.8 %collective-permute-start.2 = (bf16[2,24,512]{2,1,0:T(8,128)(2,1)S(1)}, bf16[2,24,512]{2,1,0:T(8,128)(2,1)S(1)}, u32[]{:S(2)}, u32[]{:S(2)}) collective-permute-start(bf16[2,24,512]{2,1,0:T(8,128)(2,1)S(1)} %get-tuple-element.38), channel_id=1, source_target_pairs={{0,255},{1,224},{2,225},{3,226},{4,227},{5,228},{6,229},{7,230},{8... | collective-permute-start | bytes 147464 | tf_op jit(solution)/shard_map/ppermute | solution.py:376
  22.4 4.8 %collective-permute-start.3 = (bf16[4096,128]{1,0:T(8,128)(2,1)S(1)}, bf16[4096,128]{1,0:T(8,128)(2,1)S(1)}, u32[]{:S(2)}, u32[]{:S(2)}) collective-permute-start(bf16[4096,128]{1,0:T(8,128)(2,1)S(1)} %get-tuple-element.42), channel_id=1, source_target_pairs={{0,1},{1,0},{2,3},{3,2},{4,5},{5,4},{6,7},{7,6},{8,9},{9,8},{10,11... | collective-permute-start | bytes 3145736 | tf_op jit(solution)/shard_map/ppermute | solution.py:376
  44.7 4.5 %collective-permute-start.4 = (bf16[264,128]{1,0:T(8,128)(2,1)S(1)}, bf16[264,128]{1,0:T(8,128)(2,1)S(1)}, u32[]{:S(2)}, u32[]{:S(2)}) collective-permute-start(bf16[264,128]{1,0:T(8,128)(2,1)S(1)} %reduce_sum.12), channel_id=1, source_target_pairs={{0,192},{1,193},{2,194},{3,195},{4,196},{5,197},{6,198},{7,199},{8... | collective-permute-start | bytes 202760 | tf_op jit(solution)/shard_map/ppermute | solution.py:376
  49.3 5.5 %collective-permute-start.5 = (bf16[264,128]{1,0:T(8,128)(2,1)S(1)}, bf16[264,128]{1,0:T(8,128)(2,1)S(1)}, u32[]{:S(2)}, u32[]{:S(2)}) collective-permute-start(bf16[264,128]{1,0:T(8,128)(2,1)S(1)} %add_convert_fusion.2), channel_id=1, source_target_pairs={{0,4},{1,5},{2,6},{3,7},{4,0},{5,1},{6,2},{7,3},{8,12},{9,13},{10,... | collective-permute-start | bytes 202760 | tf_op jit(solution)/shard_map/ppermute | solution.py:376
  52.4 9.7 %collective-permute-start.7 = (bf16[2,168,512]{2,1,0:T(8,128)(2,1)S(1)}, bf16[2,168,512]{2,1,0:T(8,128)(2,1)S(1)}, u32[]{:S(2)}, u32[]{:S(2)}) collective-permute-start(bf16[2,168,512]{2,1,0:T(8,128)(2,1)S(1)} %get-tuple-element.54), channel_id=1, source_target_pairs={{0,32},{1,33},{2,34},{3,35},{4,36},{5,37},{6,38},{7,39},{8,40},{9,... | collective-permute-start | bytes 1032200 | tf_op jit(solution)/shard_map/ppermute | solution.py:376
  54.8 7.3 %collective-permute-start.6 = (bf16[264,128]{1,0:T(8,128)(2,1)S(1)}, bf16[264,128]{1,0:T(8,128)(2,1)S(1)}, u32[]{:S(2)}, u32[]{:S(2)}) collective-permute-start(bf16[264,128]{1,0:T(8,128)(2,1)S(1)} %add_convert_fusion.1), channel_id=1, source_target_pairs={{0,12},{1,13},{2,14},{3,15},{4,8},{5,9},{6,10},{7,11},{8,4},{9,5},... | collective-permute-start | bytes 202760 | tf_op jit(solution)/shard_map/ppermute | solution.py:376
  63.2 14.9 %all-to-all-start.1 = ((bf16[16,264,128]{2,1,0:T(8,128)(2,1)}), bf16[16,264,128]{2,1,0:T(8,128)(2,1)S(1)}, u32[]{:S(2)}, u32[]{:S(2)}) async-start(bf16[16,264,128]{2,1,0:T(8,128)(2,1)} %broadcast_in_dim.3), calls=%async_computation.1 | async-start | bytes 2162688 | tf_op jit(solution)/shard_map/all_to_all | solution.py:389
  66.9 10.4 %collective-permute-start.8 = (bf16[2,48,512]{2,1,0:T(8,128)(2,1)S(1)}, bf16[2,48,512]{2,1,0:T(8,128)(2,1)S(1)}, u32[]{:S(2)}, u32[]{:S(2)}) collective-permute-start(bf16[2,48,512]{2,1,0:T(8,128)(2,1)S(1)} %shard_map.97), channel_id=1, source_target_pairs={{0,1},{1,2},{2,3},{3,4},{4,5},{5,6},{6,7},{7,8},{8,9},{9,10},{10,1... | collective-permute-start | bytes 294920 | tf_op jit(solution)/shard_map/ppermute | solution.py:376
  78.2 9.4 %collective-permute-start.9 = (bf16[16,264,128]{2,1,0:T(8,128)(2,1)S(1)}, bf16[16,264,128]{2,1,0:T(8,128)(2,1)S(1)}, u32[]{:S(2)}, u32[]{:S(2)}) collective-permute-start(bf16[16,264,128]{2,1,0:T(8,128)(2,1)S(1)} %all-to-all-done.1.half_ref.refs_0_), channel_id=1, source_target_pairs={{0,1},{1,0},{2,3},{3,2},{4,5},{5,4},{6,7},{7,6},{8,9},{9,8},{10,11... | collective-permute-start | bytes 3244040 | tf_op jit(solution)/shard_map/ppermute | solution.py:376

commit v7 on v6

--- a/solution.py
+++ b/solution.py
@@ -10,7 +10,7 @@
 ALL = ("xh", "xl", "yh", "yl", "zh", "zm", "zl", "c")
 LAT = ALL[:3]
 LON = ALL[3:]
-BOX = ("xl", "yh", "yl", "zl")
+BOX = ("xh", "xl", "yl", "zl")
 HEADS = 16
 HS = 32
 WL = 6
@@ -207,7 +207,7 @@
 
 
 def moved_chunk(k):
-    return lax.rem(k + 8 * lax.axis_index("xh"), 16)
+    return k + ((k ^ 2) - k) * lax.axis_index("yh")
 
 
 def vmem_call(kernel, out_shapes, scratch, flops, moved, count, mebibytes=12):
@@ -381,7 +381,7 @@
     own, back, back_lon, chunks = add(here, arrived, operands, finished)
     pieces = lax.all_to_all(chunks, BOX, 0, 0, tiled=True)
     total = jnp.sum(pieces.astype(f32), axis=0).astype(bf16)
-    for bits in (192, 4, 12):
+    for bits in (48, 4, 12):
         total = (total.astype(f32) + send(total, swapped(bits)).astype(f32)).astype(bf16)
     came = send(back, shifted(1, 0))
     edge = vmem_call(edge_kernel, [shape(2, 2 * EDGES, D)], [], 1_000_000, 1_000_000, 2)(came, back_lon)[0]

time: 89.4 us -> 89.8 us (level)
  blocking collectives: 17 us -> 18 us
    all_to_all x1, blocking collectives: 17 us -> 18 us  [sum_and_return(): pieces = lax.all_to_all(chunks, BOX, 0, 0, tiled=True)]
  transfers between devices with their start and end apart: 11 -> 11, of which waited for: 7 -> 6; matrix products, arithmetic and copies ran while one was open for 0% -> 0% of each run, Pallas kernels for 5% -> 5%
where the time goes in v7:
time: 89.8 us; the launch traced here: 89.6 us
  starting transfers between devices  46.6 us (52%)
  blocking collectives  18 us (20%)
  Pallas kernels  12 us (13%)
  waiting for transfers between devices  9.53 us (11%)
  local copies, waits for them, and re-layouts  2.26 us (3%)
  between operations  0.97 us (1%)
    ppermute x10, starting transfers between devices, send(): return lax.ppermute(value, ALL, pairs)  42.9 us
    all_to_all x1, blocking collectives, sum_and_return(): pieces = lax.all_to_all(chunks, BOX, 0, 0, tiled=True)  18 us
    ppermute x10, waiting for transfers between devices, send(): return lax.ppermute(value, ALL, pairs)  9.53 us
    pallas_call x1, Pallas kernels, block(): vmem_call(functools.partial(attend_kernel, where_am_i), [shape(STRIP, 128...  5.69 us
    all_to_all x1, starting transfers between devices, sum_and_return(): lax.all_to_all(jnp.broadcast_to(total, (16, SUMMED, 128)), BOX, 0, 0, til...  3.7 us
    pallas_call x2, Pallas kernels, unpack(): pl.pallas_call(functools.partial(unpack_kernel, where_am_i, side), out_sh...  2.84 us
    pallas_call x1, Pallas kernels, block(): vmem_call(functools.partial(finish_kernel, where_am_i), FINISHED, [], 150...  2.09 us
  transfers between devices with their start and end apart: 11, of which 6 were waited for; matrix products, arithmetic and copies ran while one was open for 0% of the time, Pallas kernels for 5%

profile of v7, /device:TPU:1, one launch (start us, length us, event | category | flops | bytes accessed | tf_op | source)
XLA Modules:
  0.0 89.6 jit_solution(17410321843909132181)
XLA Ops:
  0.6 0.0 copy-start.3
  0.6 0.0 copy-start.2
  0.7 0.0 copy-start.1
  0.7 1.1 %slice_bitcast_fusion.2 = (bf16[1,3,48,512]{3,2,1,0:T(8,128)(2,1)S(1)}, bf16[3,48,512]{2,1,0:T(8,128)(2,1)S(1)}, bf16[3,48,512]{2,1,0:T(8,128)(2,1)S(1)}, bf16[1,3,48,512]{3,2,1,0:T(8,128)(2,1)S(1)}) fusion(bf16[6,48,512]{2,1,0:T(8,128)(2,1)} %param.9, bf16[6,48,512]{2,1,0:T(8,128)(2,1)} %param.5), kind=kLoop, calls=%fused_computation.8 | loop fusion | bytes 884736 | tf_op jit(solution)/shard_map/stack | solution.py:402
  1.8 0.0 copy-start
  1.8 6.0 %collective-permute-start = (bf16[2,144,512]{2,1,0:T(8,128)(2,1)S(1)}, bf16[2,144,512]{2,1,0:T(8,128)(2,1)S(1)}, u32[]{:S(2)}, u32[]{:S(2)}) collective-permute-start(bf16[2,144,512]{2,1,0:T(8,128)(2,1)S(1)} %pad_maximum_fusion), channel_id=1, source_target_pairs={{0,224},{1,225},{2,226},{3,227},{4,228},{5,229},{6,230},{7,231},{8... | collective-permute-start | bytes 884744 | tf_op jit(solution)/shard_map/ppermute | solution.py:376
  7.8 0.0 copy-done.3
  7.8 0.0 copy-done.2
  7.9 0.0 copy-start.4
  8.0 1.0 %collective-permute-start.1 = (bf16[2,24,512]{2,1,0:T(8,128)(2,1)S(1)}, bf16[2,24,512]{2,1,0:T(8,128)(2,1)S(1)}, u32[]{:S(2)}, u32[]{:S(2)}) collective-permute-start(bf16[2,24,512]{2,1,0:T(8,128)(2,1)S(1)} %get-tuple-element.37), channel_id=1, source_target_pairs={{0,31},{1,0},{2,1},{3,2},{4,3},{5,4},{6,5},{7,6},{8,7},{9,8},{10,9... | collective-permute-start | bytes 147464 | tf_op jit(solution)/shard_map/ppermute | solution.py:376
  9.0 6.6 %collective-permute-start.2 = (bf16[2,24,512]{2,1,0:T(8,128)(2,1)S(1)}, bf16[2,24,512]{2,1,0:T(8,128)(2,1)S(1)}, u32[]{:S(2)}, u32[]{:S(2)}) collective-permute-start(bf16[2,24,512]{2,1,0:T(8,128)(2,1)S(1)} %get-tuple-element.38), channel_id=1, source_target_pairs={{0,255},{1,224},{2,225},{3,226},{4,227},{5,228},{6,229},{7,230},{8... | collective-permute-start | bytes 147464 | tf_op jit(solution)/shard_map/ppermute | solution.py:376
  15.6 0.0 copy-done.1
  15.6 0.0 copy-done
  15.6 0.2 shard_map.93
  15.7 0.0 collective-permute-done.1.halo_lon_ref
  15.7 1.0 %collective-permute-done.2.halo_cor_ref = bf16[2,24,512]{2,1,0:T(8,128)(2,1)S(1)} collective-permute-done((bf16[2,24,512]{2,1,0:T(8,128)(2,1)S(1)}, bf16[2,24,512]{2,1,0:T(8,128)(2,1)S(1)}, u32[]{:S(2)}, u32[]{:S(2)}) %collective-permute-start.2) | collective-permute-done | bytes 49184 | tf_op jit(solution)/shard_map/ppermute | solution.py:376
  16.7 0.0 collective-permute-done.halo_lat_ref
  16.7 0.0 copy-done.4
  16.7 5.7 %shard_map.94 = (bf16[4096,128]{1,0:T(8,128)(2,1)S(1)}, bf16[320,512]{1,0:T(8,128)(2,1)S(1)}, bf16[320,512]{1,0:T(8,128)(2,1)S(1)}, bf16[320,512]{1,0:T(8,128)(2...) custom-call(bf16[288,512]{1,0:T(8,128)(2,1)S(1)} %bitcast.16, bf16[288,512]{1,0:T(8,128)(2,1)S(1)} %bitcast.17, ...), custom_call_target="tpu_custom_call" | custom-call | flops 5000000000 | bytes 8000000 | tf_op jit(solution)/shard_map/pallas_call | solution.py:237
  22.4 2.5 %collective-permute-start.3 = (bf16[4096,128]{1,0:T(8,128)(2,1)S(1)}, bf16[4096,128]{1,0:T(8,128)(2,1)S(1)}, u32[]{:S(2)}, u32[]{:S(2)}) collective-permute-start(bf16[4096,128]{1,0:T(8,128)(2,1)S(1)} %get-tuple-element.42), channel_id=1, source_target_pairs={{0,1},{1,0},{2,3},{3,2},{4,5},{5,4},{6,7},{7,6},{8,9},{9,8},{10,11... | collective-permute-start | bytes 3145736 | tf_op jit(solution)/shard_map/ppermute | solution.py:376
  24.9 2.1 %shard_map.95 = (bf16[2,144,512]{2,1,0:T(8,128)(2,1)S(1)}, bf16[2,168,512]{2,1,0:T(8,128)(2,1)S(1)}, bf16[2,24,512]{2,1,0:T(8,128)(2,1)S(1)}, bf16[8,128]{1,0:T(8,128)(2,1)S(1)}, bf16[4096,128]{1,0:T(8,128)(2,1)S(1)}) custom-call(bf16[320,512]{1,0:T(8,128)(2,1)S(1)} %get-tuple-element.43.refs_0_, bf16[320,512]{1,0:T(8,128)(2,1)S(1)} %get-tuple-element.44.refs_1_, ...), custom_call_target="tpu_custom_call" | custom-call | flops 1500000000 | bytes 4000000 | tf_op jit(solution)/shard_map/pallas_call | solution.py:247
  27.0 0.2 collective-permute-done.3.arrived_ref
  27.2 0.3 shard_map.96
  27.5 18.0 %all_to_all.10 = bf16[16,264,128]{2,1,0:T(8,128)(2,1)S(1)} all-to-all(bf16[16,264,128]{2,1,0:T(8,128)(2,1)S(1)} %get-tuple-element.53), channel_id=1, replica_groups=mesh['xh'=2,'xl'=2,'yh'=2,'yl'=2,'zh'=2,'zm'=2,'zl'=2,'c'=2] {'xh','xl',..., dimensions={0} | all-to-all | bytes 2162688 | tf_op jit(solution)/shard_map/all_to_all | solution.py:382
  45.5 0.1 reduce_sum.12
  45.7 2.5 %collective-permute-start.4 = (bf16[264,128]{1,0:T(8,128)(2,1)S(1)}, bf16[264,128]{1,0:T(8,128)(2,1)S(1)}, u32[]{:S(2)}, u32[]{:S(2)}) collective-permute-start(bf16[264,128]{1,0:T(8,128)(2,1)S(1)} %reduce_sum.12), channel_id=1, source_target_pairs={{0,48},{1,49},{2,50},{3,51},{4,52},{5,53},{6,54},{7,55},{8,56},{9,... | collective-permute-start | bytes 202760 | tf_op jit(solution)/shard_map/ppermute | solution.py:376
  48.1 2.0 %collective-permute-done.4 = bf16[264,128]{1,0:T(8,128)(2,1)S(1)} collective-permute-done((bf16[264,128]{1,0:T(8,128)(2,1)S(1)}, bf16[264,128]{1,0:T(8,128)(2,1)S(1)}, u32[]{:S(2)}, u32[]{:S(2)}) %collective-permute-start.4) | collective-permute-done | bytes 67616 | tf_op jit(solution)/shard_map/ppermute | solution.py:376
  50.1 2.8 %collective-permute-start.5 = (bf16[264,128]{1,0:T(8,128)(2,1)S(1)}, bf16[264,128]{1,0:T(8,128)(2,1)S(1)}, u32[]{:S(2)}, u32[]{:S(2)}) collective-permute-start(bf16[264,128]{1,0:T(8,128)(2,1)S(1)} %add_convert_fusion.2), channel_id=1, source_target_pairs={{0,4},{1,5},{2,6},{3,7},{4,0},{5,1},{6,2},{7,3},{8,12},{9,13},{10,... | collective-permute-start | bytes 202760 | tf_op jit(solution)/shard_map/ppermute | solution.py:376
  53.0 2.6 %collective-permute-start.7 = (bf16[2,168,512]{2,1,0:T(8,128)(2,1)S(1)}, bf16[2,168,512]{2,1,0:T(8,128)(2,1)S(1)}, u32[]{:S(2)}, u32[]{:S(2)}) collective-permute-start(bf16[2,168,512]{2,1,0:T(8,128)(2,1)S(1)} %get-tuple-element.54), channel_id=1, source_target_pairs={{0,32},{1,33},{2,34},{3,35},{4,36},{5,37},{6,38},{7,39},{8,40},{9,... | collective-permute-start | bytes 1032200 | tf_op jit(solution)/shard_map/ppermute | solution.py:376
  55.5 0.0 collective-permute-done.5
  55.5 4.3 %collective-permute-start.6 = (bf16[264,128]{1,0:T(8,128)(2,1)S(1)}, bf16[264,128]{1,0:T(8,128)(2,1)S(1)}, u32[]{:S(2)}, u32[]{:S(2)}) collective-permute-start(bf16[264,128]{1,0:T(8,128)(2,1)S(1)} %add_convert_fusion.1), channel_id=1, source_target_pairs={{0,12},{1,13},{2,14},{3,15},{4,8},{5,9},{6,10},{7,11},{8,4},{9,5},... | collective-permute-start | bytes 202760 | tf_op jit(solution)/shard_map/ppermute | solution.py:376
  59.8 2.8 %collective-permute-done.7.came_ref = bf16[2,168,512]{2,1,0:T(8,128)(2,1)S(1)} collective-permute-done((bf16[2,168,512]{2,1,0:T(8,128)(2,1)S(1)}, bf16[2,168,512]{2,1,0:T(8,128)(2,1)S(1)}, u32[]{:S(2)}, u32[]{:S(2)}) %collective-permute-start.7) | collective-permute-done | bytes 344096 | tf_op jit(solution)/shard_map/ppermute | solution.py:376
  62.7 0.0 collective-permute-done.6
  62.7 1.1 %broadcast_in_dim.3 = bf16[16,264,128]{2,1,0:T(8,128)(2,1)} broadcast(bf16[264,128]{1,0:T(8,128)(2,1)S(1)} %add_convert_fusion), dimensions={1,2} | broadcast | bytes 1148928 | tf_op jit(solution)/shard_map/broadcast_in_dim | solution.py:389
  63.8 3.7 %all-to-all-start.1 = ((bf16[16,264,128]{2,1,0:T(8,128)(2,1)}), bf16[16,264,128]{2,1,0:T(8,128)(2,1)S(1)}, u32[]{:S(2)}, u32[]{:S(2)}) async-start(bf16[16,264,128]{2,1,0:T(8,128)(2,1)} %broadcast_in_dim.3), calls=%async_computation.1 | async-start | bytes 2162688 | tf_op jit(solution)/shard_map/all_to_all | solution.py:389
  67.5 8.2 %collective-permute-start.8 = (bf16[2,48,512]{2,1,0:T(8,128)(2,1)S(1)}, bf16[2,48,512]{2,1,0:T(8,128)(2,1)S(1)}, u32[]{:S(2)}, u32[]{:S(2)}) collective-permute-start(bf16[2,48,512]{2,1,0:T(8,128)(2,1)S(1)} %shard_map.97), channel_id=1, source_target_pairs={{0,1},{1,2},{2,3},{3,4},{4,5},{5,6},{6,7},{7,8},{8,9},{9,10},{10,1... | collective-permute-start | bytes 294920 | tf_op jit(solution)/shard_map/ppermute | solution.py:376
  75.7 2.7 %collective-permute-done.8.edge_ref = bf16[2,48,512]{2,1,0:T(8,128)(2,1)S(1)} collective-permute-done((bf16[2,48,512]{2,1,0:T(8,128)(2,1)S(1)}, bf16[2,48,512]{2,1,0:T(8,128)(2,1)S(1)}, u32[]{:S(2)}, u32[]{:S(2)}) %collective-permute-start.8) | collective-permute-done | bytes 98336 | tf_op jit(solution)/shard_map/ppermute | solution.py:376
  78.4 0.9 shard_map.98
  79.2 0.0 all-to-all-done.1.half_ref.refs_0_
  79.2 6.5 %collective-permute-start.9 = (bf16[16,264,128]{2,1,0:T(8,128)(2,1)S(1)}, bf16[16,264,128]{2,1,0:T(8,128)(2,1)S(1)}, u32[]{:S(2)}, u32[]{:S(2)}) collective-permute-start(bf16[16,264,128]{2,1,0:T(8,128)(2,1)S(1)} %all-to-all-done.1.half_ref.refs_0_), channel_id=1, source_target_pairs={{0,1},{1,0},{2,3},{3,2},{4,5},{5,4},{6,7},{7,6},{8,9},{9,8},{10,11... | collective-permute-start | bytes 3244040 | tf_op jit(solution)/shard_map/ppermute | solution.py:376
  85.7 1.4 %shard_map.99 = (f32[512,1536]{1,0:T(8,128)}, f32[512,512]{1,0:T(8,128)}) custom-call(bf16[16,264,128]{2,1,0:T(8,128)(2,1)S(1)} %all-to-all-done.1.half_ref.refs_0_), custom_call_target="tpu_custom_call" | custom-call | flops 1000000 | bytes 3000000 | tf_op jit(solution)/shard_map/pallas_call | solution.py:339
  87.1 0.9 %collective-permute-done.9.half_ref = bf16[16,264,128]{2,1,0:T(8,128)(2,1)S(1)} collective-permute-done((bf16[16,264,128]{2,1,0:T(8,128)(2,1)S(1)}, bf16[16,264,128]{2,1,0:T(8,128)(2,1)S(1)}, u32[]{:S(2)}, u32[]{:S(2)}) %collective-permute-start.9) | collective-permute-done | bytes 1081376 | tf_op jit(solution)/shard_map/ppermute | solution.py:376
  88.0 1.4 %shard_map.100 = (f32[512,1536]{1,0:T(8,128)}, f32[512,512]{1,0:T(8,128)}, f32[1,512]{1,0:T(1,128)}) custom-call(bf16[16,264,128]{2,1,0:T(8,128)(2,1)S(1)} %collective-permute-done.9.half_ref, bf16[16,264,128]{2,1,0:T(8,128)(2,1)S(1)} %all-to-all-done.1.half_ref.refs_0_, ...), custom_call_target="tpu_custom_call", output_to_operand_aliasing={{0}: (2, {}), {1}: (3, {})} | custom-call | flops 1000000 | bytes 3000000 | tf_op jit(solution)/shard_map/pallas_call | solution.py:339
  (9 shorter events, 0.2 us)
Async XLA Ops:
  0.6 7.2 %copy-start.3 = (bf16[6,48,512]{2,1,0:T(8,128)(2,1)S(1)}, bf16[6,48,512]{2,1,0:T(8,128)(2,1)}, u32[]{:S(2)}) copy-start(bf16[6,48,512]{2,1,0:T(8,128)(2,1)} %param.9) | copy-start | bytes 884740
  0.6 7.2 %copy-start.2 = (bf16[6,48,512]{2,1,0:T(8,128)(2,1)S(1)}, bf16[6,48,512]{2,1,0:T(8,128)(2,1)}, u32[]{:S(2)}) copy-start(bf16[6,48,512]{2,1,0:T(8,128)(2,1)} %param.5) | copy-start | bytes 884740
  0.7 14.9 %copy-start.1 = (bf16[512,512]{1,0:T(8,128)(2,1)S(1)}, bf16[512,512]{1,0:T(8,128)(2,1)}, u32[]{:S(2)}) copy-start(bf16[512,512]{1,0:T(8,128)(2,1)} %w_out_ref.1) | copy-start | bytes 1572868
  1.8 13.8 %copy-start = (bf16[512,1536]{1,0:T(8,128)(2,1)S(1)}, bf16[512,1536]{1,0:T(8,128)(2,1)}, u32[]{:S(2)}) copy-start(bf16[512,1536]{1,0:T(8,128)(2,1)} %w_qkv_ref.1) | copy-start | bytes 4718596
  1.8 14.9 %collective-permute-start = (bf16[2,144,512]{2,1,0:T(8,128)(2,1)S(1)}, bf16[2,144,512]{2,1,0:T(8,128)(2,1)S(1)}, u32[]{:S(2)}, u32[]{:S(2)}) collective-permute-start(bf16[2,144,512]{2,1,0:T(8,128)(2,1)S(1)} %pad_maximum_fusion), channel_id=1, source_target_pairs={{0,224},{1,225},{2,226},{3,227},{4,228},{5,229},{6,230},{7,231},{8... | collective-permute-start | bytes 884744 | tf_op jit(solution)/shard_map/ppermute | solution.py:376
  7.9 8.8 %copy-start.4 = (f32[512]{0:T(512)S(1)}, f32[512]{0:T(512)}, u32[]{:S(2)}) copy-start(f32[512]{0:T(512)} %param.6) | copy-start | bytes 6148
  8.0 7.8 %collective-permute-start.1 = (bf16[2,24,512]{2,1,0:T(8,128)(2,1)S(1)}, bf16[2,24,512]{2,1,0:T(8,128)(2,1)S(1)}, u32[]{:S(2)}, u32[]{:S(2)}) collective-permute-start(bf16[2,24,512]{2,1,0:T(8,128)(2,1)S(1)} %get-tuple-element.37), channel_id=1, source_target_pairs={{0,31},{1,0},{2,1},{3,2},{4,3},{5,4},{6,5},{7,6},{8,7},{9,8},{10,9... | collective-permute-start | bytes 147464 | tf_op jit(solution)/shard_map/ppermute | solution.py:376
  9.0 7.8 %collective-permute-start.2 = (bf16[2,24,512]{2,1,0:T(8,128)(2,1)S(1)}, bf16[2,24,512]{2,1,0:T(8,128)(2,1)S(1)}, u32[]{:S(2)}, u32[]{:S(2)}) collective-permute-start(bf16[2,24,512]{2,1,0:T(8,128)(2,1)S(1)} %get-tuple-element.38), channel_id=1, source_target_pairs={{0,255},{1,224},{2,225},{3,226},{4,227},{5,228},{6,229},{7,230},{8... | collective-permute-start | bytes 147464 | tf_op jit(solution)/shard_map/ppermute | solution.py:376
  22.4 4.8 %collective-permute-start.3 = (bf16[4096,128]{1,0:T(8,128)(2,1)S(1)}, bf16[4096,128]{1,0:T(8,128)(2,1)S(1)}, u32[]{:S(2)}, u32[]{:S(2)}) collective-permute-start(bf16[4096,128]{1,0:T(8,128)(2,1)S(1)} %get-tuple-element.42), channel_id=1, source_target_pairs={{0,1},{1,0},{2,3},{3,2},{4,5},{5,4},{6,7},{7,6},{8,9},{9,8},{10,11... | collective-permute-start | bytes 3145736 | tf_op jit(solution)/shard_map/ppermute | solution.py:376
  45.7 4.4 %collective-permute-start.4 = (bf16[264,128]{1,0:T(8,128)(2,1)S(1)}, bf16[264,128]{1,0:T(8,128)(2,1)S(1)}, u32[]{:S(2)}, u32[]{:S(2)}) collective-permute-start(bf16[264,128]{1,0:T(8,128)(2,1)S(1)} %reduce_sum.12), channel_id=1, source_target_pairs={{0,48},{1,49},{2,50},{3,51},{4,52},{5,53},{6,54},{7,55},{8,56},{9,... | collective-permute-start | bytes 202760 | tf_op jit(solution)/shard_map/ppermute | solution.py:376
  50.1 5.4 %collective-permute-start.5 = (bf16[264,128]{1,0:T(8,128)(2,1)S(1)}, bf16[264,128]{1,0:T(8,128)(2,1)S(1)}, u32[]{:S(2)}, u32[]{:S(2)}) collective-permute-start(bf16[264,128]{1,0:T(8,128)(2,1)S(1)} %add_convert_fusion.2), channel_id=1, source_target_pairs={{0,4},{1,5},{2,6},{3,7},{4,0},{5,1},{6,2},{7,3},{8,12},{9,13},{10,... | collective-permute-start | bytes 202760 | tf_op jit(solution)/shard_map/ppermute | solution.py:376
  53.0 9.7 %collective-permute-start.7 = (bf16[2,168,512]{2,1,0:T(8,128)(2,1)S(1)}, bf16[2,168,512]{2,1,0:T(8,128)(2,1)S(1)}, u32[]{:S(2)}, u32[]{:S(2)}) collective-permute-start(bf16[2,168,512]{2,1,0:T(8,128)(2,1)S(1)} %get-tuple-element.54), channel_id=1, source_target_pairs={{0,32},{1,33},{2,34},{3,35},{4,36},{5,37},{6,38},{7,39},{8,40},{9,... | collective-permute-start | bytes 1032200 | tf_op jit(solution)/shard_map/ppermute | solution.py:376
  55.5 7.1 %collective-permute-start.6 = (bf16[264,128]{1,0:T(8,128)(2,1)S(1)}, bf16[264,128]{1,0:T(8,128)(2,1)S(1)}, u32[]{:S(2)}, u32[]{:S(2)}) collective-permute-start(bf16[264,128]{1,0:T(8,128)(2,1)S(1)} %add_convert_fusion.1), channel_id=1, source_target_pairs={{0,12},{1,13},{2,14},{3,15},{4,8},{5,9},{6,10},{7,11},{8,4},{9,5},... | collective-permute-start | bytes 202760 | tf_op jit(solution)/shard_map/ppermute | solution.py:376
  63.8 15.4 %all-to-all-start.1 = ((bf16[16,264,128]{2,1,0:T(8,128)(2,1)}), bf16[16,264,128]{2,1,0:T(8,128)(2,1)S(1)}, u32[]{:S(2)}, u32[]{:S(2)}) async-start(bf16[16,264,128]{2,1,0:T(8,128)(2,1)} %broadcast_in_dim.3), calls=%async_computation.1 | async-start | bytes 2162688 | tf_op jit(solution)/shard_map/all_to_all | solution.py:389
  67.5 10.8 %collective-permute-start.8 = (bf16[2,48,512]{2,1,0:T(8,128)(2,1)S(1)}, bf16[2,48,512]{2,1,0:T(8,128)(2,1)S(1)}, u32[]{:S(2)}, u32[]{:S(2)}) collective-permute-start(bf16[2,48,512]{2,1,0:T(8,128)(2,1)S(1)} %shard_map.97), channel_id=1, source_target_pairs={{0,1},{1,2},{2,3},{3,4},{4,5},{5,6},{6,7},{7,8},{8,9},{9,10},{10,1... | collective-permute-start | bytes 294920 | tf_op jit(solution)/shard_map/ppermute | solution.py:376
  79.2 8.8 %collective-permute-start.9 = (bf16[16,264,128]{2,1,0:T(8,128)(2,1)S(1)}, bf16[16,264,128]{2,1,0:T(8,128)(2,1)S(1)}, u32[]{:S(2)}, u32[]{:S(2)}) collective-permute-start(bf16[16,264,128]{2,1,0:T(8,128)(2,1)S(1)} %all-to-all-done.1.half_ref.refs_0_), channel_id=1, source_target_pairs={{0,1},{1,0},{2,3},{3,2},{4,5},{5,4},{6,7},{7,6},{8,9},{9,8},{10,11... | collective-permute-start | bytes 3244040 | tf_op jit(solution)/shard_map/ppermute | solution.py:376

commit v8 on v6

--- a/solution.py
+++ b/solution.py
@@ -300,23 +300,23 @@
     low = core == side
 
     def store(start):
-        for block in range(4):
-            cols = slice(block * 256, (block + 1) * 256)
+        for block in range(8):
+            cols = slice(block * 128, (block + 1) * 128)
             if start:
-                for k in range(4 * block, 4 * block + 4):
+                for k in range(2 * block, 2 * block + 2):
                     at = slice(k // 2 * 128, (k // 2 + 1) * 128)
                     wide_s[k % 2 * CHUNK : (k % 2 + 1) * CHUNK, at] = half_ref[moved_chunk(k), :CHUNK].astype(f32)
 
             def copy(ref, first):
-                to = ref.at[:, first : first + 256]
+                to = ref.at[:, first : first + 128]
                 move = pltpu.make_async_copy(wide_s.at[:, cols], to, sems.at[block])
                 move.start() if start else move.wait()
 
-            pl.when(low)(lambda: copy(qkv_ref, block * 256))
-            if block < 2:
-                pl.when(jnp.logical_not(low))(lambda: copy(qkv_ref, 2 * D + block * 256))
+            pl.when(low)(lambda: copy(qkv_ref, block * 128))
+            if block < 4:
+                pl.when(jnp.logical_not(low))(lambda: copy(qkv_ref, 2 * D + block * 128))
             else:
-                pl.when(jnp.logical_not(low))(lambda: copy(out_ref, block * 256 - D))
+                pl.when(jnp.logical_not(low))(lambda: copy(out_ref, block * 128 - D))
 
     if side:
         own_ref, gain_ref, gain_s, gain_sem = refs[0], refs[5], *refs[6:8]
@@ -342,7 +342,7 @@
         in_specs=[whole] + [whole, stay, stay] * side,
         out_specs=[stay] * (2 + side),
         scratch_shapes=[pltpu.VMEM((1, D), f32), pltpu.SemaphoreType.DMA] * side
-        + [pltpu.VMEM((D, 2 * D), f32), pltpu.SemaphoreType.DMA((4,))],
+        + [pltpu.VMEM((D, 2 * D), f32), pltpu.SemaphoreType.DMA((8,))],
         input_output_aliases={2: 0, 3: 1} if side else {},
         compiler_params=pltpu.CompilerParams(vmem_limit_bytes=12 * 1024 * 1024),
         cost_estimate=pl.CostEstimate(flops=1_000_000, bytes_accessed=3_000_000, transcendentals=0),

time: 89.4 us -> 89.4 us (level)
  no operation moved by 1% of the time
where the time goes in v8:
time: 89.4 us; the launch traced here: 89.2 us
  starting transfers between devices  46.5 us (52%)
  blocking collectives  17 us (19%)
  Pallas kernels  12 us (13%)
  waiting for transfers between devices  10.2 us (11%)
  local copies, waits for them, and re-layouts  2.26 us (3%)
  between operations  0.96 us (1%)
    ppermute x10, starting transfers between devices, send(): return lax.ppermute(value, ALL, pairs)  42.8 us
    all_to_all x1, blocking collectives, sum_and_return(): pieces = lax.all_to_all(chunks, BOX, 0, 0, tiled=True)  17 us
    ppermute x10, waiting for transfers between devices, send(): return lax.ppermute(value, ALL, pairs)  10.2 us
    pallas_call x1, Pallas kernels, block(): vmem_call(functools.partial(attend_kernel, where_am_i), [shape(STRIP, 128...  5.69 us
    all_to_all x1, starting transfers between devices, sum_and_return(): lax.all_to_all(jnp.broadcast_to(total, (16, SUMMED, 128)), BOX, 0, 0, til...  3.7 us
    pallas_call x2, Pallas kernels, unpack(): pl.pallas_call(functools.partial(unpack_kernel, where_am_i, side), out_sh...  2.83 us
    pallas_call x1, Pallas kernels, block(): vmem_call(functools.partial(finish_kernel, where_am_i), FINISHED, [], 150...  2.09 us
  transfers between devices with their start and end apart: 11, of which 7 were waited for; matrix products, arithmetic and copies ran while one was open for 0% of the time, Pallas kernels for 5%

profile of v8, /device:TPU:1, one launch (start us, length us, event | category | flops | bytes accessed | tf_op | source)
XLA Modules:
  0.0 89.2 jit_solution(12368266946671557563)
XLA Ops:
  0.6 0.0 copy-start.3
  0.6 0.0 copy-start.2
  0.7 0.0 copy-start.1
  0.7 1.1 %slice_bitcast_fusion.2 = (bf16[1,3,48,512]{3,2,1,0:T(8,128)(2,1)S(1)}, bf16[3,48,512]{2,1,0:T(8,128)(2,1)S(1)}, bf16[3,48,512]{2,1,0:T(8,128)(2,1)S(1)}, bf16[1,3,48,512]{3,2,1,0:T(8,128)(2,1)S(1)}) fusion(bf16[6,48,512]{2,1,0:T(8,128)(2,1)} %param.9, bf16[6,48,512]{2,1,0:T(8,128)(2,1)} %param.5), kind=kLoop, calls=%fused_computation.8 | loop fusion | bytes 884736 | tf_op jit(solution)/shard_map/stack | solution.py:402
  1.8 0.0 copy-start
  1.8 6.0 %collective-permute-start = (bf16[2,144,512]{2,1,0:T(8,128)(2,1)S(1)}, bf16[2,144,512]{2,1,0:T(8,128)(2,1)S(1)}, u32[]{:S(2)}, u32[]{:S(2)}) collective-permute-start(bf16[2,144,512]{2,1,0:T(8,128)(2,1)S(1)} %pad_maximum_fusion), channel_id=1, source_target_pairs={{0,224},{1,225},{2,226},{3,227},{4,228},{5,229},{6,230},{7,231},{8... | collective-permute-start | bytes 884744 | tf_op jit(solution)/shard_map/ppermute | solution.py:376
  7.8 0.0 copy-done.3
  7.8 0.0 copy-done.2
  7.9 0.0 copy-start.4
  8.0 1.0 %collective-permute-start.1 = (bf16[2,24,512]{2,1,0:T(8,128)(2,1)S(1)}, bf16[2,24,512]{2,1,0:T(8,128)(2,1)S(1)}, u32[]{:S(2)}, u32[]{:S(2)}) collective-permute-start(bf16[2,24,512]{2,1,0:T(8,128)(2,1)S(1)} %get-tuple-element.37), channel_id=1, source_target_pairs={{0,31},{1,0},{2,1},{3,2},{4,3},{5,4},{6,5},{7,6},{8,7},{9,8},{10,9... | collective-permute-start | bytes 147464 | tf_op jit(solution)/shard_map/ppermute | solution.py:376
  9.0 6.6 %collective-permute-start.2 = (bf16[2,24,512]{2,1,0:T(8,128)(2,1)S(1)}, bf16[2,24,512]{2,1,0:T(8,128)(2,1)S(1)}, u32[]{:S(2)}, u32[]{:S(2)}) collective-permute-start(bf16[2,24,512]{2,1,0:T(8,128)(2,1)S(1)} %get-tuple-element.38), channel_id=1, source_target_pairs={{0,255},{1,224},{2,225},{3,226},{4,227},{5,228},{6,229},{7,230},{8... | collective-permute-start | bytes 147464 | tf_op jit(solution)/shard_map/ppermute | solution.py:376
  15.6 0.0 copy-done.1
  15.6 0.0 copy-done
  15.6 0.2 shard_map.93
  15.7 0.0 collective-permute-done.1.halo_lon_ref
  15.7 1.0 %collective-permute-done.2.halo_cor_ref = bf16[2,24,512]{2,1,0:T(8,128)(2,1)S(1)} collective-permute-done((bf16[2,24,512]{2,1,0:T(8,128)(2,1)S(1)}, bf16[2,24,512]{2,1,0:T(8,128)(2,1)S(1)}, u32[]{:S(2)}, u32[]{:S(2)}) %collective-permute-start.2) | collective-permute-done | bytes 49184 | tf_op jit(solution)/shard_map/ppermute | solution.py:376
  16.7 0.0 collective-permute-done.halo_lat_ref
  16.7 0.0 copy-done.4
  16.7 5.7 %shard_map.94 = (bf16[4096,128]{1,0:T(8,128)(2,1)S(1)}, bf16[320,512]{1,0:T(8,128)(2,1)S(1)}, bf16[320,512]{1,0:T(8,128)(2,1)S(1)}, bf16[320,512]{1,0:T(8,128)(2...) custom-call(bf16[288,512]{1,0:T(8,128)(2,1)S(1)} %bitcast.16, bf16[288,512]{1,0:T(8,128)(2,1)S(1)} %bitcast.17, ...), custom_call_target="tpu_custom_call" | custom-call | flops 5000000000 | bytes 8000000 | tf_op jit(solution)/shard_map/pallas_call | solution.py:237
  22.4 2.5 %collective-permute-start.3 = (bf16[4096,128]{1,0:T(8,128)(2,1)S(1)}, bf16[4096,128]{1,0:T(8,128)(2,1)S(1)}, u32[]{:S(2)}, u32[]{:S(2)}) collective-permute-start(bf16[4096,128]{1,0:T(8,128)(2,1)S(1)} %get-tuple-element.42), channel_id=1, source_target_pairs={{0,1},{1,0},{2,3},{3,2},{4,5},{5,4},{6,7},{7,6},{8,9},{9,8},{10,11... | collective-permute-start | bytes 3145736 | tf_op jit(solution)/shard_map/ppermute | solution.py:376
  24.9 2.1 %shard_map.95 = (bf16[2,144,512]{2,1,0:T(8,128)(2,1)S(1)}, bf16[2,168,512]{2,1,0:T(8,128)(2,1)S(1)}, bf16[2,24,512]{2,1,0:T(8,128)(2,1)S(1)}, bf16[8,128]{1,0:T(8,128)(2,1)S(1)}, bf16[4096,128]{1,0:T(8,128)(2,1)S(1)}) custom-call(bf16[320,512]{1,0:T(8,128)(2,1)S(1)} %get-tuple-element.43.refs_0_, bf16[320,512]{1,0:T(8,128)(2,1)S(1)} %get-tuple-element.44.refs_1_, ...), custom_call_target="tpu_custom_call" | custom-call | flops 1500000000 | bytes 4000000 | tf_op jit(solution)/shard_map/pallas_call | solution.py:247
  27.0 0.2 collective-permute-done.3.arrived_ref
  27.2 0.3 shard_map.96
  27.5 17.0 %all_to_all.10 = bf16[16,264,128]{2,1,0:T(8,128)(2,1)S(1)} all-to-all(bf16[16,264,128]{2,1,0:T(8,128)(2,1)S(1)} %get-tuple-element.53), channel_id=1, replica_groups=mesh['xh'=2,'xl'=2,'yh'=2,'yl'=2,'zh'=2,'zm'=2,'zl'=2,'c'=2] {'xl','yh',..., dimensions={0} | all-to-all | bytes 2162688 | tf_op jit(solution)/shard_map/all_to_all | solution.py:382
  44.6 0.1 reduce_sum.12
  44.7 2.9 %collective-permute-start.4 = (bf16[264,128]{1,0:T(8,128)(2,1)S(1)}, bf16[264,128]{1,0:T(8,128)(2,1)S(1)}, u32[]{:S(2)}, u32[]{:S(2)}) collective-permute-start(bf16[264,128]{1,0:T(8,128)(2,1)S(1)} %reduce_sum.12), channel_id=1, source_target_pairs={{0,192},{1,193},{2,194},{3,195},{4,196},{5,197},{6,198},{7,199},{8... | collective-permute-start | bytes 202760 | tf_op jit(solution)/shard_map/ppermute | solution.py:376
  47.6 1.7 %collective-permute-done.4 = bf16[264,128]{1,0:T(8,128)(2,1)S(1)} collective-permute-done((bf16[264,128]{1,0:T(8,128)(2,1)S(1)}, bf16[264,128]{1,0:T(8,128)(2,1)S(1)}, u32[]{:S(2)}, u32[]{:S(2)}) %collective-permute-start.4) | collective-permute-done | bytes 67616 | tf_op jit(solution)/shard_map/ppermute | solution.py:376
  49.3 3.1 %collective-permute-start.5 = (bf16[264,128]{1,0:T(8,128)(2,1)S(1)}, bf16[264,128]{1,0:T(8,128)(2,1)S(1)}, u32[]{:S(2)}, u32[]{:S(2)}) collective-permute-start(bf16[264,128]{1,0:T(8,128)(2,1)S(1)} %add_convert_fusion.2), channel_id=1, source_target_pairs={{0,4},{1,5},{2,6},{3,7},{4,0},{5,1},{6,2},{7,3},{8,12},{9,13},{10,... | collective-permute-start | bytes 202760 | tf_op jit(solution)/shard_map/ppermute | solution.py:376
  52.4 1.2 %collective-permute-start.7 = (bf16[2,168,512]{2,1,0:T(8,128)(2,1)S(1)}, bf16[2,168,512]{2,1,0:T(8,128)(2,1)S(1)}, u32[]{:S(2)}, u32[]{:S(2)}) collective-permute-start(bf16[2,168,512]{2,1,0:T(8,128)(2,1)S(1)} %get-tuple-element.54), channel_id=1, source_target_pairs={{0,32},{1,33},{2,34},{3,35},{4,36},{5,37},{6,38},{7,39},{8,40},{9,... | collective-permute-start | bytes 1032200 | tf_op jit(solution)/shard_map/ppermute | solution.py:376
  53.6 1.2 %collective-permute-done.5 = bf16[264,128]{1,0:T(8,128)(2,1)S(1)} collective-permute-done((bf16[264,128]{1,0:T(8,128)(2,1)S(1)}, bf16[264,128]{1,0:T(8,128)(2,1)S(1)}, u32[]{:S(2)}, u32[]{:S(2)}) %collective-permute-start.5) | collective-permute-done | bytes 67616 | tf_op jit(solution)/shard_map/ppermute | solution.py:376
  54.8 4.7 %collective-permute-start.6 = (bf16[264,128]{1,0:T(8,128)(2,1)S(1)}, bf16[264,128]{1,0:T(8,128)(2,1)S(1)}, u32[]{:S(2)}, u32[]{:S(2)}) collective-permute-start(bf16[264,128]{1,0:T(8,128)(2,1)S(1)} %add_convert_fusion.1), channel_id=1, source_target_pairs={{0,12},{1,13},{2,14},{3,15},{4,8},{5,9},{6,10},{7,11},{8,4},{9,5},... | collective-permute-start | bytes 202760 | tf_op jit(solution)/shard_map/ppermute | solution.py:376
  59.4 2.6 %collective-permute-done.7.came_ref = bf16[2,168,512]{2,1,0:T(8,128)(2,1)S(1)} collective-permute-done((bf16[2,168,512]{2,1,0:T(8,128)(2,1)S(1)}, bf16[2,168,512]{2,1,0:T(8,128)(2,1)S(1)}, u32[]{:S(2)}, u32[]{:S(2)}) %collective-permute-start.7) | collective-permute-done | bytes 344096 | tf_op jit(solution)/shard_map/ppermute | solution.py:376
  62.1 0.0 collective-permute-done.6
  62.1 1.1 %broadcast_in_dim.3 = bf16[16,264,128]{2,1,0:T(8,128)(2,1)} broadcast(bf16[264,128]{1,0:T(8,128)(2,1)S(1)} %add_convert_fusion), dimensions={1,2} | broadcast | bytes 1148928 | tf_op jit(solution)/shard_map/broadcast_in_dim | solution.py:389
  63.2 3.7 %all-to-all-start.1 = ((bf16[16,264,128]{2,1,0:T(8,128)(2,1)}), bf16[16,264,128]{2,1,0:T(8,128)(2,1)S(1)}, u32[]{:S(2)}, u32[]{:S(2)}) async-start(bf16[16,264,128]{2,1,0:T(8,128)(2,1)} %broadcast_in_dim.3), calls=%async_computation.1 | async-start | bytes 2162688 | tf_op jit(solution)/shard_map/all_to_all | solution.py:389
  66.9 7.8 %collective-permute-start.8 = (bf16[2,48,512]{2,1,0:T(8,128)(2,1)S(1)}, bf16[2,48,512]{2,1,0:T(8,128)(2,1)S(1)}, u32[]{:S(2)}, u32[]{:S(2)}) collective-permute-start(bf16[2,48,512]{2,1,0:T(8,128)(2,1)S(1)} %shard_map.97), channel_id=1, source_target_pairs={{0,1},{1,2},{2,3},{3,4},{4,5},{5,6},{6,7},{7,8},{8,9},{9,10},{10,1... | collective-permute-start | bytes 294920 | tf_op jit(solution)/shard_map/ppermute | solution.py:376
  74.7 2.6 %collective-permute-done.8.edge_ref = bf16[2,48,512]{2,1,0:T(8,128)(2,1)S(1)} collective-permute-done((bf16[2,48,512]{2,1,0:T(8,128)(2,1)S(1)}, bf16[2,48,512]{2,1,0:T(8,128)(2,1)S(1)}, u32[]{:S(2)}, u32[]{:S(2)}) %collective-permute-start.8) | collective-permute-done | bytes 98336 | tf_op jit(solution)/shard_map/ppermute | solution.py:376
  77.3 0.9 shard_map.98
  78.2 0.0 all-to-all-done.1.half_ref.refs_0_
  78.2 7.1 %collective-permute-start.9 = (bf16[16,264,128]{2,1,0:T(8,128)(2,1)S(1)}, bf16[16,264,128]{2,1,0:T(8,128)(2,1)S(1)}, u32[]{:S(2)}, u32[]{:S(2)}) collective-permute-start(bf16[16,264,128]{2,1,0:T(8,128)(2,1)S(1)} %all-to-all-done.1.half_ref.refs_0_), channel_id=1, source_target_pairs={{0,1},{1,0},{2,3},{3,2},{4,5},{5,4},{6,7},{7,6},{8,9},{9,8},{10,11... | collective-permute-start | bytes 3244040 | tf_op jit(solution)/shard_map/ppermute | solution.py:376
  85.3 1.4 %shard_map.99 = (f32[512,1536]{1,0:T(8,128)}, f32[512,512]{1,0:T(8,128)}) custom-call(bf16[16,264,128]{2,1,0:T(8,128)(2,1)S(1)} %all-to-all-done.1.half_ref.refs_0_), custom_call_target="tpu_custom_call" | custom-call | flops 1000000 | bytes 3000000 | tf_op jit(solution)/shard_map/pallas_call | solution.py:339
  86.7 0.9 %collective-permute-done.9.half_ref = bf16[16,264,128]{2,1,0:T(8,128)(2,1)S(1)} collective-permute-done((bf16[16,264,128]{2,1,0:T(8,128)(2,1)S(1)}, bf16[16,264,128]{2,1,0:T(8,128)(2,1)S(1)}, u32[]{:S(2)}, u32[]{:S(2)}) %collective-permute-start.9) | collective-permute-done | bytes 1081376 | tf_op jit(solution)/shard_map/ppermute | solution.py:376
  87.6 1.4 %shard_map.100 = (f32[512,1536]{1,0:T(8,128)}, f32[512,512]{1,0:T(8,128)}, f32[1,512]{1,0:T(1,128)}) custom-call(bf16[16,264,128]{2,1,0:T(8,128)(2,1)S(1)} %collective-permute-done.9.half_ref, bf16[16,264,128]{2,1,0:T(8,128)(2,1)S(1)} %all-to-all-done.1.half_ref.refs_0_, ...), custom_call_target="tpu_custom_call", output_to_operand_aliasing={{0}: (2, {}), {1}: (3, {})} | custom-call | flops 1000000 | bytes 3000000 | tf_op jit(solution)/shard_map/pallas_call | solution.py:339
  (9 shorter events, 0.2 us)
Async XLA Ops:
  0.6 7.2 %copy-start.3 = (bf16[6,48,512]{2,1,0:T(8,128)(2,1)S(1)}, bf16[6,48,512]{2,1,0:T(8,128)(2,1)}, u32[]{:S(2)}) copy-start(bf16[6,48,512]{2,1,0:T(8,128)(2,1)} %param.9) | copy-start | bytes 884740
  0.6 7.2 %copy-start.2 = (bf16[6,48,512]{2,1,0:T(8,128)(2,1)S(1)}, bf16[6,48,512]{2,1,0:T(8,128)(2,1)}, u32[]{:S(2)}) copy-start(bf16[6,48,512]{2,1,0:T(8,128)(2,1)} %param.5) | copy-start | bytes 884740
  0.7 14.9 %copy-start.1 = (bf16[512,512]{1,0:T(8,128)(2,1)S(1)}, bf16[512,512]{1,0:T(8,128)(2,1)}, u32[]{:S(2)}) copy-start(bf16[512,512]{1,0:T(8,128)(2,1)} %w_out_ref.1) | copy-start | bytes 1572868
  1.8 13.8 %copy-start = (bf16[512,1536]{1,0:T(8,128)(2,1)S(1)}, bf16[512,1536]{1,0:T(8,128)(2,1)}, u32[]{:S(2)}) copy-start(bf16[512,1536]{1,0:T(8,128)(2,1)} %w_qkv_ref.1) | copy-start | bytes 4718596
  1.8 14.9 %collective-permute-start = (bf16[2,144,512]{2,1,0:T(8,128)(2,1)S(1)}, bf16[2,144,512]{2,1,0:T(8,128)(2,1)S(1)}, u32[]{:S(2)}, u32[]{:S(2)}) collective-permute-start(bf16[2,144,512]{2,1,0:T(8,128)(2,1)S(1)} %pad_maximum_fusion), channel_id=1, source_target_pairs={{0,224},{1,225},{2,226},{3,227},{4,228},{5,229},{6,230},{7,231},{8... | collective-permute-start | bytes 884744 | tf_op jit(solution)/shard_map/ppermute | solution.py:376
  7.9 8.8 %copy-start.4 = (f32[512]{0:T(512)S(1)}, f32[512]{0:T(512)}, u32[]{:S(2)}) copy-start(f32[512]{0:T(512)} %param.6) | copy-start | bytes 6148
  8.0 7.8 %collective-permute-start.1 = (bf16[2,24,512]{2,1,0:T(8,128)(2,1)S(1)}, bf16[2,24,512]{2,1,0:T(8,128)(2,1)S(1)}, u32[]{:S(2)}, u32[]{:S(2)}) collective-permute-start(bf16[2,24,512]{2,1,0:T(8,128)(2,1)S(1)} %get-tuple-element.37), channel_id=1, source_target_pairs={{0,31},{1,0},{2,1},{3,2},{4,3},{5,4},{6,5},{7,6},{8,7},{9,8},{10,9... | collective-permute-start | bytes 147464 | tf_op jit(solution)/shard_map/ppermute | solution.py:376
  9.0 7.8 %collective-permute-start.2 = (bf16[2,24,512]{2,1,0:T(8,128)(2,1)S(1)}, bf16[2,24,512]{2,1,0:T(8,128)(2,1)S(1)}, u32[]{:S(2)}, u32[]{:S(2)}) collective-permute-start(bf16[2,24,512]{2,1,0:T(8,128)(2,1)S(1)} %get-tuple-element.38), channel_id=1, source_target_pairs={{0,255},{1,224},{2,225},{3,226},{4,227},{5,228},{6,229},{7,230},{8... | collective-permute-start | bytes 147464 | tf_op jit(solution)/shard_map/ppermute | solution.py:376
  22.4 4.8 %collective-permute-start.3 = (bf16[4096,128]{1,0:T(8,128)(2,1)S(1)}, bf16[4096,128]{1,0:T(8,128)(2,1)S(1)}, u32[]{:S(2)}, u32[]{:S(2)}) collective-permute-start(bf16[4096,128]{1,0:T(8,128)(2,1)S(1)} %get-tuple-element.42), channel_id=1, source_target_pairs={{0,1},{1,0},{2,3},{3,2},{4,5},{5,4},{6,7},{7,6},{8,9},{9,8},{10,11... | collective-permute-start | bytes 3145736 | tf_op jit(solution)/shard_map/ppermute | solution.py:376
  44.7 4.5 %collective-permute-start.4 = (bf16[264,128]{1,0:T(8,128)(2,1)S(1)}, bf16[264,128]{1,0:T(8,128)(2,1)S(1)}, u32[]{:S(2)}, u32[]{:S(2)}) collective-permute-start(bf16[264,128]{1,0:T(8,128)(2,1)S(1)} %reduce_sum.12), channel_id=1, source_target_pairs={{0,192},{1,193},{2,194},{3,195},{4,196},{5,197},{6,198},{7,199},{8... | collective-permute-start | bytes 202760 | tf_op jit(solution)/shard_map/ppermute | solution.py:376
  49.3 5.5 %collective-permute-start.5 = (bf16[264,128]{1,0:T(8,128)(2,1)S(1)}, bf16[264,128]{1,0:T(8,128)(2,1)S(1)}, u32[]{:S(2)}, u32[]{:S(2)}) collective-permute-start(bf16[264,128]{1,0:T(8,128)(2,1)S(1)} %add_convert_fusion.2), channel_id=1, source_target_pairs={{0,4},{1,5},{2,6},{3,7},{4,0},{5,1},{6,2},{7,3},{8,12},{9,13},{10,... | collective-permute-start | bytes 202760 | tf_op jit(solution)/shard_map/ppermute | solution.py:376
  52.4 9.7 %collective-permute-start.7 = (bf16[2,168,512]{2,1,0:T(8,128)(2,1)S(1)}, bf16[2,168,512]{2,1,0:T(8,128)(2,1)S(1)}, u32[]{:S(2)}, u32[]{:S(2)}) collective-permute-start(bf16[2,168,512]{2,1,0:T(8,128)(2,1)S(1)} %get-tuple-element.54), channel_id=1, source_target_pairs={{0,32},{1,33},{2,34},{3,35},{4,36},{5,37},{6,38},{7,39},{8,40},{9,... | collective-permute-start | bytes 1032200 | tf_op jit(solution)/shard_map/ppermute | solution.py:376
  54.8 7.3 %collective-permute-start.6 = (bf16[264,128]{1,0:T(8,128)(2,1)S(1)}, bf16[264,128]{1,0:T(8,128)(2,1)S(1)}, u32[]{:S(2)}, u32[]{:S(2)}) collective-permute-start(bf16[264,128]{1,0:T(8,128)(2,1)S(1)} %add_convert_fusion.1), channel_id=1, source_target_pairs={{0,12},{1,13},{2,14},{3,15},{4,8},{5,9},{6,10},{7,11},{8,4},{9,5},... | collective-permute-start | bytes 202760 | tf_op jit(solution)/shard_map/ppermute | solution.py:376
  63.2 14.9 %all-to-all-start.1 = ((bf16[16,264,128]{2,1,0:T(8,128)(2,1)}), bf16[16,264,128]{2,1,0:T(8,128)(2,1)S(1)}, u32[]{:S(2)}, u32[]{:S(2)}) async-start(bf16[16,264,128]{2,1,0:T(8,128)(2,1)} %broadcast_in_dim.3), calls=%async_computation.1 | async-start | bytes 2162688 | tf_op jit(solution)/shard_map/all_to_all | solution.py:389
  66.9 10.4 %collective-permute-start.8 = (bf16[2,48,512]{2,1,0:T(8,128)(2,1)S(1)}, bf16[2,48,512]{2,1,0:T(8,128)(2,1)S(1)}, u32[]{:S(2)}, u32[]{:S(2)}) collective-permute-start(bf16[2,48,512]{2,1,0:T(8,128)(2,1)S(1)} %shard_map.97), channel_id=1, source_target_pairs={{0,1},{1,2},{2,3},{3,4},{4,5},{5,6},{6,7},{7,8},{8,9},{9,10},{10,1... | collective-permute-start | bytes 294920 | tf_op jit(solution)/shard_map/ppermute | solution.py:376
  78.2 9.4 %collective-permute-start.9 = (bf16[16,264,128]{2,1,0:T(8,128)(2,1)S(1)}, bf16[16,264,128]{2,1,0:T(8,128)(2,1)S(1)}, u32[]{:S(2)}, u32[]{:S(2)}) collective-permute-start(bf16[16,264,128]{2,1,0:T(8,128)(2,1)S(1)} %all-to-all-done.1.half_ref.refs_0_), channel_id=1, source_target_pairs={{0,1},{1,0},{2,3},{3,2},{4,5},{5,4},{6,7},{7,6},{8,9},{9,8},{10,11... | collective-permute-start | bytes 3244040 | tf_op jit(solution)/shard_map/ppermute | solution.py:376
